TPU v7x, 1024 devices: a whole 8x8x8 slice. The times are simulated.
1024 devices in a mesh: ctx: 16 (over z, core), grp: 64 (over x, y).
Axes of the slice: x: 8, y: 8, z: 8, core: 2. Of those that a mesh axis runs over, the one named last changes fastest.
Arguments:
- latent: bfloat16 [64, 2048, 576], P('grp', 'ctx'), may hold values from -6 to 6
- queries: bfloat16 [64, 64, 73728], P('grp', 'ctx'), may hold values from -4 to 4
- out_grad: bfloat16 [64, 64, 65536], P('grp', 'ctx'), may hold values from -6 to 6
- hidden: bfloat16 [64, 2048, 7168], P('grp', None, 'ctx'), may hold values from -6 to 6
- doc_ids: int32 [64, 2048], P('grp', 'ctx'), may hold values from 0 to 7, never falling along the last dimension, each value on 1 to 1024 neighbouring positions
- clip_limits: float32 [64, 8], P('grp'), may hold values from 0.05 to 20
Outputs:
- grad_keys: bfloat16 [64, 2048, 576], P('grp', 'ctx')
- weight_grad: float32 [576, 7168], P('grp', 'ctx')
Inputs may be any that keep to these rules, and one draw needn't show every extreme that they name: `doc_ids`: within each group the ids never fall; each document has 1 to 1024 tokens and one has exactly 1024.
All inputs are finite; a program needn't handle non-finite values.
Results may differ from a plain program's by a relative error of at most 0.0095.
Values may be sent and summed in bfloat16 or wider, within the bound.
No kernel may reach another device: no remote copies, remote signals or barrier semaphores. Data moves between devices by JAX's collectives and lax.ppermute only.
A program may use at most 64 MiB of HBM per device.

v0:
```python
import math

import jax
import jax.numpy as jnp
from jax import lax
from jax.sharding import PartitionSpec as P

LATENT = 512
HEADS = 128


score_scale = 192.0 ** (-0.5)
norm_eps = 1e-06


def shifted(value, axis, by):
    length = lax.axis_size(axis)
    pairs = [(i, i + by) for i in range(length) if 0 <= i + by < length]
    return lax.ppermute(value, axis, pairs)


def sent_to_all(value, axis):
    copies = jnp.broadcast_to(value, (lax.axis_size(axis), *value.shape))
    return lax.all_to_all(copies, axis, split_axis=0, concat_axis=0, tiled=True)


def laid_out(blocks, dim):
    shape = list(blocks.shape[1:])
    shape[dim] *= blocks.shape[0]
    return jnp.moveaxis(blocks, 0, dim).reshape(shape)


def gathered_copies(value, axis, dim):
    blocks = sent_to_all(value, axis)
    return laid_out(blocks, dim)


def split_up(value, dim, length):
    before, after = (value.shape[:dim], value.shape[dim + 1 :])
    return jnp.moveaxis(value.reshape(*before, length, -1, *after), dim, 0)


def sent_and_summed(value, axis, dim):
    length = lax.axis_size(axis)
    blocks = lax.all_to_all(split_up(value, dim, length), axis, 0, 0, tiled=True)
    return jnp.sum(blocks, axis=0)


def block_grads(query_block, grad_block, window_keys, allowed):
    latent_width = grad_block.shape[-1]
    scores = (
        jnp.einsum("qhc,kc->qhk", query_block, window_keys, preferred_element_type=jnp.float32)
        * score_scale
    )
    scores = jnp.where(allowed[:, None, :], scores, -1e30)
    top_score = jnp.max(scores, axis=-1, keepdims=True)
    weights = jnp.exp(scores - top_score)
    weights = weights / jnp.sum(weights, axis=-1, keepdims=True)
    prob_grad = jnp.einsum(
        "qhc,kc->qhk", grad_block, window_keys[:, :latent_width], preferred_element_type=jnp.float32
    )
    row_dots = jnp.sum(weights * prob_grad, axis=-1, keepdims=True)
    score_grad = (weights * (prob_grad - row_dots) * score_scale).astype(jnp.bfloat16)
    weights_low = weights.astype(jnp.bfloat16)
    key_grad = jnp.einsum(
        "qhk,qhc->kc", score_grad, query_block, preferred_element_type=jnp.float32
    )
    value_grad = jnp.einsum(
        "qhk,qhc->kc", weights_low, grad_block, preferred_element_type=jnp.float32
    )
    return key_grad.at[:, :latent_width].add(value_grad)


def scale_rows(values, row_ids, norms, limits):
    member = (row_ids[:, None] == jnp.arange(limits.shape[0], dtype=jnp.int32)[None, :]).astype(
        jnp.float32
    )
    factor = jnp.minimum(1.0, limits / jnp.sqrt(norms + norm_eps))
    return (values * jnp.sum(member * factor[None, :], axis=1)[:, None]).astype(jnp.bfloat16)


def doc_squares(values, row_ids, ndocs):
    member = (row_ids[:, None] == jnp.arange(ndocs, dtype=jnp.int32)[None, :]).astype(jnp.float32)
    return jnp.sum(member * jnp.sum(values * values, axis=1)[:, None], axis=0)


def on_device(latent, queries, out_grad, hidden, doc_ids, clip_limits):
    ctx_count = lax.axis_size("ctx")
    position = lax.axis_index("ctx")
    tok_dev = latent.shape[1]
    key_width = latent.shape[2]
    seq_len = tok_dev * ctx_count
    q_dev = queries.shape[1]
    span = seq_len // 2 + q_dev
    whole_keys, whole_ids = (
        lax.all_gather(latent, "ctx", axis=1, tiled=True),
        lax.all_gather(doc_ids, "ctx", axis=1, tiled=True),
    )
    whole_keys = whole_keys[0]
    whole_ids = whole_ids[0]
    first_query = position * tok_dev + tok_dev - q_dev
    start = jnp.clip(first_query + q_dev - span, 0, seq_len - span)
    window_keys = lax.dynamic_slice_in_dim(whole_keys, start, span, 0)
    window_ids = lax.dynamic_slice_in_dim(whole_ids, start, span, 0)
    key_pos = start + jnp.arange(span, dtype=jnp.int32)
    query_pos = first_query + jnp.arange(q_dev, dtype=jnp.int32)
    query_ids = doc_ids[0, tok_dev - q_dev :]
    allowed = (window_ids[None, :] == query_ids[:, None]) & (key_pos[None, :] <= query_pos[:, None])
    head_block = math.gcd(HEADS, 32)
    blocks = HEADS // head_block
    query_heads = queries[0].reshape(q_dev, blocks, head_block, key_width).transpose(1, 0, 2, 3)
    grad_heads = out_grad[0].reshape(q_dev, blocks, head_block, LATENT).transpose(1, 0, 2, 3)

    def add_block(total, operands):
        return (total + block_grads(operands[0], operands[1], window_keys, allowed), None)

    window_grad = lax.scan(
        add_block, jnp.zeros((span, key_width), jnp.float32), (query_heads, grad_heads)
    )[0]
    partial_value = lax.dynamic_update_slice(
        jnp.zeros((seq_len, key_width), jnp.float32), window_grad, (start, jnp.int32(0))
    )
    limits = clip_limits[0]
    ndocs = limits.shape[0]
    reach = min(ctx_count, -(-span // tok_dev))
    shard_parts = partial_value.reshape(ctx_count, tok_dev, key_width)
    padded = jnp.concatenate(
        [jnp.zeros((reach, tok_dev, key_width), jnp.float32), shard_parts], axis=0
    )
    mine = lax.dynamic_slice_in_dim(padded, position + 1, reach, 0)
    pieces = mine[::-1].astype(jnp.bfloat16)
    running = pieces[0].astype(jnp.float32)
    for offset in range(1, reach):
        arrived = shifted(pieces[offset], "ctx", -offset)
        running = running + arrived.astype(jnp.float32)
    grad_keys = running.astype(jnp.bfloat16)[None]
    full_grad = gathered_copies(grad_keys[0], "ctx", 0)
    values = full_grad.astype(jnp.float32)
    scaled = scale_rows(values, whole_ids, doc_squares(values, whole_ids, ndocs), limits)
    hidden_rows = hidden[0]
    weight_grad = sent_and_summed(
        lax.dot_general(
            scaled, hidden_rows, (((0,), (0,)), ((), ())), preferred_element_type=jnp.float32
        ),
        "grp",
        0,
    )
    return (grad_keys, weight_grad)


def solution(mesh):
    return jax.shard_map(
        on_device,
        mesh=mesh,
        in_specs=(
            P("grp", "ctx", None),
            P("grp", "ctx", None),
            P("grp", "ctx", None),
            P("grp", None, "ctx"),
            P("grp", "ctx"),
            P("grp", None),
        ),
        out_specs=(P("grp", "ctx", None), P("grp", "ctx")),
        check_vma=False,
    )
```

profile of v0, /device:TPU:4, one launch (start us, length us, event | category | flops | bytes accessed | tf_op | source)
XLA Modules:
  0.0 378.4 jit_solution(13929108379515192473)
XLA Ops:
  7.9 2.6 reshape_squeeze.6
  12.5 29.4 %all_gather.6 = s32[1,2048]{1,0:T(1,128)S(1)} all-gather(s32[1,128]{1,0:T(1,128)S(1)} %copy-done.3), channel_id=1, replica_groups=mesh['ctx'=16,'grp'=64] {'ctx'}, dimensions={1}, use_global_device_ids=true | all-gather | bytes 8704 | tf_op jit(solution)/shard_map/all_gather | solution.py:97
  42.0 28.6 %all-gather.2.cloned.1.call-done = bf16[1,2048,576]{1,2,0:T(8,128)(2,1)} async-done(((bf16[1,128,576]{1,2,0:T(8,128)(2,1)}), bf16[1,2048,576]{1,2,0:T(8,128)(2,1)}) %all-gather.2.cloned.1.call-update) | async-done | bytes 2359312 | tf_op jit(solution)/shard_map/all_gather | solution.py:96
  70.7 3.0 constant_dynamic-slice_fusion
  73.7 2.4 copy.104
  76.1 76.7 %while.14 = (s32[]{:T(128)}, f32[1028,576]{1,0:T(8,128)}, bf16[4,4,32,576]{3,2,0,1:T(8,128)(2,1)}, bf16[1028,576]{1,0:T(8,128)(2,1)S(1)}, bf16[4,4,32,512]{3,2,0...) while((s32[]{:T(128)}, f32[1028,576]{1,0:T(8,128)}, ...), condition=%wide.region_5.6_spmd.clone, body=%wide.region_0.5_spmd.clone.sunk | while | flops 576748352 | bytes 24305904 | solution.py:117
  81.8 4.1 %convolution_bitcast_fusion.3 = f32[1028,576]{1,0:T(8,128)} fusion(f32[4,32,1028]{2,1,0:T(8,128)} %fusion.72, bf16[4,4,32,576]{3,2,0,1:T(8,128)(2,1)} %get-tuple-element.348, s32[]{:T(128)} %get-tuple-element.335, f32[4,32,1028]{2,1,0:T(8,128)} %get-tuple-element.322, f32[4,32]{1,0:T(4,128)S(1)} %get-tuple-element.323), kind=kOutput, calls=%fused_computation.3.clone.1 | convolution fusion | flops 152507008 | bytes 4896256 | tf_op jit(solution)/shard_map/while/body/eval_jaxpr/qhk,qhc->kc/dot_general | solution.py:65
  86.5 4.7 %fusion.75 = f32[1028,576]{1,0:T(8,128)} fusion(f32[1028,576]{1,0:T(8,128)} %convolution_bitcast_fusion.3, pred[]{:T(512)} %compare_reduce_fusion.2, bf16[4,4,32,512]{3,2,0,1:T(8,128)(2,1)} %get-tuple-element.350, s32[]{:T(128)} %get-tuple-element.335, f32[4,32]{1,0:T(4,128)S(1)} %get-tuple-element.323, f32[4,32,1028]{2,1,0:T(8,128)} %copy-done.1), kind=kOutput, calls=%fused_computation.7.clone.1 | convolution fusion | flops 136190592 | bytes 5539328 | tf_op jit(solution)/shard_map/while/body/eval_jaxpr/qhk,qhc->kc/dot_general | solution.py:68
  91.2 3.5 select_add_fusion.2
  100.4 4.1 %convolution_bitcast_fusion.3 = f32[1028,576]{1,0:T(8,128)} fusion(f32[4,32,1028]{2,1,0:T(8,128)} %fusion.72, bf16[4,4,32,576]{3,2,0,1:T(8,128)(2,1)} %get-tuple-element.348, s32[]{:T(128)} %get-tuple-element.335, f32[4,32,1028]{2,1,0:T(8,128)} %get-tuple-element.322, f32[4,32]{1,0:T(4,128)S(1)} %get-tuple-element.323), kind=kOutput, calls=%fused_computation.3.clone.1 | convolution fusion | flops 152507008 | bytes 4896256 | tf_op jit(solution)/shard_map/while/body/eval_jaxpr/qhk,qhc->kc/dot_general | solution.py:65
  105.1 4.7 %fusion.75 = f32[1028,576]{1,0:T(8,128)} fusion(f32[1028,576]{1,0:T(8,128)} %convolution_bitcast_fusion.3, pred[]{:T(512)} %compare_reduce_fusion.2, bf16[4,4,32,512]{3,2,0,1:T(8,128)(2,1)} %get-tuple-element.350, s32[]{:T(128)} %get-tuple-element.335, f32[4,32]{1,0:T(4,128)S(1)} %get-tuple-element.323, f32[4,32,1028]{2,1,0:T(8,128)} %copy-done.1), kind=kOutput, calls=%fused_computation.7.clone.1 | convolution fusion | flops 136190592 | bytes 5539328 | tf_op jit(solution)/shard_map/while/body/eval_jaxpr/qhk,qhc->kc/dot_general | solution.py:68
  109.7 4.3 %select_add_fusion.2 = f32[1028,576]{1,0:T(8,128)} fusion(f32[1028,576]{1,0:T(8,128)} %fusion.75, f32[1028,576]{1,0:T(8,128)} %get-tuple-element.336, pred[]{:T(512)S(6)} %compare.22), kind=kLoop, calls=%fused_computation.8.clone.1 | loop fusion | flops 1184256 | bytes 7105537 | tf_op jit(solution)/shard_map/while/body/eval_jaxpr/add | solution.py:115
  119.7 4.1 %convolution_bitcast_fusion.3 = f32[1028,576]{1,0:T(8,128)} fusion(f32[4,32,1028]{2,1,0:T(8,128)} %fusion.72, bf16[4,4,32,576]{3,2,0,1:T(8,128)(2,1)} %get-tuple-element.348, s32[]{:T(128)} %get-tuple-element.335, f32[4,32,1028]{2,1,0:T(8,128)} %get-tuple-element.322, f32[4,32]{1,0:T(4,128)S(1)} %get-tuple-element.323), kind=kOutput, calls=%fused_computation.3.clone.1 | convolution fusion | flops 152507008 | bytes 4896256 | tf_op jit(solution)/shard_map/while/body/eval_jaxpr/qhk,qhc->kc/dot_general | solution.py:65
  124.4 4.7 %fusion.75 = f32[1028,576]{1,0:T(8,128)} fusion(f32[1028,576]{1,0:T(8,128)} %convolution_bitcast_fusion.3, pred[]{:T(512)} %compare_reduce_fusion.2, bf16[4,4,32,512]{3,2,0,1:T(8,128)(2,1)} %get-tuple-element.350, s32[]{:T(128)} %get-tuple-element.335, f32[4,32]{1,0:T(4,128)S(1)} %get-tuple-element.323, f32[4,32,1028]{2,1,0:T(8,128)} %copy-done.1), kind=kOutput, calls=%fused_computation.7.clone.1 | convolution fusion | flops 136190592 | bytes 5539328 | tf_op jit(solution)/shard_map/while/body/eval_jaxpr/qhk,qhc->kc/dot_general | solution.py:68
  129.1 4.3 %select_add_fusion.2 = f32[1028,576]{1,0:T(8,128)} fusion(f32[1028,576]{1,0:T(8,128)} %fusion.75, f32[1028,576]{1,0:T(8,128)} %get-tuple-element.336, pred[]{:T(512)S(6)} %compare.22), kind=kLoop, calls=%fused_computation.8.clone.1 | loop fusion | flops 1184256 | bytes 7105537 | tf_op jit(solution)/shard_map/while/body/eval_jaxpr/add | solution.py:115
  139.1 4.1 %convolution_bitcast_fusion.3 = f32[1028,576]{1,0:T(8,128)} fusion(f32[4,32,1028]{2,1,0:T(8,128)} %fusion.72, bf16[4,4,32,576]{3,2,0,1:T(8,128)(2,1)} %get-tuple-element.348, s32[]{:T(128)} %get-tuple-element.335, f32[4,32,1028]{2,1,0:T(8,128)} %get-tuple-element.322, f32[4,32]{1,0:T(4,128)S(1)} %get-tuple-element.323), kind=kOutput, calls=%fused_computation.3.clone.1 | convolution fusion | flops 152507008 | bytes 4896256 | tf_op jit(solution)/shard_map/while/body/eval_jaxpr/qhk,qhc->kc/dot_general | solution.py:65
  143.8 4.7 %fusion.75 = f32[1028,576]{1,0:T(8,128)} fusion(f32[1028,576]{1,0:T(8,128)} %convolution_bitcast_fusion.3, pred[]{:T(512)} %compare_reduce_fusion.2, bf16[4,4,32,512]{3,2,0,1:T(8,128)(2,1)} %get-tuple-element.350, s32[]{:T(128)} %get-tuple-element.335, f32[4,32]{1,0:T(4,128)S(1)} %get-tuple-element.323, f32[4,32,1028]{2,1,0:T(8,128)} %copy-done.1), kind=kOutput, calls=%fused_computation.7.clone.1 | convolution fusion | flops 136190592 | bytes 5539328 | tf_op jit(solution)/shard_map/while/body/eval_jaxpr/qhk,qhc->kc/dot_general | solution.py:68
  148.4 4.3 %select_add_fusion.2 = f32[1028,576]{1,0:T(8,128)} fusion(f32[1028,576]{1,0:T(8,128)} %fusion.75, f32[1028,576]{1,0:T(8,128)} %get-tuple-element.336, pred[]{:T(512)S(6)} %compare.22), kind=kLoop, calls=%fused_computation.8.clone.1 | loop fusion | flops 1184256 | bytes 7105537 | tf_op jit(solution)/shard_map/while/body/eval_jaxpr/add | solution.py:115
  156.7 11.2 %dynamic_update_slice.3 = bf16[2048,576]{0,1:T(8,128)(2,1)} dynamic-update-slice(bf16[2048,576]{0,1:T(8,128)(2,1)} %broadcast_in_dim.43, bf16[1028,576]{0,1:T(8,128)(2,1)S(1)} %copy.107, s32[]{:T(128)S(6)} %min.8, s32[]{:T(128)} %constant.107.clone.1) | dynamic-update-slice | bytes 2368516 | tf_op jit(solution)/shard_map/dynamic_update_slice | solution.py:120
  167.9 2.4 copy.123
  172.6 6.8 %rev.3 = bf16[9,128,576]{1,0,2:T(8,128)(2,1)} reverse(bf16[9,128,576]{1,0,2:T(8,128)(2,1)} %pad_dynamic-slice_fusion), dimensions={0} | reverse | bytes 2654208 | tf_op jit(solution)/shard_map/rev | solution.py:131
  179.4 7.1 %fusion.45 = (bf16[1,128,576]{1,0,2:T(2,128)(2,1)S(1)}, bf16[1,128,576]{1,0,2:T(2,128)(2,1)S(1)}, bf16[1,128,576]{1,0,2:T(2,128)(2,1)S(1)}, bf16[1,128,576]{1,0,...) fusion(bf16[9,128,576]{1,0,2:T(8,128)(2,1)} %rev.3), kind=kLoop, calls=%fused_computation.74 | loop fusion | flops 73728 | bytes 2801664 | tf_op jit(solution)/shard_map/slice | solution.py:134
  194.5 2.4 collective-permute-done.1
  199.6 11.9 %collective-permute-done.3 = bf16[128,576]{0,1:T(8,128)(2,1)S(1)} collective-permute-done((bf16[128,576]{0,1:T(8,128)(2,1)S(1)}, bf16[128,576]{0,1:T(8,128)(2,1)S(1)}, u32[]{:S(2)}, u32[]{:S(2)}) %collective-permute-start.3) | collective-permute-done | bytes 147488 | tf_op jit(solution)/shard_map/ppermute | solution.py:19
  212.5 8.5 %collective-permute-done.5 = bf16[128,576]{0,1:T(8,128)(2,1)S(1)} collective-permute-done((bf16[128,576]{0,1:T(8,128)(2,1)S(1)}, bf16[128,576]{0,1:T(8,128)(2,1)S(1)}, u32[]{:S(2)}, u32[]{:S(2)}) %collective-permute-start.5) | collective-permute-done | bytes 147488 | tf_op jit(solution)/shard_map/ppermute | solution.py:19
  221.0 5.3 %collective-permute-done.6 = bf16[128,576]{0,1:T(8,128)(2,1)S(1)} collective-permute-done((bf16[128,576]{0,1:T(8,128)(2,1)S(1)}, bf16[128,576]{0,1:T(8,128)(2,1)S(1)}, u32[]{:S(2)}, u32[]{:S(2)}) %collective-permute-start.6) | collective-permute-done | bytes 147488 | tf_op jit(solution)/shard_map/ppermute | solution.py:19
  226.9 75.5 %all_to_all.10 = bf16[16,128,576]{1,2,0:T(8,128)(2,1)S(1)} all-to-all(bf16[16,128,576]{1,2,0:T(8,128)(2,1)S(1)} %broadcast_in_dim.46), channel_id=1, replica_groups=mesh['ctx'=16,'grp'=64] {'ctx'}, dimensions={0} | all-to-all | bytes 4718592 | tf_op jit(solution)/shard_map/all_to_all | solution.py:24
  305.1 4.6 %dot_general.32 = bf16[64,9,2048]{2,1,0:T(8,128)(2,1)} reshape(bf16[576,2048]{1,0:T(8,128)(2,1)} %fusion.38) | data formatting | bytes 4718592 | tf_op jit(solution)/shard_map/dot_general | solution.py:142
  309.7 4.1 %fusion.39 = f32[64,9,448]{2,0,1:T(8,128)S(1)} fusion(bf16[64,9,2048]{2,1,0:T(8,128)(2,1)} %dot_general.32, bf16[1,2048,448]{1,2,0:T(8,128)(2,1)S(1)} %copy-done), kind=kOutput, calls=%fused_computation.49 | convolution fusion | flops 1056964608 | bytes 5226496 | tf_op jit(solution)/shard_map/dot_general | solution.py:142
  315.8 2.7 reshape.84
  318.5 43.8 %all_to_all.11 = f32[64,1,4032]{2,1,0:T(1,128)} all-to-all(f32[64,1,4032]{2,1,0:T(1,128)S(1)} %reshape.84), channel_id=1, replica_groups=mesh['ctx'=16,'grp'=64] {'grp'}, dimensions={0} | all-to-all | bytes 2064384 | tf_op jit(solution)/shard_map/all_to_all | solution.py:45
  362.9 4.4 %reduce.14 = f32[64,4032]{1,0:T(8,128)S(1)} reduce(f32[64,1,4032]{2,1,0:T(1,128)} %all_to_all.11, f32[]{:T(128)} %broadcast.105), dimensions={1}, to_apply=%all_to_all.7.reduce_sub_computation | reduce | bytes 2064388 | tf_op jit(solution)/shard_map/all_to_all | solution.py:45
  (78 shorter events, 56.0 us)
Async XLA Ops:
  7.2 302.5 %copy-start = (bf16[1,2048,448]{1,2,0:T(8,128)(2,1)S(1)}, bf16[1,2048,448]{1,2,0:T(8,128)(2,1)}, u32[]{:S(2)}) copy-start(bf16[1,2048,448]{1,2,0:T(8,128)(2,1)} %param.13) | copy-start | bytes 5505028
  7.2 5.3 %copy-start.3 = (s32[1,128]{1,0:T(1,128)S(1)}, s32[1,128]{1,0:T(1,128)}, u32[]{:S(2)}) copy-start(s32[1,128]{1,0:T(1,128)} %param.14) | copy-start | bytes 1540
  7.2 63.5 %all-gather.2.cloned.1.call-start = ((), (), s32[]{:S(2)}) async-start(), calls=%async_computation.2 | async-start | bytes 2506752 | tf_op jit(solution)/shard_map/all_gather | solution.py:96
  77.8 0.8 copy-start.1
  96.3 0.8 copy-start.1
  115.7 0.8 copy-start.1
  135.0 0.8 copy-start.1
  186.5 6.7 %collective-permute-start = (bf16[128,576]{0,1:T(8,128)(2,1)S(1)}, bf16[128,576]{0,1:T(8,128)(2,1)S(1)}, u32[]{:S(2)}, u32[]{:S(2)}) collective-permute-start(bf16[128,576]{0,1:T(8,128)(2,1)S(1)} %bitcast.132), channel_id=1, source_target_pairs={{64,0},{128,64},{192,128},{256,192},{320,256},{384,320},{448,384},... | collective-permute-start | bytes 442376 | tf_op jit(solution)/shard_map/ppermute | solution.py:19
  187.8 9.1 %collective-permute-start.1 = (bf16[128,576]{0,1:T(8,128)(2,1)S(1)}, bf16[128,576]{0,1:T(8,128)(2,1)S(1)}, u32[]{:S(2)}, u32[]{:S(2)}) collective-permute-start(bf16[128,576]{0,1:T(8,128)(2,1)S(1)} %bitcast.130), channel_id=1, source_target_pairs={{128,0},{192,64},{256,128},{320,192},{384,256},{448,320},{512,384}... | collective-permute-start | bytes 442376 | tf_op jit(solution)/shard_map/ppermute | solution.py:19
  189.2 9.2 %collective-permute-start.2 = (bf16[128,576]{0,1:T(8,128)(2,1)S(1)}, bf16[128,576]{0,1:T(8,128)(2,1)S(1)}, u32[]{:S(2)}, u32[]{:S(2)}) collective-permute-start(bf16[128,576]{0,1:T(8,128)(2,1)S(1)} %bitcast.127), channel_id=1, source_target_pairs={{192,0},{256,64},{320,128},{384,192},{448,256},{512,320},{576,384}... | collective-permute-start | bytes 442376 | tf_op jit(solution)/shard_map/ppermute | solution.py:19
  190.5 21.0 %collective-permute-start.3 = (bf16[128,576]{0,1:T(8,128)(2,1)S(1)}, bf16[128,576]{0,1:T(8,128)(2,1)S(1)}, u32[]{:S(2)}, u32[]{:S(2)}) collective-permute-start(bf16[128,576]{0,1:T(8,128)(2,1)S(1)} %bitcast.125), channel_id=1, source_target_pairs={{256,0},{320,64},{384,128},{448,192},{512,256},{576,320},{640,384}... | collective-permute-start | bytes 442376 | tf_op jit(solution)/shard_map/ppermute | solution.py:19
  191.8 20.7 %collective-permute-start.4 = (bf16[128,576]{0,1:T(8,128)(2,1)S(1)}, bf16[128,576]{0,1:T(8,128)(2,1)S(1)}, u32[]{:S(2)}, u32[]{:S(2)}) collective-permute-start(bf16[128,576]{0,1:T(8,128)(2,1)S(1)} %bitcast.128), channel_id=1, source_target_pairs={{320,0},{384,64},{448,128},{512,192},{576,256},{640,320},{704,384}... | collective-permute-start | bytes 442376 | tf_op jit(solution)/shard_map/ppermute | solution.py:19
  193.2 27.7 %collective-permute-start.5 = (bf16[128,576]{0,1:T(8,128)(2,1)S(1)}, bf16[128,576]{0,1:T(8,128)(2,1)S(1)}, u32[]{:S(2)}, u32[]{:S(2)}) collective-permute-start(bf16[128,576]{0,1:T(8,128)(2,1)S(1)} %bitcast.131), channel_id=1, source_target_pairs={{384,0},{448,64},{512,128},{576,192},{640,256},{704,320},{768,384}... | collective-permute-start | bytes 442376 | tf_op jit(solution)/shard_map/ppermute | solution.py:19
  196.9 29.3 %collective-permute-start.6 = (bf16[128,576]{0,1:T(8,128)(2,1)S(1)}, bf16[128,576]{0,1:T(8,128)(2,1)S(1)}, u32[]{:S(2)}, u32[]{:S(2)}) collective-permute-start(bf16[128,576]{0,1:T(8,128)(2,1)S(1)} %bitcast.129), channel_id=1, source_target_pairs={{448,0},{512,64},{576,128},{640,192},{704,256},{768,320},{832,384}... | collective-permute-start | bytes 442376 | tf_op jit(solution)/shard_map/ppermute | solution.py:19
  198.3 27.9 %collective-permute-start.7 = (bf16[128,576]{0,1:T(8,128)(2,1)S(1)}, bf16[128,576]{0,1:T(8,128)(2,1)S(1)}, u32[]{:S(2)}, u32[]{:S(2)}) collective-permute-start(bf16[128,576]{0,1:T(8,128)(2,1)S(1)} %bitcast.126), channel_id=1, source_target_pairs={{512,0},{576,64},{640,128},{704,192},{768,256},{832,320},{896,384}... | collective-permute-start | bytes 442376 | tf_op jit(solution)/shard_map/ppermute | solution.py:19
  226.4 75.9 %copy-start.2 = (bf16[128,576]{0,1:T(8,128)(2,1)}, bf16[128,576]{0,1:T(8,128)(2,1)S(1)}, u32[]{:S(2)}) copy-start(bf16[128,576]{0,1:T(8,128)(2,1)S(1)} %add_convert_fusion) | copy-start | bytes 442372
  302.4 0.7 copy-start.4
Sparse Core Ops, SparseCore 0:
  10.7 59.9 all-gather.1
where the time goes:
time: 380 us; the launch traced here: 378 us
  blocking collectives  149 us (39%)
  waiting for transfers between devices  58.5 us (15%)
  matrix products  54 us (14%)
  local copies, waits for them, and re-layouts  52.5 us (14%)
  other arithmetic  40 us (11%)
  between operations  14.3 us (4%)
  starting transfers between devices  10.4 us (3%)
    all_to_all x1, blocking collectives, sent_to_all(): return lax.all_to_all(copies, axis, split_axis=0, concat_axis=0, tiled=True)  75.5 us
    all_to_all x1, blocking collectives, sent_and_summed(): lax.all_to_all(split_up(value, dim, length), axis, 0, 0, tiled=True)  43.8 us
    all_gather x1, blocking collectives, on_device(): lax.all_gather(doc_ids, 'ctx', axis=1, tiled=True)  29.4 us
    ppermute x8, waiting for transfers between devices, shifted(): return lax.ppermute(value, axis, pairs)  29.2 us
    all_gather x1, waiting for transfers between devices, on_device(): lax.all_gather(latent, 'ctx', axis=1, tiled=True)  28.6 us
    dot_general x4, matrix products, block_grads(): jnp.einsum('qhk,qhc->kc', weights_low, grad_block, preferred_element_type...  18.6 us
    add x4, other arithmetic, add_block(): total + block_grads(operands[0], operands[1], window_keys, allowed)  16.5 us
    dot_general x4, matrix products, block_grads(): jnp.einsum('qhk,qhc->kc', score_grad, query_block, preferred_element_type...  16.3 us
  transfers between devices with their start and end apart: 9, of which 7 were waited for; matrix products, arithmetic and copies ran while one was open for 1% of the time, Pallas kernels for 0%

commit v1 on v0

v1 whole, which is shorter than its diff:
```python
import functools

import jax
import jax.numpy as jnp
from jax import lax
from jax.experimental import pallas as pl
from jax.experimental.pallas import tpu as pltpu
from jax.sharding import PartitionSpec as P

LATENT = 512
KW = 576
HEADS = 128
TOK = 128
Q_DEV = 4
NDOC = 8
CHIPS = 8
BACK = 5
ROWS = 592
PAIR = 2 * TOK
QH = Q_DEV * HEADS
SLOT = 512
GRP_ROWS = 9
TAIL = 56

score_scale = 192.0 ** (-0.5)
norm_eps = 1e-06
VMEM_BYTES = 56 * 1024 * 1024


def chip_shift(value, by0, by1):
    pairs = []
    for chip in range(CHIPS):
        for core, by in ((0, by0), (1, by1)):
            if by is not None:
                pairs.append((2 * chip + core, 2 * ((chip + by) % CHIPS) + core))
    return lax.ppermute(value, "ctx", pairs)


def core_swap(value):
    return lax.ppermute(value, "ctx", [(i, i ^ 1) for i in range(2 * CHIPS)])


def attention_kernel(
    info, o0, o1, o2, o3, o4, p0, p1, p2, p3, p4, rows_ref, cols_ref,
    keep_ref, send_ref, mid_ref, keys, score, dprob, mixed,
):
    chip, core = info[0], info[1]
    own, par = (o0, o1, o2, o3, o4), (p0, p1, p2, p3, p4)

    @pl.when(core == 0)
    def _():
        for k in range(BACK):
            keys[k, :, :TOK] = own[k][...]
            keys[k, :, TOK:] = par[k][...]

    @pl.when(core != 0)
    def _():
        for k in range(BACK):
            keys[k, :, :TOK] = par[k][...]
            keys[k, :, TOK:] = own[k][...]

    own_ids = o0[KW:ROWS, :].astype(jnp.float32)[0:1]
    lane = lax.broadcasted_iota(jnp.int32, (1, TOK), 1)
    query_ids = [
        jnp.sum(jnp.where(lane == TOK - Q_DEV + i, own_ids, 0.0), axis=1, keepdims=True)
        for i in range(Q_DEV)
    ]
    pair_lane = lax.broadcasted_iota(jnp.int32, (1, PAIR), 1)
    tops = [None] * Q_DEV
    for k in range(BACK):
        both = jnp.dot(rows_ref[...], keys[k, :KW, :], preferred_element_type=jnp.float32)
        ids = keys[k, KW:ROWS, :].astype(jnp.float32)[0:1]
        place = pair_lane - k * PAIR
        there = chip - k >= 0
        for i in range(Q_DEV):
            at = core * TOK + TOK - Q_DEV + i
            allowed = (ids == query_ids[i]) & (place <= at) & there
            part = slice(i * HEADS, (i + 1) * HEADS)
            s = jnp.where(allowed, both[part] * score_scale, -1e30)
            score[k, part, :] = s
            tops[i] = s if k == 0 else jnp.maximum(tops[i], s)
        dprob[k] = both[QH:]
    for i in range(Q_DEV):
        part = slice(i * HEADS, (i + 1) * HEADS)
        top = jnp.max(tops[i], axis=1, keepdims=True)
        total = dots = None
        for k in range(BACK):
            e = jnp.exp(score[k, part, :] - top)
            score[k, part, :] = e
            w = e * dprob[k, part, :]
            total = e if k == 0 else total + e
            dots = w if k == 0 else dots + w
        inv = 1.0 / jnp.sum(total, axis=1, keepdims=True)
        row_dot = jnp.sum(dots, axis=1, keepdims=True) * inv
        for k in range(BACK):
            prob = score[k, part, :] * inv
            grad = prob * (dprob[k, part, :] - row_dot) * score_scale
            mixed[k, part, :] = grad.astype(jnp.bfloat16)
            mixed[k, QH + i * HEADS : QH + (i + 1) * HEADS, :] = prob.astype(jnp.bfloat16)

    blank = jnp.zeros((ROWS - KW, PAIR), jnp.bfloat16)
    for slot in range(2):
        keep_ref[slot, KW:, :] = blank
        send_ref[slot, KW:, :] = blank
    mid_ref[KW:, :] = (keys[2, KW:ROWS, :].astype(jnp.float32) * 0.5).astype(jnp.bfloat16)
    for k in range(BACK):
        g = jnp.dot(cols_ref[...], mixed[k], preferred_element_type=jnp.float32)
        g = g.astype(jnp.bfloat16)
        if k == 2:
            mid_ref[:KW, :] = g
            continue
        slot, keeper = (k, 0) if k < 2 else (4 - k, 1)

        @pl.when(core == keeper)
        def _():
            keep_ref[slot, :KW, :] = g

        @pl.when(core != keeper)
        def _():
            send_ref[slot, :KW, :] = g


def vmem():
    return pl.BlockSpec(memory_space=pltpu.VMEM)


def smem():
    return pl.BlockSpec(memory_space=pltpu.SMEM)


def attention(info, own, par, rows, cols):
    block = jax.ShapeDtypeStruct((2, ROWS, PAIR), jnp.bfloat16)
    return pl.pallas_call(
        attention_kernel,
        out_shape=(block, block, jax.ShapeDtypeStruct((ROWS, PAIR), jnp.bfloat16)),
        in_specs=[smem()] + [vmem()] * 12,
        out_specs=(vmem(), vmem(), vmem()),
        scratch_shapes=[
            pltpu.VMEM((BACK, ROWS, PAIR), jnp.bfloat16),
            pltpu.VMEM((BACK, QH, PAIR), jnp.float32),
            pltpu.VMEM((BACK, QH, PAIR), jnp.float32),
            pltpu.VMEM((BACK, 2 * QH, PAIR), jnp.bfloat16),
        ],
        compiler_params=pltpu.CompilerParams(vmem_limit_bytes=VMEM_BYTES),
        name="attention_grads",
    )(info, *own, *par, rows, cols)


def down_kernel(
    info, limits, g0, r1, r2, r3, s1, s2, s3, r4, s4, hidden,
    out_ref, own_ref, last, scaled, weight,
):
    chip, core = info[0], info[1]

    @pl.when(core == 0)
    def _():
        last[:, :TOK] = r4[...]
        last[:, TOK:] = s4[...]
        own_ref[...] = s2[:KW, :TOK]

    @pl.when(core != 0)
    def _():
        last[:, :TOK] = s4[...]
        last[:, TOK:] = r4[...]
        own_ref[...] = r2[:KW, TOK:]

    away = jnp.where(core == 0, -1, 1)
    blocks = [(g0, 0)]
    blocks += [(r, away * (j + 1)) for j, r in enumerate((r1, r2, r3))]
    blocks += [(s, -away * (j + 1)) for j, s in enumerate((s1, s2, s3))]
    blocks += [(last, 4)]
    doc = lax.broadcasted_iota(jnp.int32, (NDOC, PAIR), 0).astype(jnp.float32)
    squares = jnp.zeros((NDOC, PAIR), jnp.float32)
    members = []
    for ref, _ in blocks:
        x = ref[:KW, :].astype(jnp.float32)
        ids = ref[KW:ROWS, :].astype(jnp.float32)[0:1]
        member = doc == ids
        members.append(member)
        squares = squares + jnp.where(member, jnp.sum(x * x, axis=0, keepdims=True), 0.0)
    norms = jnp.sum(squares, axis=1, keepdims=True)
    factor = jnp.minimum(1.0, limits[:, 0:1] / jnp.sqrt(norms + norm_eps))
    for (ref, by), member in zip(blocks, members, strict=True):
        gain = jnp.sum(jnp.where(member, factor, 0.0), axis=0, keepdims=True)
        shard = lax.rem(chip + by + 2 * CHIPS - 2, CHIPS)
        x = ref[:KW, :].astype(jnp.float32) * gain
        scaled[:, pl.ds(pl.multiple_of(shard * PAIR, PAIR), PAIR)] = x.astype(jnp.bfloat16)
    product = lax.dot_general(
        scaled[...], hidden[...], (((1,), (1,)), ((), ())), preferred_element_type=jnp.float32
    )
    width = product.shape[1]
    weight[...] = jnp.zeros_like(weight)
    weight[:, :width] = product.astype(jnp.bfloat16)
    whole = weight[...]
    row = lax.broadcasted_iota(jnp.int32, (SLOT, KW), 0)
    col = lax.broadcasted_iota(jnp.int32, (SLOT, KW), 1)
    pick = (col == row + lax.shift_right_logical(row, 3)).astype(jnp.bfloat16)
    first = jnp.dot(pick, whole, preferred_element_type=jnp.float32)
    row = lax.broadcasted_iota(jnp.int32, (SLOT // 8, KW), 0)
    col = lax.broadcasted_iota(jnp.int32, (SLOT // 8, KW), 1)
    pick = (col == row * GRP_ROWS + 8).astype(jnp.bfloat16)
    ninth = jnp.dot(pick, whole, preferred_element_type=jnp.float32).astype(jnp.bfloat16)
    row = lax.broadcasted_iota(jnp.int32, (SLOT, 128), 0)
    col = lax.broadcasted_iota(jnp.int32, (SLOT, 128), 1)
    pieces = []
    for s in range(8):
        pick = ((row == col - 64 + s * TAIL) & (col >= 64) & (col < 64 + TAIL)).astype(jnp.bfloat16)
        pieces.append(
            jnp.dot(ninth, pick, preferred_element_type=jnp.float32).astype(jnp.bfloat16)
        )
    pieces = jnp.concatenate(pieces, axis=0)
    row = lax.broadcasted_iota(jnp.int32, (SLOT, SLOT), 0)
    col = lax.broadcasted_iota(jnp.int32, (SLOT, SLOT), 1)
    pick = (col == (row & 7) * 64 + lax.shift_right_logical(row, 3)).astype(jnp.bfloat16)
    tail = jnp.dot(pick, pieces, preferred_element_type=jnp.float32)
    out_ref[:, :384] = first[:, :384].astype(jnp.bfloat16)
    out_ref[:, 384:] = (first[:, 384:] + tail).astype(jnp.bfloat16)


def down_grad(info, limits, blocks, hidden):
    return pl.pallas_call(
        down_kernel,
        out_shape=(
            jax.ShapeDtypeStruct((SLOT, SLOT), jnp.bfloat16),
            jax.ShapeDtypeStruct((KW, TOK), jnp.bfloat16),
        ),
        in_specs=[smem()] + [vmem()] * 11,
        out_specs=(vmem(), vmem()),
        scratch_shapes=[
            pltpu.VMEM((ROWS, PAIR), jnp.bfloat16),
            pltpu.VMEM((KW, CHIPS * PAIR), jnp.bfloat16),
            pltpu.VMEM((KW, SLOT), jnp.bfloat16),
        ],
        compiler_params=pltpu.CompilerParams(vmem_limit_bytes=VMEM_BYTES),
        name="down_grad",
    )(info, limits, *blocks, hidden)


def added(*terms):
    total = terms[0].astype(jnp.float32)
    for term in terms[1:]:
        total = total + term.astype(jnp.float32)
    return total.astype(jnp.bfloat16)


def group_part(latent, queries, out_grad, hidden, doc_ids, clip_limits):
    position = lax.axis_index("ctx")
    core = position % 2
    info = jnp.stack([position // 2, core]).astype(jnp.int32)
    ids = jnp.pad(doc_ids.astype(jnp.bfloat16), ((0, ROWS - KW - 1), (0, 0)))
    keys = jnp.concatenate([latent[0].T, ids], axis=0)
    own = [keys, chip_shift(keys, 1, 1), chip_shift(keys, 2, 2), chip_shift(keys, 3, 3)]
    own.append(chip_shift(chip_shift(keys, -2, -2), -2, -2))
    par = [core_swap(value) for value in own]
    query_rows = queries[0].reshape(QH, KW)
    grad_rows = out_grad[0].reshape(QH, LATENT)
    rows = jnp.concatenate([query_rows, jnp.pad(grad_rows, ((0, 0), (0, KW - LATENT)))], axis=0)
    keep, send, mid = attention(info, own, par, rows, rows.T)

    arrived = core_swap(send)
    moved = chip_shift(added(keep[0], arrived[0]), 1, -1)
    moved = chip_shift(added(keep[1], arrived[1], moved), 1, -1)
    mine = added(mid, moved)
    total = added(mine, core_swap(mine))

    ring = [total]
    for _ in range(3):
        ring.append(chip_shift(ring[-1], 1, -1))
    half = jnp.where(core == 0, ring[3][:, :TOK], ring[3][:, TOK:])
    ring.append(chip_shift(half, 1, -1))
    swapped = [core_swap(value) for value in ring[1:]]
    limits = jnp.broadcast_to(clip_limits[0][:, None], (NDOC, 128))
    blocks = ring[:4] + swapped[:3] + [ring[4], swapped[3]]
    chunks, own_grad = down_grad(info, limits, blocks, hidden[0].T)
    return own_grad, chunks


def on_device(latent, queries, out_grad, hidden, doc_ids, clip_limits):
    own_grad, chunks = group_part(latent, queries, out_grad, hidden, doc_ids, clip_limits)
    groups = lax.axis_size("grp")
    chunks = chunks.reshape(groups, SLOT // groups, SLOT)
    chunks = lax.all_to_all(chunks, "grp", 0, 0, tiled=True)
    mine = jnp.sum(chunks.astype(jnp.float32), axis=0)
    width = hidden.shape[2]
    ninth = mine[:, width : width + TAIL].reshape(1, width)
    weight_grad = jnp.concatenate([mine[:, :width], ninth], axis=0)
    return own_grad.T[None], weight_grad


def solution(mesh):
    return jax.shard_map(
        on_device,
        mesh=mesh,
        in_specs=(
            P("grp", "ctx", None),
            P("grp", "ctx", None),
            P("grp", "ctx", None),
            P("grp", None, "ctx"),
            P("grp", "ctx"),
            P("grp", None),
        ),
        out_specs=(P("grp", "ctx", None), P("grp", "ctx")),
        check_vma=False,
    )
```

time: 380 us -> 177 us (0.47)
  blocking collectives: 149 us -> 33.3 us
  starting transfers between devices: 10.4 us -> 69.9 us
  matrix products: 54 us -> 0 us
  local copies, waits for them, and re-layouts: 52.5 us -> 5.8 us
  other arithmetic: 40 us -> 6.55 us
  Pallas kernels: 0 us -> 17.2 us
  waiting for transfers between devices: 58.5 us -> 41.9 us
  between operations: 14.3 us -> 1.1 us
    all_to_all x2 -> x1, blocking collectives: 119 us -> 33.3 us  [on_device(): chunks = lax.all_to_all(chunks, 'grp', 0, 0, tiled=True)]
    ppermute x8 -> x22, starting transfers between devices: 10.3 us -> 69.9 us  [the longest x11 47 us: chip_shift(): return lax.ppermute(value, 'ctx', pairs)]
    dot_general x17 -> x0, matrix products: 54 us -> none  [the longest x4 18.6 us: block_grads(): jnp.einsum('qhk,qhc->kc', weights_low, grad_block, preferred_element_type...]
    all_gather x1 -> x0, blocking collectives: 29.4 us -> none  [on_device(): lax.all_gather(doc_ids, 'ctx', axis=1, tiled=True)]
    all_gather x1 -> x0, waiting for transfers between devices: 28.6 us -> none  [on_device(): lax.all_gather(latent, 'ctx', axis=1, tiled=True)]
    pallas_call x0 -> x2, Pallas kernels: none -> 17.2 us  [the longest x1 10.1 us: attention(): pl.pallas_call(attention_kernel, out_shape=(block, block, jax.ShapeDtypeS...]
    add x6 -> x0, other arithmetic: 16.5 us -> none  [the longest x4 16.5 us: add_block(): total + block_grads(operands[0], operands[1], window_keys, allowed)]
    ppermute x8 -> x22, waiting for transfers between devices: 29.2 us -> 41.9 us  [the longest x11 37.1 us: chip_shift(): return lax.ppermute(value, 'ctx', pairs)]
  transfers between devices with their start and end apart: 9 -> 22, of which waited for: 7 -> 11; matrix products, arithmetic and copies ran while one was open for 1% -> 3% of each run, Pallas kernels for 0% -> 0%
where the time goes in v1:
time: 177 us; the launch traced here: 176 us
  starting transfers between devices  69.9 us (39%)
  waiting for transfers between devices  41.9 us (24%)
  blocking collectives  33.3 us (19%)
  Pallas kernels  17.2 us (10%)
  other arithmetic  6.55 us (4%)
  local copies, waits for them, and re-layouts  5.8 us (3%)
    ppermute x11, starting transfers between devices, chip_shift(): return lax.ppermute(value, 'ctx', pairs)  47 us
    ppermute x11, waiting for transfers between devices, chip_shift(): return lax.ppermute(value, 'ctx', pairs)  37.1 us
    all_to_all x1, blocking collectives, on_device(): chunks = lax.all_to_all(chunks, 'grp', 0, 0, tiled=True)  33.3 us
    ppermute x11, starting transfers between devices, core_swap(): return lax.ppermute(value, 'ctx', [(i, i ^ 1) for i in range(2 * CHIPS)])  22.9 us
    pallas_call x1, Pallas kernels, attention(): pl.pallas_call(attention_kernel, out_shape=(block, block, jax.ShapeDtypeS...  10.1 us
    pallas_call x1, Pallas kernels, down_grad(): pl.pallas_call(down_kernel, out_shape=(jax.ShapeDtypeStruct((SLOT, SLOT),...  7.07 us
    ppermute x11, waiting for transfers between devices, core_swap(): return lax.ppermute(value, 'ctx', [(i, i ^ 1) for i in range(2 * CHIPS)])  4.83 us
  transfers between devices with their start and end apart: 22, of which 11 were waited for; matrix products, arithmetic and copies ran while one was open for 3% of the time, Pallas kernels for 0%

profile of v1, /device:TPU:4, one launch (start us, length us, event | category | flops | bytes accessed | tf_op | source)
XLA Modules:
  0.0 175.7 jit_solution(5936148655183653166)
XLA Ops:
  2.2 16.5 %collective-permute-start.3 = (bf16[592,128]{1,0:T(8,128)(2,1)S(1)}, bf16[592,128]{1,0:T(8,128)(2,1)}, u32[]{:S(2)}, u32[]{:S(2)}) collective-permute-start(bf16[592,128]{1,0:T(8,128)(2,1)S(1)} %fusion.5.o0), channel_id=1, source_target_pairs={{0,768},{64,832},{128,896},{192,960},{256,0},{320,64},{384,128},{4... | collective-permute-start | bytes 454664 | tf_op jit(solution)/shard_map/ppermute | solution.py:36
  18.8 4.3 %collective-permute-start = (bf16[592,128]{1,0:T(8,128)(2,1)S(1)}, bf16[592,128]{1,0:T(8,128)(2,1)S(1)}, u32[]{:S(2)}, u32[]{:S(2)}) collective-permute-start(bf16[592,128]{1,0:T(8,128)(2,1)S(1)} %fusion.5.o0), channel_id=1, source_target_pairs={{0,128},{64,192},{128,256},{192,320},{256,384},{320,448},{384,512}... | collective-permute-start | bytes 454664 | tf_op jit(solution)/shard_map/ppermute | solution.py:36
  23.1 1.9 %collective-permute-start.1 = (bf16[592,128]{1,0:T(8,128)(2,1)S(1)}, bf16[592,128]{1,0:T(8,128)(2,1)S(1)}, u32[]{:S(2)}, u32[]{:S(2)}) collective-permute-start(bf16[592,128]{1,0:T(8,128)(2,1)S(1)} %fusion.5.o0), channel_id=1, source_target_pairs={{0,256},{64,320},{128,384},{192,448},{256,512},{320,576},{384,640}... | collective-permute-start | bytes 454664 | tf_op jit(solution)/shard_map/ppermute | solution.py:36
  25.0 2.5 %collective-permute-start.2 = (bf16[592,128]{1,0:T(8,128)(2,1)S(1)}, bf16[592,128]{1,0:T(8,128)(2,1)S(1)}, u32[]{:S(2)}, u32[]{:S(2)}) collective-permute-start(bf16[592,128]{1,0:T(8,128)(2,1)S(1)} %fusion.5.o0), channel_id=1, source_target_pairs={{0,384},{64,448},{128,512},{192,576},{256,640},{320,704},{384,768}... | collective-permute-start | bytes 454664 | tf_op jit(solution)/shard_map/ppermute | solution.py:36
  27.5 5.5 %collective-permute-start.4 = (bf16[592,128]{1,0:T(8,128)(2,1)}, bf16[592,128]{1,0:T(8,128)(2,1)S(1)}, u32[]{:S(2)}, u32[]{:S(2)}) collective-permute-start(bf16[592,128]{1,0:T(8,128)(2,1)} %collective-permute-done.3), channel_id=1, source_target_pairs={{0,768},{64,832},{128,896},{192,960},{256,0},{320,64},{384,128},{4... | collective-permute-start | bytes 454664 | tf_op jit(solution)/shard_map/ppermute | solution.py:36
  33.0 1.9 %collective-permute-start.5 = (bf16[592,128]{1,0:T(8,128)(2,1)S(1)}, bf16[592,128]{1,0:T(8,128)(2,1)S(1)}, u32[]{:S(2)}, u32[]{:S(2)}) collective-permute-start(bf16[592,128]{1,0:T(8,128)(2,1)S(1)} %fusion.5.o0), channel_id=1, source_target_pairs={{0,64},{64,0},{128,192},{192,128},{256,320},{320,256},{384,448},{4... | collective-permute-start | bytes 454664 | tf_op jit(solution)/shard_map/ppermute | solution.py:40
  37.6 2.4 %collective-permute-start.6 = (bf16[592,128]{1,0:T(8,128)(2,1)S(1)}, bf16[592,128]{1,0:T(8,128)(2,1)S(1)}, u32[]{:S(2)}, u32[]{:S(2)}) collective-permute-start(bf16[592,128]{1,0:T(8,128)(2,1)S(1)} %collective-permute-done.o1), channel_id=1, source_target_pairs={{0,64},{64,0},{128,192},{192,128},{256,320},{320,256},{384,448},{4... | collective-permute-start | bytes 454664 | tf_op jit(solution)/shard_map/ppermute | solution.py:40
  41.5 1.9 %collective-permute-start.7 = (bf16[592,128]{1,0:T(8,128)(2,1)S(1)}, bf16[592,128]{1,0:T(8,128)(2,1)S(1)}, u32[]{:S(2)}, u32[]{:S(2)}) collective-permute-start(bf16[592,128]{1,0:T(8,128)(2,1)S(1)} %collective-permute-done.1.o2), channel_id=1, source_target_pairs={{0,64},{64,0},{128,192},{192,128},{256,320},{320,256},{384,448},{4... | collective-permute-start | bytes 454664 | tf_op jit(solution)/shard_map/ppermute | solution.py:40
  43.7 2.2 %collective-permute-start.8 = (bf16[592,128]{1,0:T(8,128)(2,1)S(1)}, bf16[592,128]{1,0:T(8,128)(2,1)}, u32[]{:S(2)}, u32[]{:S(2)}) collective-permute-start(bf16[592,128]{1,0:T(8,128)(2,1)S(1)} %collective-permute-done.2.o3), channel_id=1, source_target_pairs={{0,64},{64,0},{128,192},{192,128},{256,320},{320,256},{384,448},{4... | collective-permute-start | bytes 454664 | tf_op jit(solution)/shard_map/ppermute | solution.py:40
  45.9 2.2 %collective-permute-start.9 = (bf16[592,128]{1,0:T(8,128)(2,1)S(1)}, bf16[592,128]{1,0:T(8,128)(2,1)}, u32[]{:S(2)}, u32[]{:S(2)}) collective-permute-start(bf16[592,128]{1,0:T(8,128)(2,1)S(1)} %collective-permute-done.4.o4), channel_id=1, source_target_pairs={{0,64},{64,0},{128,192},{192,128},{256,320},{320,256},{384,448},{4... | collective-permute-start | bytes 454664 | tf_op jit(solution)/shard_map/ppermute | solution.py:40
  52.3 10.1 %attention_grads.1 = (bf16[2,592,256]{2,1,0:T(8,128)(2,1)}, bf16[2,592,256]{2,1,0:T(8,128)(2,1)}, bf16[592,256]{1,0:T(8,128)(2,1)}) custom-call(s32[2]{0:T(128)} %pad_add_fusion.info, bf16[592,128]{1,0:T(8,128)(2,1)} %copy-done.2, bf16[592,128]{1,0:T(8,128)(2,1)} %copy-done.10, bf16[592,128]{1,0:T(8,128)(2,1)} %copy-done.11, bf16[592,128]{1,0:T(8,128)(2,1)} %copy-done.12, ...), custom_call_target="tpu_custom_call" | custom-call | tf_op jit(solution)/shard_map/attention_grads/pallas_call | solution.py:133
  62.4 2.3 %collective-permute-start.10 = (bf16[2,592,256]{2,1,0:T(8,128)(2,1)}, bf16[2,592,256]{2,1,0:T(8,128)(2,1)S(1)}, u32[]{:S(2)}, u32[]{:S(2)}) collective-permute-start(bf16[2,592,256]{2,1,0:T(8,128)(2,1)} %get-tuple-element.9), channel_id=1, source_target_pairs={{0,64},{64,0},{128,192},{192,128},{256,320},{320,256},{384,448},{4... | collective-permute-start | bytes 1818632 | tf_op jit(solution)/shard_map/ppermute | solution.py:40
  64.7 1.9 %collective-permute-done.10 = bf16[2,592,256]{2,1,0:T(8,128)(2,1)S(1)} collective-permute-done((bf16[2,592,256]{2,1,0:T(8,128)(2,1)}, bf16[2,592,256]{2,1,0:T(8,128)(2,1)S(1)}, u32[]{:S(2)}, u32[]{:S(2)}) %collective-permute-start.10) | collective-permute-done | bytes 606240 | tf_op jit(solution)/shard_map/ppermute | solution.py:40
  67.7 4.7 %collective-permute-start.11 = (bf16[592,256]{1,0:T(8,128)(2,1)S(1)}, bf16[592,256]{1,0:T(8,128)(2,1)S(1)}, u32[]{:S(2)}, u32[]{:S(2)}) collective-permute-start(bf16[592,256]{1,0:T(8,128)(2,1)S(1)} %fusion.3), channel_id=1, source_target_pairs={{0,128},{64,960},{128,256},{192,64},{256,384},{320,192},{384,512},... | collective-permute-start | bytes 909320 | tf_op jit(solution)/shard_map/ppermute | solution.py:36
  72.4 5.2 %collective-permute-done.11 = bf16[592,256]{1,0:T(8,128)(2,1)S(1)} collective-permute-done((bf16[592,256]{1,0:T(8,128)(2,1)S(1)}, bf16[592,256]{1,0:T(8,128)(2,1)S(1)}, u32[]{:S(2)}, u32[]{:S(2)}) %collective-permute-start.11) | collective-permute-done | bytes 303136 | tf_op jit(solution)/shard_map/ppermute | solution.py:36
  78.7 3.5 %collective-permute-start.12 = (bf16[592,256]{1,0:T(8,128)(2,1)S(1)}, bf16[592,256]{1,0:T(8,128)(2,1)S(1)}, u32[]{:S(2)}, u32[]{:S(2)}) collective-permute-start(bf16[592,256]{1,0:T(8,128)(2,1)S(1)} %fusion.2), channel_id=1, source_target_pairs={{0,128},{64,960},{128,256},{192,64},{256,384},{320,192},{384,512},... | collective-permute-start | bytes 909320 | tf_op jit(solution)/shard_map/ppermute | solution.py:36
  82.3 6.4 %collective-permute-done.12 = bf16[592,256]{1,0:T(8,128)(2,1)S(1)} collective-permute-done((bf16[592,256]{1,0:T(8,128)(2,1)S(1)}, bf16[592,256]{1,0:T(8,128)(2,1)S(1)}, u32[]{:S(2)}, u32[]{:S(2)}) %collective-permute-start.12) | collective-permute-done | bytes 303136 | tf_op jit(solution)/shard_map/ppermute | solution.py:36
  88.7 1.9 %collective-permute-start.13 = (bf16[592,256]{1,0:T(8,128)(2,1)S(1)}, bf16[592,256]{1,0:T(8,128)(2,1)S(1)}, u32[]{:S(2)}, u32[]{:S(2)}) collective-permute-start(bf16[592,256]{1,0:T(8,128)(2,1)S(1)} %add_convert_fusion.1), channel_id=1, source_target_pairs={{0,64},{64,0},{128,192},{192,128},{256,320},{320,256},{384,448},{4... | collective-permute-start | bytes 909320 | tf_op jit(solution)/shard_map/ppermute | solution.py:40
  92.3 2.3 %collective-permute-start.14 = (bf16[592,256]{1,0:T(8,128)(2,1)S(1)}, bf16[592,256]{1,0:T(8,128)(2,1)S(1)}, u32[]{:S(2)}, u32[]{:S(2)}) collective-permute-start(bf16[592,256]{1,0:T(8,128)(2,1)S(1)} %add_convert_fusion.g0), channel_id=1, source_target_pairs={{0,128},{64,960},{128,256},{192,64},{256,384},{320,192},{384,512},... | collective-permute-start | bytes 909320 | tf_op jit(solution)/shard_map/ppermute | solution.py:36
  94.6 7.6 %collective-permute-done.14.r1 = bf16[592,256]{1,0:T(8,128)(2,1)S(1)} collective-permute-done((bf16[592,256]{1,0:T(8,128)(2,1)S(1)}, bf16[592,256]{1,0:T(8,128)(2,1)S(1)}, u32[]{:S(2)}, u32[]{:S(2)}) %collective-permute-start.14) | collective-permute-done | bytes 303136 | tf_op jit(solution)/shard_map/ppermute | solution.py:36
  102.3 1.9 %collective-permute-start.15 = (bf16[592,256]{1,0:T(8,128)(2,1)S(1)}, bf16[592,256]{1,0:T(8,128)(2,1)S(1)}, u32[]{:S(2)}, u32[]{:S(2)}) collective-permute-start(bf16[592,256]{1,0:T(8,128)(2,1)S(1)} %collective-permute-done.14.r1), channel_id=1, source_target_pairs={{0,128},{64,960},{128,256},{192,64},{256,384},{320,192},{384,512},... | collective-permute-start | bytes 909320 | tf_op jit(solution)/shard_map/ppermute | solution.py:36
  104.2 8.0 %collective-permute-done.15.r2 = bf16[592,256]{1,0:T(8,128)(2,1)S(1)} collective-permute-done((bf16[592,256]{1,0:T(8,128)(2,1)S(1)}, bf16[592,256]{1,0:T(8,128)(2,1)S(1)}, u32[]{:S(2)}, u32[]{:S(2)}) %collective-permute-start.15) | collective-permute-done | bytes 303136 | tf_op jit(solution)/shard_map/ppermute | solution.py:36
  112.2 1.9 %collective-permute-start.16 = (bf16[592,256]{1,0:T(8,128)(2,1)S(1)}, bf16[592,256]{1,0:T(8,128)(2,1)S(1)}, u32[]{:S(2)}, u32[]{:S(2)}) collective-permute-start(bf16[592,256]{1,0:T(8,128)(2,1)S(1)} %collective-permute-done.15.r2), channel_id=1, source_target_pairs={{0,128},{64,960},{128,256},{192,64},{256,384},{320,192},{384,512},... | collective-permute-start | bytes 909320 | tf_op jit(solution)/shard_map/ppermute | solution.py:36
  114.1 1.9 %collective-permute-start.17 = (bf16[592,256]{1,0:T(8,128)(2,1)S(1)}, bf16[592,256]{1,0:T(8,128)(2,1)S(1)}, u32[]{:S(2)}, u32[]{:S(2)}) collective-permute-start(bf16[592,256]{1,0:T(8,128)(2,1)S(1)} %collective-permute-done.14.r1), channel_id=1, source_target_pairs={{0,64},{64,0},{128,192},{192,128},{256,320},{320,256},{384,448},{4... | collective-permute-start | bytes 909320 | tf_op jit(solution)/shard_map/ppermute | solution.py:40
  116.0 2.4 %collective-permute-start.18 = (bf16[592,256]{1,0:T(8,128)(2,1)S(1)}, bf16[592,256]{1,0:T(8,128)(2,1)S(1)}, u32[]{:S(2)}, u32[]{:S(2)}) collective-permute-start(bf16[592,256]{1,0:T(8,128)(2,1)S(1)} %collective-permute-done.15.r2), channel_id=1, source_target_pairs={{0,64},{64,0},{128,192},{192,128},{256,320},{320,256},{384,448},{4... | collective-permute-start | bytes 909320 | tf_op jit(solution)/shard_map/ppermute | solution.py:40
  118.4 3.6 %collective-permute-done.16.r3 = bf16[592,256]{1,0:T(8,128)(2,1)S(1)} collective-permute-done((bf16[592,256]{1,0:T(8,128)(2,1)S(1)}, bf16[592,256]{1,0:T(8,128)(2,1)S(1)}, u32[]{:S(2)}, u32[]{:S(2)}) %collective-permute-start.16) | collective-permute-done | bytes 303136 | tf_op jit(solution)/shard_map/ppermute | solution.py:36
  122.1 1.9 %collective-permute-start.20 = (bf16[592,128]{1,0:T(8,128)(2,1)S(1)}, bf16[592,128]{1,0:T(8,128)(2,1)S(1)}, u32[]{:S(2)}, u32[]{:S(2)}) collective-permute-start(bf16[592,128]{1,0:T(8,128)(2,1)S(1)} %slice_select_fusion), channel_id=1, source_target_pairs={{0,128},{64,960},{128,256},{192,64},{256,384},{320,192},{384,512},... | collective-permute-start | bytes 454664 | tf_op jit(solution)/shard_map/ppermute | solution.py:36
  124.0 1.9 %collective-permute-start.19 = (bf16[592,256]{1,0:T(8,128)(2,1)S(1)}, bf16[592,256]{1,0:T(8,128)(2,1)S(1)}, u32[]{:S(2)}, u32[]{:S(2)}) collective-permute-start(bf16[592,256]{1,0:T(8,128)(2,1)S(1)} %collective-permute-done.16.r3), channel_id=1, source_target_pairs={{0,64},{64,0},{128,192},{192,128},{256,320},{320,256},{384,448},{4... | collective-permute-start | bytes 909320 | tf_op jit(solution)/shard_map/ppermute | solution.py:40
  125.9 4.4 %collective-permute-done.20.r4 = bf16[592,128]{1,0:T(8,128)(2,1)S(1)} collective-permute-done((bf16[592,128]{1,0:T(8,128)(2,1)S(1)}, bf16[592,128]{1,0:T(8,128)(2,1)S(1)}, u32[]{:S(2)}, u32[]{:S(2)}) %collective-permute-start.20) | collective-permute-done | bytes 151584 | tf_op jit(solution)/shard_map/ppermute | solution.py:36
  130.4 1.9 %collective-permute-start.21 = (bf16[592,128]{1,0:T(8,128)(2,1)S(1)}, bf16[592,128]{1,0:T(8,128)(2,1)S(1)}, u32[]{:S(2)}, u32[]{:S(2)}) collective-permute-start(bf16[592,128]{1,0:T(8,128)(2,1)S(1)} %collective-permute-done.20.r4), channel_id=1, source_target_pairs={{0,64},{64,0},{128,192},{192,128},{256,320},{320,256},{384,448},{4... | collective-permute-start | bytes 454664 | tf_op jit(solution)/shard_map/ppermute | solution.py:40
  134.5 7.1 %down_grad.1 = (bf16[512,512]{1,0:T(8,128)(2,1)}, bf16[576,128]{1,0:T(8,128)(2,1)}) custom-call(s32[2]{0:T(128)} %pad_add_fusion.info, f32[8,128]{1,0:T(8,128)} %broadcast_in_dim.11.limits, bf16[592,256]{1,0:T(8,128)(2,1)} %copy-done, bf16[592,256]{1,0:T(8,128)(2,1)} %copy-done.5, bf16[592,256]{1,0:T(8,128)(2,1)} %copy-done.6, bf16[592,256]{1,0:T(8,128)(2,1)} %copy-done.1, ...), custom_call_target="tpu_custom_call" | custom-call | tf_op jit(solution)/shard_map/down_grad/pallas_call | solution.py:221
  141.5 33.3 %all_to_all.5 = bf16[64,8,512]{2,1,0:T(8,128)(2,1)S(1)} all-to-all(bf16[64,8,512]{2,1,0:T(8,128)(2,1)} %bitcast.23), channel_id=1, replica_groups=mesh['ctx'=16,'grp'=64] {'grp'}, dimensions={0} | all-to-all | bytes 1048576 | tf_op jit(solution)/shard_map/all_to_all | solution.py:282
  (74 shorter events, 17.1 us)
Async XLA Ops:
  2.2 35.1 %copy-start.2 = (bf16[592,128]{1,0:T(8,128)(2,1)}, bf16[592,128]{1,0:T(8,128)(2,1)S(1)}, u32[]{:S(2)}) copy-start(bf16[592,128]{1,0:T(8,128)(2,1)S(1)} %fusion.5.o0) | copy-start | bytes 454660
  2.2 34.7 %copy-start.3 = (bf16[1,4,65536]{2,1,0:T(4,128)(2,1)S(1)}, bf16[1,4,65536]{2,1,0:T(4,128)(2,1)}, u32[]{:S(2)}) copy-start(bf16[1,4,65536]{2,1,0:T(4,128)(2,1)} %param.8) | copy-start | bytes 1572868
  2.2 25.2 %collective-permute-start.3 = (bf16[592,128]{1,0:T(8,128)(2,1)S(1)}, bf16[592,128]{1,0:T(8,128)(2,1)}, u32[]{:S(2)}, u32[]{:S(2)}) collective-permute-start(bf16[592,128]{1,0:T(8,128)(2,1)S(1)} %fusion.5.o0), channel_id=1, source_target_pairs={{0,768},{64,832},{128,896},{192,960},{256,0},{320,64},{384,128},{4... | collective-permute-start | bytes 454664 | tf_op jit(solution)/shard_map/ppermute | solution.py:36
  18.8 18.8 %collective-permute-start = (bf16[592,128]{1,0:T(8,128)(2,1)S(1)}, bf16[592,128]{1,0:T(8,128)(2,1)S(1)}, u32[]{:S(2)}, u32[]{:S(2)}) collective-permute-start(bf16[592,128]{1,0:T(8,128)(2,1)S(1)} %fusion.5.o0), channel_id=1, source_target_pairs={{0,128},{64,192},{128,256},{192,320},{256,384},{320,448},{384,512}... | collective-permute-start | bytes 454664 | tf_op jit(solution)/shard_map/ppermute | solution.py:36
  23.1 18.5 %collective-permute-start.1 = (bf16[592,128]{1,0:T(8,128)(2,1)S(1)}, bf16[592,128]{1,0:T(8,128)(2,1)S(1)}, u32[]{:S(2)}, u32[]{:S(2)}) collective-permute-start(bf16[592,128]{1,0:T(8,128)(2,1)S(1)} %fusion.5.o0), channel_id=1, source_target_pairs={{0,256},{64,320},{128,384},{192,448},{256,512},{320,576},{384,640}... | collective-permute-start | bytes 454664 | tf_op jit(solution)/shard_map/ppermute | solution.py:36
  25.0 18.7 %collective-permute-start.2 = (bf16[592,128]{1,0:T(8,128)(2,1)S(1)}, bf16[592,128]{1,0:T(8,128)(2,1)S(1)}, u32[]{:S(2)}, u32[]{:S(2)}) collective-permute-start(bf16[592,128]{1,0:T(8,128)(2,1)S(1)} %fusion.5.o0), channel_id=1, source_target_pairs={{0,384},{64,448},{128,512},{192,576},{256,640},{320,704},{384,768}... | collective-permute-start | bytes 454664 | tf_op jit(solution)/shard_map/ppermute | solution.py:36
  27.5 18.4 %collective-permute-start.4 = (bf16[592,128]{1,0:T(8,128)(2,1)}, bf16[592,128]{1,0:T(8,128)(2,1)S(1)}, u32[]{:S(2)}, u32[]{:S(2)}) collective-permute-start(bf16[592,128]{1,0:T(8,128)(2,1)} %collective-permute-done.3), channel_id=1, source_target_pairs={{0,768},{64,832},{128,896},{192,960},{256,0},{320,64},{384,128},{4... | collective-permute-start | bytes 454664 | tf_op jit(solution)/shard_map/ppermute | solution.py:36
  33.0 18.5 %collective-permute-start.5 = (bf16[592,128]{1,0:T(8,128)(2,1)S(1)}, bf16[592,128]{1,0:T(8,128)(2,1)S(1)}, u32[]{:S(2)}, u32[]{:S(2)}) collective-permute-start(bf16[592,128]{1,0:T(8,128)(2,1)S(1)} %fusion.5.o0), channel_id=1, source_target_pairs={{0,64},{64,0},{128,192},{192,128},{256,320},{320,256},{384,448},{4... | collective-permute-start | bytes 454664 | tf_op jit(solution)/shard_map/ppermute | solution.py:40
  37.6 11.9 %copy-start.10 = (bf16[592,128]{1,0:T(8,128)(2,1)}, bf16[592,128]{1,0:T(8,128)(2,1)S(1)}, u32[]{:S(2)}) copy-start(bf16[592,128]{1,0:T(8,128)(2,1)S(1)} %collective-permute-done.o1) | copy-start | bytes 454660
  37.6 13.9 %collective-permute-start.6 = (bf16[592,128]{1,0:T(8,128)(2,1)S(1)}, bf16[592,128]{1,0:T(8,128)(2,1)S(1)}, u32[]{:S(2)}, u32[]{:S(2)}) collective-permute-start(bf16[592,128]{1,0:T(8,128)(2,1)S(1)} %collective-permute-done.o1), channel_id=1, source_target_pairs={{0,64},{64,0},{128,192},{192,128},{256,320},{320,256},{384,448},{4... | collective-permute-start | bytes 454664 | tf_op jit(solution)/shard_map/ppermute | solution.py:40
  41.5 7.9 %copy-start.11 = (bf16[592,128]{1,0:T(8,128)(2,1)}, bf16[592,128]{1,0:T(8,128)(2,1)S(1)}, u32[]{:S(2)}) copy-start(bf16[592,128]{1,0:T(8,128)(2,1)S(1)} %collective-permute-done.1.o2) | copy-start | bytes 454660
  41.5 10.0 %collective-permute-start.7 = (bf16[592,128]{1,0:T(8,128)(2,1)S(1)}, bf16[592,128]{1,0:T(8,128)(2,1)S(1)}, u32[]{:S(2)}, u32[]{:S(2)}) collective-permute-start(bf16[592,128]{1,0:T(8,128)(2,1)S(1)} %collective-permute-done.1.o2), channel_id=1, source_target_pairs={{0,64},{64,0},{128,192},{192,128},{256,320},{320,256},{384,448},{4... | collective-permute-start | bytes 454664 | tf_op jit(solution)/shard_map/ppermute | solution.py:40
  43.7 7.8 %collective-permute-start.8 = (bf16[592,128]{1,0:T(8,128)(2,1)S(1)}, bf16[592,128]{1,0:T(8,128)(2,1)}, u32[]{:S(2)}, u32[]{:S(2)}) collective-permute-start(bf16[592,128]{1,0:T(8,128)(2,1)S(1)} %collective-permute-done.2.o3), channel_id=1, source_target_pairs={{0,64},{64,0},{128,192},{192,128},{256,320},{320,256},{384,448},{4... | collective-permute-start | bytes 454664 | tf_op jit(solution)/shard_map/ppermute | solution.py:40
  45.9 5.6 %collective-permute-start.9 = (bf16[592,128]{1,0:T(8,128)(2,1)S(1)}, bf16[592,128]{1,0:T(8,128)(2,1)}, u32[]{:S(2)}, u32[]{:S(2)}) collective-permute-start(bf16[592,128]{1,0:T(8,128)(2,1)S(1)} %collective-permute-done.4.o4), channel_id=1, source_target_pairs={{0,64},{64,0},{128,192},{192,128},{256,320},{320,256},{384,448},{4... | collective-permute-start | bytes 454664 | tf_op jit(solution)/shard_map/ppermute | solution.py:40
  62.4 26.2 %copy-start.4 = (bf16[592,256]{1,0:T(8,128)(2,1)S(1)}, bf16[592,256]{1,0:T(8,128)(2,1)}, u32[]{:S(2)}) copy-start(bf16[592,256]{1,0:T(8,128)(2,1)} %get-tuple-element.7) | copy-start | bytes 909316
  62.4 4.3 %collective-permute-start.10 = (bf16[2,592,256]{2,1,0:T(8,128)(2,1)}, bf16[2,592,256]{2,1,0:T(8,128)(2,1)S(1)}, u32[]{:S(2)}, u32[]{:S(2)}) collective-permute-start(bf16[2,592,256]{2,1,0:T(8,128)(2,1)} %get-tuple-element.9), channel_id=1, source_target_pairs={{0,64},{64,0},{128,192},{192,128},{256,320},{320,256},{384,448},{4... | collective-permute-start | bytes 1818632 | tf_op jit(solution)/shard_map/ppermute | solution.py:40
  67.7 9.9 %collective-permute-start.11 = (bf16[592,256]{1,0:T(8,128)(2,1)S(1)}, bf16[592,256]{1,0:T(8,128)(2,1)S(1)}, u32[]{:S(2)}, u32[]{:S(2)}) collective-permute-start(bf16[592,256]{1,0:T(8,128)(2,1)S(1)} %fusion.3), channel_id=1, source_target_pairs={{0,128},{64,960},{128,256},{192,64},{256,384},{320,192},{384,512},... | collective-permute-start | bytes 909320 | tf_op jit(solution)/shard_map/ppermute | solution.py:36
  78.7 54.9 %copy-start.19 = (f32[1,8]{1,0:T(1,128)S(1)}, f32[1,8]{1,0:T(1,128)}, u32[]{:S(2)}) copy-start(f32[1,8]{1,0:T(1,128)} %param.11) | copy-start | bytes 100
  78.7 9.9 %collective-permute-start.12 = (bf16[592,256]{1,0:T(8,128)(2,1)S(1)}, bf16[592,256]{1,0:T(8,128)(2,1)S(1)}, u32[]{:S(2)}, u32[]{:S(2)}) collective-permute-start(bf16[592,256]{1,0:T(8,128)(2,1)S(1)} %fusion.2), channel_id=1, source_target_pairs={{0,128},{64,960},{128,256},{192,64},{256,384},{320,192},{384,512},... | collective-permute-start | bytes 909320 | tf_op jit(solution)/shard_map/ppermute | solution.py:36
  88.7 3.5 %collective-permute-start.13 = (bf16[592,256]{1,0:T(8,128)(2,1)S(1)}, bf16[592,256]{1,0:T(8,128)(2,1)S(1)}, u32[]{:S(2)}, u32[]{:S(2)}) collective-permute-start(bf16[592,256]{1,0:T(8,128)(2,1)S(1)} %add_convert_fusion.1), channel_id=1, source_target_pairs={{0,64},{64,0},{128,192},{192,128},{256,320},{320,256},{384,448},{4... | collective-permute-start | bytes 909320 | tf_op jit(solution)/shard_map/ppermute | solution.py:40
  92.3 42.1 %copy-start = (bf16[592,256]{1,0:T(8,128)(2,1)}, bf16[592,256]{1,0:T(8,128)(2,1)S(1)}, u32[]{:S(2)}) copy-start(bf16[592,256]{1,0:T(8,128)(2,1)S(1)} %add_convert_fusion.g0) | copy-start | bytes 909316
  92.3 9.9 %collective-permute-start.14 = (bf16[592,256]{1,0:T(8,128)(2,1)S(1)}, bf16[592,256]{1,0:T(8,128)(2,1)S(1)}, u32[]{:S(2)}, u32[]{:S(2)}) collective-permute-start(bf16[592,256]{1,0:T(8,128)(2,1)S(1)} %add_convert_fusion.g0), channel_id=1, source_target_pairs={{0,128},{64,960},{128,256},{192,64},{256,384},{320,192},{384,512},... | collective-permute-start | bytes 909320 | tf_op jit(solution)/shard_map/ppermute | solution.py:36
  102.2 32.1 %copy-start.5 = (bf16[592,256]{1,0:T(8,128)(2,1)}, bf16[592,256]{1,0:T(8,128)(2,1)S(1)}, u32[]{:S(2)}) copy-start(bf16[592,256]{1,0:T(8,128)(2,1)S(1)} %collective-permute-done.14.r1) | copy-start | bytes 909316
  102.3 9.9 %collective-permute-start.15 = (bf16[592,256]{1,0:T(8,128)(2,1)S(1)}, bf16[592,256]{1,0:T(8,128)(2,1)S(1)}, u32[]{:S(2)}, u32[]{:S(2)}) collective-permute-start(bf16[592,256]{1,0:T(8,128)(2,1)S(1)} %collective-permute-done.14.r1), channel_id=1, source_target_pairs={{0,128},{64,960},{128,256},{192,64},{256,384},{320,192},{384,512},... | collective-permute-start | bytes 909320 | tf_op jit(solution)/shard_map/ppermute | solution.py:36
  112.2 22.2 %copy-start.6 = (bf16[592,256]{1,0:T(8,128)(2,1)}, bf16[592,256]{1,0:T(8,128)(2,1)S(1)}, u32[]{:S(2)}) copy-start(bf16[592,256]{1,0:T(8,128)(2,1)S(1)} %collective-permute-done.15.r2) | copy-start | bytes 909316
  112.2 9.9 %collective-permute-start.16 = (bf16[592,256]{1,0:T(8,128)(2,1)S(1)}, bf16[592,256]{1,0:T(8,128)(2,1)S(1)}, u32[]{:S(2)}, u32[]{:S(2)}) collective-permute-start(bf16[592,256]{1,0:T(8,128)(2,1)S(1)} %collective-permute-done.15.r2), channel_id=1, source_target_pairs={{0,128},{64,960},{128,256},{192,64},{256,384},{320,192},{384,512},... | collective-permute-start | bytes 909320 | tf_op jit(solution)/shard_map/ppermute | solution.py:36
  114.1 18.2 %collective-permute-start.17 = (bf16[592,256]{1,0:T(8,128)(2,1)S(1)}, bf16[592,256]{1,0:T(8,128)(2,1)S(1)}, u32[]{:S(2)}, u32[]{:S(2)}) collective-permute-start(bf16[592,256]{1,0:T(8,128)(2,1)S(1)} %collective-permute-done.14.r1), channel_id=1, source_target_pairs={{0,64},{64,0},{128,192},{192,128},{256,320},{320,256},{384,448},{4... | collective-permute-start | bytes 909320 | tf_op jit(solution)/shard_map/ppermute | solution.py:40
  116.0 16.3 %collective-permute-start.18 = (bf16[592,256]{1,0:T(8,128)(2,1)S(1)}, bf16[592,256]{1,0:T(8,128)(2,1)S(1)}, u32[]{:S(2)}, u32[]{:S(2)}) collective-permute-start(bf16[592,256]{1,0:T(8,128)(2,1)S(1)} %collective-permute-done.15.r2), channel_id=1, source_target_pairs={{0,64},{64,0},{128,192},{192,128},{256,320},{320,256},{384,448},{4... | collective-permute-start | bytes 909320 | tf_op jit(solution)/shard_map/ppermute | solution.py:40
  122.1 12.3 %copy-start.1 = (bf16[592,256]{1,0:T(8,128)(2,1)}, bf16[592,256]{1,0:T(8,128)(2,1)S(1)}, u32[]{:S(2)}) copy-start(bf16[592,256]{1,0:T(8,128)(2,1)S(1)} %collective-permute-done.16.r3) | copy-start | bytes 909316
  122.1 8.3 %collective-permute-start.20 = (bf16[592,128]{1,0:T(8,128)(2,1)S(1)}, bf16[592,128]{1,0:T(8,128)(2,1)S(1)}, u32[]{:S(2)}, u32[]{:S(2)}) collective-permute-start(bf16[592,128]{1,0:T(8,128)(2,1)S(1)} %slice_select_fusion), channel_id=1, source_target_pairs={{0,128},{64,960},{128,256},{192,64},{256,384},{320,192},{384,512},... | collective-permute-start | bytes 454664 | tf_op jit(solution)/shard_map/ppermute | solution.py:36
  124.0 9.6 %collective-permute-start.19 = (bf16[592,256]{1,0:T(8,128)(2,1)S(1)}, bf16[592,256]{1,0:T(8,128)(2,1)S(1)}, u32[]{:S(2)}, u32[]{:S(2)}) collective-permute-start(bf16[592,256]{1,0:T(8,128)(2,1)S(1)} %collective-permute-done.16.r3), channel_id=1, source_target_pairs={{0,64},{64,0},{128,192},{192,128},{256,320},{320,256},{384,448},{4... | collective-permute-start | bytes 909320 | tf_op jit(solution)/shard_map/ppermute | solution.py:40
  130.4 3.3 %collective-permute-start.21 = (bf16[592,128]{1,0:T(8,128)(2,1)S(1)}, bf16[592,128]{1,0:T(8,128)(2,1)S(1)}, u32[]{:S(2)}, u32[]{:S(2)}) collective-permute-start(bf16[592,128]{1,0:T(8,128)(2,1)S(1)} %collective-permute-done.20.r4), channel_id=1, source_target_pairs={{0,64},{64,0},{128,192},{192,128},{256,320},{320,256},{384,448},{4... | collective-permute-start | bytes 454664 | tf_op jit(solution)/shard_map/ppermute | solution.py:40
  (10 other events, 21.2 us)

commit v2 on v1

--- a/solution.py
+++ b/solution.py
@@ -41,25 +41,18 @@
 
 
 def attention_kernel(
-    info, o0, o1, o2, o3, o4, p0, p1, p2, p3, p4, rows_ref, cols_ref,
+    info, own, par, rows_ref, cols_ref,
     keep_ref, send_ref, mid_ref, keys, score, dprob, mixed,
 ):
     chip, core = info[0], info[1]
-    own, par = (o0, o1, o2, o3, o4), (p0, p1, p2, p3, p4)
-
-    @pl.when(core == 0)
-    def _():
-        for k in range(BACK):
-            keys[k, :, :TOK] = own[k][...]
-            keys[k, :, TOK:] = par[k][...]
-
-    @pl.when(core != 0)
-    def _():
-        for k in range(BACK):
-            keys[k, :, :TOK] = par[k][...]
-            keys[k, :, TOK:] = own[k][...]
-
-    own_ids = o0[KW:ROWS, :].astype(jnp.float32)[0:1]
+
+    mine = pl.ds(pl.multiple_of(core * TOK, TOK), TOK)
+    other = pl.ds(pl.multiple_of((1 - core) * TOK, TOK), TOK)
+    for k in range(BACK):
+        keys[k, :, mine] = own[k]
+        keys[k, :, other] = par[k]
+
+    own_ids = own[0, KW:ROWS, :].astype(jnp.float32)[0:1]
     lane = lax.broadcasted_iota(jnp.int32, (1, TOK), 1)
     query_ids = [
         jnp.sum(jnp.where(lane == TOK - Q_DEV + i, own_ids, 0.0), axis=1, keepdims=True)
@@ -103,21 +96,16 @@
         keep_ref[slot, KW:, :] = blank
         send_ref[slot, KW:, :] = blank
     mid_ref[KW:, :] = (keys[2, KW:ROWS, :].astype(jnp.float32) * 0.5).astype(jnp.bfloat16)
-    for k in range(BACK):
+
+    def grads(k):
         g = jnp.dot(cols_ref[...], mixed[k], preferred_element_type=jnp.float32)
-        g = g.astype(jnp.bfloat16)
-        if k == 2:
-            mid_ref[:KW, :] = g
-            continue
-        slot, keeper = (k, 0) if k < 2 else (4 - k, 1)
-
-        @pl.when(core == keeper)
-        def _():
-            keep_ref[slot, :KW, :] = g
-
-        @pl.when(core != keeper)
-        def _():
-            send_ref[slot, :KW, :] = g
+        return g.astype(jnp.bfloat16)
+
+    for slot in range(2):
+        send_ref[slot, :KW, :] = grads(jnp.where(core == 0, 4 - slot, slot))
+    for slot in range(2):
+        keep_ref[slot, :KW, :] = grads(jnp.where(core == 0, slot, 4 - slot))
+    mid_ref[:KW, :] = grads(2)
 
 
 def vmem():
@@ -133,7 +121,7 @@
     return pl.pallas_call(
         attention_kernel,
         out_shape=(block, block, jax.ShapeDtypeStruct((ROWS, PAIR), jnp.bfloat16)),
-        in_specs=[smem()] + [vmem()] * 12,
+        in_specs=[smem()] + [vmem()] * 4,
         out_specs=(vmem(), vmem(), vmem()),
         scratch_shapes=[
             pltpu.VMEM((BACK, ROWS, PAIR), jnp.bfloat16),
@@ -143,31 +131,29 @@
         ],
         compiler_params=pltpu.CompilerParams(vmem_limit_bytes=VMEM_BYTES),
         name="attention_grads",
-    )(info, *own, *par, rows, cols)
+    )(info, own, par, rows, cols)
 
 
 def down_kernel(
-    info, limits, g0, r1, r2, r3, s1, s2, s3, r4, s4, hidden,
-    out_ref, own_ref, last, scaled, weight,
+    info, limits, g0, r12, r34, s12, s34, hidden, out_ref, own_ref, last, scaled, weight,
 ):
     chip, core = info[0], info[1]
+    mine = pl.ds(pl.multiple_of(core * TOK, TOK), TOK)
+    other = pl.ds(pl.multiple_of((1 - core) * TOK, TOK), TOK)
+    last[:, mine] = r34[:, PAIR:]
+    last[:, other] = s34[:, PAIR:]
 
     @pl.when(core == 0)
     def _():
-        last[:, :TOK] = r4[...]
-        last[:, TOK:] = s4[...]
-        own_ref[...] = s2[:KW, :TOK]
+        own_ref[...] = s12[1, :KW, :TOK]
 
     @pl.when(core != 0)
     def _():
-        last[:, :TOK] = s4[...]
-        last[:, TOK:] = r4[...]
-        own_ref[...] = r2[:KW, TOK:]
+        own_ref[...] = r12[1, :KW, TOK:]
 
     away = jnp.where(core == 0, -1, 1)
-    blocks = [(g0, 0)]
-    blocks += [(r, away * (j + 1)) for j, r in enumerate((r1, r2, r3))]
-    blocks += [(s, -away * (j + 1)) for j, s in enumerate((s1, s2, s3))]
+    blocks = [(g0, 0), (r12.at[0], away), (r12.at[1], 2 * away), (r34.at[:, :PAIR], 3 * away)]
+    blocks += [(s12.at[0], -away), (s12.at[1], -2 * away), (s34.at[:, :PAIR], -3 * away)]
     blocks += [(last, 4)]
     doc = lax.broadcasted_iota(jnp.int32, (NDOC, PAIR), 0).astype(jnp.float32)
     squares = jnp.zeros((NDOC, PAIR), jnp.float32)
@@ -224,7 +210,7 @@
             jax.ShapeDtypeStruct((SLOT, SLOT), jnp.bfloat16),
             jax.ShapeDtypeStruct((KW, TOK), jnp.bfloat16),
         ),
-        in_specs=[smem()] + [vmem()] * 11,
+        in_specs=[smem()] + [vmem()] * 7,
         out_specs=(vmem(), vmem()),
         scratch_shapes=[
             pltpu.VMEM((ROWS, PAIR), jnp.bfloat16),
@@ -249,28 +235,36 @@
     info = jnp.stack([position // 2, core]).astype(jnp.int32)
     ids = jnp.pad(doc_ids.astype(jnp.bfloat16), ((0, ROWS - KW - 1), (0, 0)))
     keys = jnp.concatenate([latent[0].T, ids], axis=0)
-    own = [keys, chip_shift(keys, 1, 1), chip_shift(keys, 2, 2), chip_shift(keys, 3, 3)]
-    own.append(chip_shift(chip_shift(keys, -2, -2), -2, -2))
-    par = [core_swap(value) for value in own]
-    query_rows = queries[0].reshape(QH, KW)
-    grad_rows = out_grad[0].reshape(QH, LATENT)
+    near = chip_shift(keys, 1, 1)
+    fourth = chip_shift(keys, 4, 4)
+    next_near = chip_shift(keys, 2, 2)
+    next_near, query_rows, grad_rows = lax.optimization_barrier((next_near, queries, out_grad))
+    query_rows = query_rows[0].reshape(QH, KW)
+    grad_rows = grad_rows[0].reshape(QH, LATENT)
     rows = jnp.concatenate([query_rows, jnp.pad(grad_rows, ((0, 0), (0, KW - LATENT)))], axis=0)
-    keep, send, mid = attention(info, own, par, rows, rows.T)
+    cols = rows.T
+    limits = jnp.broadcast_to(clip_limits[0][:, None], (NDOC, 128))
+    own = jnp.stack([keys, near, next_near, chip_shift(near, 2, 2), fourth])
+    own, rows, cols, info, limits = lax.optimization_barrier((own, rows, cols, info, limits))
+    par = core_swap(own)
+    keep, send, mid = attention(info, own, par, rows, cols)
 
     arrived = core_swap(send)
-    moved = chip_shift(added(keep[0], arrived[0]), 1, -1)
-    moved = chip_shift(added(keep[1], arrived[1], moved), 1, -1)
-    mine = added(mid, moved)
+    far = chip_shift(added(keep[0], arrived[0]), 2, -2)
+    close = chip_shift(added(keep[1], arrived[1]), 1, -1)
+    mine = added(mid, far, close)
     total = added(mine, core_swap(mine))
 
-    ring = [total]
-    for _ in range(3):
-        ring.append(chip_shift(ring[-1], 1, -1))
-    half = jnp.where(core == 0, ring[3][:, :TOK], ring[3][:, TOK:])
-    ring.append(chip_shift(half, 1, -1))
-    swapped = [core_swap(value) for value in ring[1:]]
-    limits = jnp.broadcast_to(clip_limits[0][:, None], (NDOC, 128))
-    blocks = ring[:4] + swapped[:3] + [ring[4], swapped[3]]
+    one = chip_shift(total, 1, -1)
+    two = chip_shift(total, 2, -2)
+    three = chip_shift(one, 2, -2)
+    half = jnp.where(core == 0, two[:, :TOK], two[:, TOK:])
+    four = chip_shift(half, 2, -2)
+    one, two, three = lax.optimization_barrier((one, two, three))
+    nearer = jnp.stack([one, two])
+    nearer_par = core_swap(nearer)
+    farther = jnp.concatenate([three, four], axis=1)
+    blocks = [total, nearer, farther, nearer_par, core_swap(farther)]
     chunks, own_grad = down_grad(info, limits, blocks, hidden[0].T)
     return own_grad, chunks
 

time: 177 us -> 159 us (0.90)
  starting transfers between devices: 69.9 us -> 58 us
  waiting for transfers between devices: 41.9 us -> 35.9 us
  local copies, waits for them, and re-layouts: 5.8 us -> 7.89 us
    ppermute x11 -> x5, starting transfers between devices: 22.9 us -> 9.83 us  [core_swap(): return lax.ppermute(value, 'ctx', [(i, i ^ 1) for i in range(2 * CHIPS)])]
    ppermute x11 -> x10, waiting for transfers between devices: 37.1 us -> 29.7 us  [chip_shift(): return lax.ppermute(value, 'ctx', pairs)]
    unnamed x40 -> x24, local copies, waits for them, and re-layouts: 0.83 us -> 2.87 us
    ppermute x11 -> x5, waiting for transfers between devices: 4.83 us -> 6.16 us  [core_swap(): return lax.ppermute(value, 'ctx', [(i, i ^ 1) for i in range(2 * CHIPS)])]
    ppermute x11 -> x10, starting transfers between devices: 47 us -> 48.2 us  [chip_shift(): return lax.ppermute(value, 'ctx', pairs)]
  transfers between devices with their start and end apart: 22 -> 15, of which waited for: 11 -> 11; matrix products, arithmetic and copies ran while one was open for 3% -> 5% of each run, Pallas kernels for 0% -> 0%
where the time goes in v2:
time: 159 us; the launch traced here: 158 us
  starting transfers between devices  58 us (36%)
  waiting for transfers between devices  35.9 us (23%)
  blocking collectives  33.3 us (21%)
  Pallas kernels  15.6 us (10%)
  local copies, waits for them, and re-layouts  7.89 us (5%)
  other arithmetic  6.71 us (4%)
    ppermute x10, starting transfers between devices, chip_shift(): return lax.ppermute(value, 'ctx', pairs)  48.2 us
    all_to_all x1, blocking collectives, on_device(): chunks = lax.all_to_all(chunks, 'grp', 0, 0, tiled=True)  33.3 us
    ppermute x10, waiting for transfers between devices, chip_shift(): return lax.ppermute(value, 'ctx', pairs)  29.7 us
    ppermute x5, starting transfers between devices, core_swap(): return lax.ppermute(value, 'ctx', [(i, i ^ 1) for i in range(2 * CHIPS)])  9.83 us
    pallas_call x1, Pallas kernels, attention(): pl.pallas_call(attention_kernel, out_shape=(block, block, jax.ShapeDtypeS...  8.67 us
    pallas_call x1, Pallas kernels, down_grad(): pl.pallas_call(down_kernel, out_shape=(jax.ShapeDtypeStruct((SLOT, SLOT),...  6.89 us
    ppermute x5, waiting for transfers between devices, core_swap(): return lax.ppermute(value, 'ctx', [(i, i ^ 1) for i in range(2 * CHIPS)])  6.16 us
  transfers between devices with their start and end apart: 15, of which 11 were waited for; matrix products, arithmetic and copies ran while one was open for 5% of the time, Pallas kernels for 0%

profile of v2, /device:TPU:4, one launch (start us, length us, event | category | flops | bytes accessed | tf_op | source)
XLA Modules:
  0.0 158.3 jit_solution(3865896257533813873)
XLA Ops:
  2.3 7.9 %collective-permute-start.1 = (bf16[592,128]{1,0:T(8,128)(2,1)S(1)}, bf16[592,128]{1,0:T(8,128)(2,1)}, u32[]{:S(2)}, u32[]{:S(2)}) collective-permute-start(bf16[592,128]{1,0:T(8,128)(2,1)S(1)} %fusion.5), channel_id=1, source_target_pairs={{0,256},{64,320},{128,384},{192,448},{256,512},{320,576},{384,640}... | collective-permute-start | bytes 454664 | tf_op jit(solution)/shard_map/ppermute | solution.py:36
  10.2 5.2 %collective-permute-start = (bf16[592,128]{1,0:T(8,128)(2,1)S(1)}, bf16[592,128]{1,0:T(8,128)(2,1)S(1)}, u32[]{:S(2)}, u32[]{:S(2)}) collective-permute-start(bf16[592,128]{1,0:T(8,128)(2,1)S(1)} %fusion.5), channel_id=1, source_target_pairs={{0,128},{64,192},{128,256},{192,320},{256,384},{320,448},{384,512}... | collective-permute-start | bytes 454664 | tf_op jit(solution)/shard_map/ppermute | solution.py:36
  15.4 11.9 %collective-permute-start.3 = (bf16[592,128]{1,0:T(8,128)(2,1)S(1)}, bf16[592,128]{1,0:T(8,128)(2,1)S(1)}, u32[]{:S(2)}, u32[]{:S(2)}) collective-permute-start(bf16[592,128]{1,0:T(8,128)(2,1)S(1)} %fusion.5), channel_id=1, source_target_pairs={{0,512},{64,576},{128,640},{192,704},{256,768},{320,832},{384,896}... | collective-permute-start | bytes 454664 | tf_op jit(solution)/shard_map/ppermute | solution.py:36
  28.8 1.5 reshape_squeeze.7
  32.4 1.9 %collective-permute-start.2 = (bf16[592,128]{1,0:T(8,128)(2,1)S(1)}, bf16[592,128]{1,0:T(8,128)(2,1)S(1)}, u32[]{:S(2)}, u32[]{:S(2)}) collective-permute-start(bf16[592,128]{1,0:T(8,128)(2,1)S(1)} %collective-permute-done), channel_id=1, source_target_pairs={{0,256},{64,320},{128,384},{192,448},{256,512},{320,576},{384,640}... | collective-permute-start | bytes 454664 | tf_op jit(solution)/shard_map/ppermute | solution.py:36
  34.3 1.3 fusion.6
  35.6 10.8 %collective-permute-done.2 = bf16[592,128]{1,0:T(8,128)(2,1)S(1)} collective-permute-done((bf16[592,128]{1,0:T(8,128)(2,1)S(1)}, bf16[592,128]{1,0:T(8,128)(2,1)S(1)}, u32[]{:S(2)}, u32[]{:S(2)}) %collective-permute-start.2) | collective-permute-done | bytes 151584 | tf_op jit(solution)/shard_map/ppermute | solution.py:36
  47.3 1.9 %collective-permute-start.4 = (bf16[5,592,128]{2,1,0:T(8,128)(2,1)S(1)}, bf16[5,592,128]{2,1,0:T(8,128)(2,1)S(1)}, u32[]{:S(2)}, u32[]{:S(2)}) collective-permute-start(bf16[5,592,128]{2,1,0:T(8,128)(2,1)S(1)} %bitcast_dynamic-update-slice_fusion.own), channel_id=1, source_target_pairs={{0,64},{64,0},{128,192},{192,128},{256,320},{320,256},{384,448},{4... | collective-permute-start | bytes 2273288 | tf_op jit(solution)/shard_map/ppermute | solution.py:40
  49.2 1.5 copy.11.rows_ref
  52.3 8.7 %attention_grads.1 = (bf16[2,592,256]{2,1,0:T(8,128)(2,1)}, bf16[2,592,256]{2,1,0:T(8,128)(2,1)}, bf16[592,256]{1,0:T(8,128)(2,1)}) custom-call(s32[2]{0:T(128)} %pad_add_fusion.info, bf16[5,592,128]{2,1,0:T(8,128)(2,1)} %copy-done.3, bf16[5,592,128]{2,1,0:T(8,128)(2,1)} %copy-done.4, bf16[1024,576]{1,0:T(8,128)(2,1)} %copy.11.rows_ref, ...), custom_call_target="tpu_custom_call" | custom-call | tf_op jit(solution)/shard_map/attention_grads/pallas_call | solution.py:121
  60.9 2.2 %collective-permute-start.5 = (bf16[2,592,256]{2,1,0:T(8,128)(2,1)}, bf16[2,592,256]{2,1,0:T(8,128)(2,1)S(1)}, u32[]{:S(2)}, u32[]{:S(2)}) collective-permute-start(bf16[2,592,256]{2,1,0:T(8,128)(2,1)} %get-tuple-element.28), channel_id=1, source_target_pairs={{0,64},{64,0},{128,192},{192,128},{256,320},{320,256},{384,448},{4... | collective-permute-start | bytes 1818632 | tf_op jit(solution)/shard_map/ppermute | solution.py:40
  63.1 2.1 %collective-permute-done.5 = bf16[2,592,256]{2,1,0:T(8,128)(2,1)S(1)} collective-permute-done((bf16[2,592,256]{2,1,0:T(8,128)(2,1)}, bf16[2,592,256]{2,1,0:T(8,128)(2,1)S(1)}, u32[]{:S(2)}, u32[]{:S(2)}) %collective-permute-start.5) | collective-permute-done | bytes 606240 | tf_op jit(solution)/shard_map/ppermute | solution.py:40
  65.2 1.2 fusion.2
  66.4 1.9 %collective-permute-start.6 = (bf16[592,256]{1,0:T(8,128)(2,1)S(1)}, bf16[592,256]{1,0:T(8,128)(2,1)S(1)}, u32[]{:S(2)}, u32[]{:S(2)}) collective-permute-start(bf16[592,256]{1,0:T(8,128)(2,1)S(1)} %get-tuple-element.34), channel_id=1, source_target_pairs={{0,256},{64,832},{128,384},{192,960},{256,512},{320,64},{384,640},... | collective-permute-start | bytes 909320 | tf_op jit(solution)/shard_map/ppermute | solution.py:36
  68.3 2.2 %collective-permute-start.7 = (bf16[592,256]{1,0:T(8,128)(2,1)S(1)}, bf16[592,256]{1,0:T(8,128)(2,1)S(1)}, u32[]{:S(2)}, u32[]{:S(2)}) collective-permute-start(bf16[592,256]{1,0:T(8,128)(2,1)S(1)} %get-tuple-element.35), channel_id=1, source_target_pairs={{0,128},{64,960},{128,256},{192,64},{256,384},{320,192},{384,512},... | collective-permute-start | bytes 909320 | tf_op jit(solution)/shard_map/ppermute | solution.py:36
  70.5 8.8 %collective-permute-done.6 = bf16[592,256]{1,0:T(8,128)(2,1)S(1)} collective-permute-done((bf16[592,256]{1,0:T(8,128)(2,1)S(1)}, bf16[592,256]{1,0:T(8,128)(2,1)S(1)}, u32[]{:S(2)}, u32[]{:S(2)}) %collective-permute-start.6) | collective-permute-done | bytes 303136 | tf_op jit(solution)/shard_map/ppermute | solution.py:36
  79.3 2.1 %collective-permute-done.7 = bf16[592,256]{1,0:T(8,128)(2,1)S(1)} collective-permute-done((bf16[592,256]{1,0:T(8,128)(2,1)S(1)}, bf16[592,256]{1,0:T(8,128)(2,1)S(1)}, u32[]{:S(2)}, u32[]{:S(2)}) %collective-permute-start.7) | collective-permute-done | bytes 303136 | tf_op jit(solution)/shard_map/ppermute | solution.py:36
  81.5 1.9 %collective-permute-start.8 = (bf16[592,256]{1,0:T(8,128)(2,1)S(1)}, bf16[592,256]{1,0:T(8,128)(2,1)S(1)}, u32[]{:S(2)}, u32[]{:S(2)}) collective-permute-start(bf16[592,256]{1,0:T(8,128)(2,1)S(1)} %add_convert_fusion.1), channel_id=1, source_target_pairs={{0,64},{64,0},{128,192},{192,128},{256,320},{320,256},{384,448},{4... | collective-permute-start | bytes 909320 | tf_op jit(solution)/shard_map/ppermute | solution.py:40
  83.5 1.6 collective-permute-done.8
  85.1 2.0 %collective-permute-start.9 = (bf16[592,256]{1,0:T(8,128)(2,1)S(1)}, bf16[592,256]{1,0:T(8,128)(2,1)S(1)}, u32[]{:S(2)}, u32[]{:S(2)}) collective-permute-start(bf16[592,256]{1,0:T(8,128)(2,1)S(1)} %add_convert_fusion.g0), channel_id=1, source_target_pairs={{0,128},{64,960},{128,256},{192,64},{256,384},{320,192},{384,512},... | collective-permute-start | bytes 909320 | tf_op jit(solution)/shard_map/ppermute | solution.py:36
  87.1 4.5 %collective-permute-start.10 = (bf16[592,256]{1,0:T(8,128)(2,1)S(1)}, bf16[592,256]{1,0:T(8,128)(2,1)S(1)}, u32[]{:S(2)}, u32[]{:S(2)}) collective-permute-start(bf16[592,256]{1,0:T(8,128)(2,1)S(1)} %add_convert_fusion.g0), channel_id=1, source_target_pairs={{0,256},{64,832},{128,384},{192,960},{256,512},{320,64},{384,640},... | collective-permute-start | bytes 909320 | tf_op jit(solution)/shard_map/ppermute | solution.py:36
  91.6 3.5 %collective-permute-done.9 = bf16[592,256]{1,0:T(8,128)(2,1)S(1)} collective-permute-done((bf16[592,256]{1,0:T(8,128)(2,1)S(1)}, bf16[592,256]{1,0:T(8,128)(2,1)S(1)}, u32[]{:S(2)}, u32[]{:S(2)}) %collective-permute-start.9) | collective-permute-done | bytes 303136 | tf_op jit(solution)/shard_map/ppermute | solution.py:36
  95.1 2.4 %collective-permute-start.11 = (bf16[592,256]{1,0:T(8,128)(2,1)S(1)}, bf16[592,256]{1,0:T(8,128)(2,1)S(1)}, u32[]{:S(2)}, u32[]{:S(2)}) collective-permute-start(bf16[592,256]{1,0:T(8,128)(2,1)S(1)} %collective-permute-done.9), channel_id=1, source_target_pairs={{0,256},{64,832},{128,384},{192,960},{256,512},{320,64},{384,640},... | collective-permute-start | bytes 909320 | tf_op jit(solution)/shard_map/ppermute | solution.py:36
  97.5 2.4 %collective-permute-done.10 = bf16[592,256]{1,0:T(8,128)(2,1)S(1)} collective-permute-done((bf16[592,256]{1,0:T(8,128)(2,1)S(1)}, bf16[592,256]{1,0:T(8,128)(2,1)S(1)}, u32[]{:S(2)}, u32[]{:S(2)}) %collective-permute-start.10) | collective-permute-done | bytes 303136 | tf_op jit(solution)/shard_map/ppermute | solution.py:36
  99.9 8.4 %collective-permute-start.12 = (bf16[592,128]{1,0:T(8,128)(2,1)S(1)}, bf16[592,128]{1,0:T(8,128)(2,1)S(1)}, u32[]{:S(2)}, u32[]{:S(2)}) collective-permute-start(bf16[592,128]{1,0:T(8,128)(2,1)S(1)} %slice_select_fusion), channel_id=1, source_target_pairs={{0,256},{64,832},{128,384},{192,960},{256,512},{320,64},{384,640},... | collective-permute-start | bytes 454664 | tf_op jit(solution)/shard_map/ppermute | solution.py:36
  108.3 1.1 collective-permute-done.11
  109.5 1.9 %collective-permute-start.13 = (bf16[2,592,256]{2,1,0:T(8,128)(2,1)S(1)}, bf16[2,592,256]{2,1,0:T(8,128)(2,1)S(1)}, u32[]{:S(2)}, u32[]{:S(2)}) collective-permute-start(bf16[2,592,256]{2,1,0:T(8,128)(2,1)S(1)} %pad_maximum_fusion.r12), channel_id=1, source_target_pairs={{0,64},{64,0},{128,192},{192,128},{256,320},{320,256},{384,448},{4... | collective-permute-start | bytes 1818632 | tf_op jit(solution)/shard_map/ppermute | solution.py:40
  111.4 1.1 collective-permute-done.12
  112.5 1.9 %collective-permute-start.14 = (bf16[592,384]{1,0:T(8,128)(2,1)S(1)}, bf16[592,384]{1,0:T(8,128)(2,1)S(1)}, u32[]{:S(2)}, u32[]{:S(2)}) collective-permute-start(bf16[592,384]{1,0:T(8,128)(2,1)S(1)} %constant_dynamic-update-slice_fusion.r34), channel_id=1, source_target_pairs={{0,64},{64,0},{128,192},{192,128},{256,320},{320,256},{384,448},{4... | collective-permute-start | bytes 1363976 | tf_op jit(solution)/shard_map/ppermute | solution.py:40
  114.5 1.8 %collective-permute-done.14.s34 = bf16[592,384]{1,0:T(8,128)(2,1)S(1)} collective-permute-done((bf16[592,384]{1,0:T(8,128)(2,1)S(1)}, bf16[592,384]{1,0:T(8,128)(2,1)S(1)}, u32[]{:S(2)}, u32[]{:S(2)}) %collective-permute-start.14) | collective-permute-done | bytes 454688 | tf_op jit(solution)/shard_map/ppermute | solution.py:40
  117.2 6.9 %down_grad.1 = (bf16[512,512]{1,0:T(8,128)(2,1)}, bf16[576,128]{1,0:T(8,128)(2,1)}) custom-call(s32[2]{0:T(128)} %pad_add_fusion.info, f32[8,128]{1,0:T(8,128)} %broadcast_in_dim.11.limits, bf16[592,256]{1,0:T(8,128)(2,1)} %copy-done.2, bf16[2,592,256]{2,1,0:T(8,128)(2,1)} %copy-done, bf16[592,384]{1,0:T(8,128)(2,1)} %copy-done.1, ...), custom_call_target="tpu_custom_call" | custom-call | tf_op jit(solution)/shard_map/down_grad/pallas_call | solution.py:207
  124.1 33.3 %all_to_all.5 = bf16[64,8,512]{2,1,0:T(8,128)(2,1)S(1)} all-to-all(bf16[64,8,512]{2,1,0:T(8,128)(2,1)} %bitcast.36), channel_id=1, replica_groups=mesh['ctx'=16,'grp'=64] {'grp'}, dimensions={0} | all-to-all | bytes 1048576 | tf_op jit(solution)/shard_map/all_to_all | solution.py:276
  (47 shorter events, 9.9 us)
Async XLA Ops:
  1.3 29.2 %copy-start.6 = (bf16[1,4,73728]{2,1,0:T(4,128)(2,1)S(1)}, bf16[1,4,73728]{2,1,0:T(4,128)(2,1)}, u32[]{:S(2)}) copy-start(bf16[1,4,73728]{2,1,0:T(4,128)(2,1)} %param.7) | copy-start | bytes 1769476
  2.3 26.5 %collective-permute-start.1 = (bf16[592,128]{1,0:T(8,128)(2,1)S(1)}, bf16[592,128]{1,0:T(8,128)(2,1)}, u32[]{:S(2)}, u32[]{:S(2)}) collective-permute-start(bf16[592,128]{1,0:T(8,128)(2,1)S(1)} %fusion.5), channel_id=1, source_target_pairs={{0,256},{64,320},{128,384},{192,448},{256,512},{320,576},{384,640}... | collective-permute-start | bytes 454664 | tf_op jit(solution)/shard_map/ppermute | solution.py:36
  10.2 21.2 %collective-permute-start = (bf16[592,128]{1,0:T(8,128)(2,1)S(1)}, bf16[592,128]{1,0:T(8,128)(2,1)S(1)}, u32[]{:S(2)}, u32[]{:S(2)}) collective-permute-start(bf16[592,128]{1,0:T(8,128)(2,1)S(1)} %fusion.5), channel_id=1, source_target_pairs={{0,128},{64,192},{128,256},{192,320},{256,384},{320,448},{384,512}... | collective-permute-start | bytes 454664 | tf_op jit(solution)/shard_map/ppermute | solution.py:36
  15.4 31.0 %collective-permute-start.3 = (bf16[592,128]{1,0:T(8,128)(2,1)S(1)}, bf16[592,128]{1,0:T(8,128)(2,1)S(1)}, u32[]{:S(2)}, u32[]{:S(2)}) collective-permute-start(bf16[592,128]{1,0:T(8,128)(2,1)S(1)} %fusion.5), channel_id=1, source_target_pairs={{0,512},{64,576},{128,640},{192,704},{256,768},{320,832},{384,896}... | collective-permute-start | bytes 454664 | tf_op jit(solution)/shard_map/ppermute | solution.py:36
  32.4 14.1 %copy-start.9 = (f32[1,8]{1,0:T(1,128)S(1)}, f32[1,8]{1,0:T(1,128)}, u32[]{:S(2)}) copy-start(f32[1,8]{1,0:T(1,128)} %param.11) | copy-start | bytes 100
  32.4 14.0 %collective-permute-start.2 = (bf16[592,128]{1,0:T(8,128)(2,1)S(1)}, bf16[592,128]{1,0:T(8,128)(2,1)S(1)}, u32[]{:S(2)}, u32[]{:S(2)}) collective-permute-start(bf16[592,128]{1,0:T(8,128)(2,1)S(1)} %collective-permute-done), channel_id=1, source_target_pairs={{0,256},{64,320},{128,384},{192,448},{256,512},{320,576},{384,640}... | collective-permute-start | bytes 454664 | tf_op jit(solution)/shard_map/ppermute | solution.py:36
  46.5 4.9 %copy-start.3 = (bf16[5,592,128]{2,1,0:T(8,128)(2,1)}, bf16[5,592,128]{2,1,0:T(8,128)(2,1)S(1)}, u32[]{:S(2)}) copy-start(bf16[5,592,128]{2,1,0:T(8,128)(2,1)S(1)} %bitcast_dynamic-update-slice_fusion.own) | copy-start | bytes 2273284
  47.3 4.1 %collective-permute-start.4 = (bf16[5,592,128]{2,1,0:T(8,128)(2,1)S(1)}, bf16[5,592,128]{2,1,0:T(8,128)(2,1)S(1)}, u32[]{:S(2)}, u32[]{:S(2)}) collective-permute-start(bf16[5,592,128]{2,1,0:T(8,128)(2,1)S(1)} %bitcast_dynamic-update-slice_fusion.own), channel_id=1, source_target_pairs={{0,64},{64,0},{128,192},{192,128},{256,320},{320,256},{384,448},{4... | collective-permute-start | bytes 2273288 | tf_op jit(solution)/shard_map/ppermute | solution.py:40
  51.4 0.9 copy-start.4
  60.9 20.5 %copy-start.8 = (bf16[592,256]{1,0:T(8,128)(2,1)S(1)}, bf16[592,256]{1,0:T(8,128)(2,1)}, u32[]{:S(2)}) copy-start(bf16[592,256]{1,0:T(8,128)(2,1)} %get-tuple-element.26) | copy-start | bytes 909316
  60.9 4.3 %collective-permute-start.5 = (bf16[2,592,256]{2,1,0:T(8,128)(2,1)}, bf16[2,592,256]{2,1,0:T(8,128)(2,1)S(1)}, u32[]{:S(2)}, u32[]{:S(2)}) collective-permute-start(bf16[2,592,256]{2,1,0:T(8,128)(2,1)} %get-tuple-element.28), channel_id=1, source_target_pairs={{0,64},{64,0},{128,192},{192,128},{256,320},{320,256},{384,448},{4... | collective-permute-start | bytes 1818632 | tf_op jit(solution)/shard_map/ppermute | solution.py:40
  66.4 12.9 %collective-permute-start.6 = (bf16[592,256]{1,0:T(8,128)(2,1)S(1)}, bf16[592,256]{1,0:T(8,128)(2,1)S(1)}, u32[]{:S(2)}, u32[]{:S(2)}) collective-permute-start(bf16[592,256]{1,0:T(8,128)(2,1)S(1)} %get-tuple-element.34), channel_id=1, source_target_pairs={{0,256},{64,832},{128,384},{192,960},{256,512},{320,64},{384,640},... | collective-permute-start | bytes 909320 | tf_op jit(solution)/shard_map/ppermute | solution.py:36
  68.3 13.1 %collective-permute-start.7 = (bf16[592,256]{1,0:T(8,128)(2,1)S(1)}, bf16[592,256]{1,0:T(8,128)(2,1)S(1)}, u32[]{:S(2)}, u32[]{:S(2)}) collective-permute-start(bf16[592,256]{1,0:T(8,128)(2,1)S(1)} %get-tuple-element.35), channel_id=1, source_target_pairs={{0,128},{64,960},{128,256},{192,64},{256,384},{320,192},{384,512},... | collective-permute-start | bytes 909320 | tf_op jit(solution)/shard_map/ppermute | solution.py:36
  81.5 3.5 %collective-permute-start.8 = (bf16[592,256]{1,0:T(8,128)(2,1)S(1)}, bf16[592,256]{1,0:T(8,128)(2,1)S(1)}, u32[]{:S(2)}, u32[]{:S(2)}) collective-permute-start(bf16[592,256]{1,0:T(8,128)(2,1)S(1)} %add_convert_fusion.1), channel_id=1, source_target_pairs={{0,64},{64,0},{128,192},{192,128},{256,320},{320,256},{384,448},{4... | collective-permute-start | bytes 909320 | tf_op jit(solution)/shard_map/ppermute | solution.py:40
  85.1 31.1 %copy-start.2 = (bf16[592,256]{1,0:T(8,128)(2,1)}, bf16[592,256]{1,0:T(8,128)(2,1)S(1)}, u32[]{:S(2)}) copy-start(bf16[592,256]{1,0:T(8,128)(2,1)S(1)} %add_convert_fusion.g0) | copy-start | bytes 909316
  85.1 9.9 %collective-permute-start.9 = (bf16[592,256]{1,0:T(8,128)(2,1)S(1)}, bf16[592,256]{1,0:T(8,128)(2,1)S(1)}, u32[]{:S(2)}, u32[]{:S(2)}) collective-permute-start(bf16[592,256]{1,0:T(8,128)(2,1)S(1)} %add_convert_fusion.g0), channel_id=1, source_target_pairs={{0,128},{64,960},{128,256},{192,64},{256,384},{320,192},{384,512},... | collective-permute-start | bytes 909320 | tf_op jit(solution)/shard_map/ppermute | solution.py:36
  87.1 12.8 %collective-permute-start.10 = (bf16[592,256]{1,0:T(8,128)(2,1)S(1)}, bf16[592,256]{1,0:T(8,128)(2,1)S(1)}, u32[]{:S(2)}, u32[]{:S(2)}) collective-permute-start(bf16[592,256]{1,0:T(8,128)(2,1)S(1)} %add_convert_fusion.g0), channel_id=1, source_target_pairs={{0,256},{64,832},{128,384},{192,960},{256,512},{320,64},{384,640},... | collective-permute-start | bytes 909320 | tf_op jit(solution)/shard_map/ppermute | solution.py:36
  95.1 14.3 %collective-permute-start.11 = (bf16[592,256]{1,0:T(8,128)(2,1)S(1)}, bf16[592,256]{1,0:T(8,128)(2,1)S(1)}, u32[]{:S(2)}, u32[]{:S(2)}) collective-permute-start(bf16[592,256]{1,0:T(8,128)(2,1)S(1)} %collective-permute-done.9), channel_id=1, source_target_pairs={{0,256},{64,832},{128,384},{192,960},{256,512},{320,64},{384,640},... | collective-permute-start | bytes 909320 | tf_op jit(solution)/shard_map/ppermute | solution.py:36
  99.9 12.6 %collective-permute-start.12 = (bf16[592,128]{1,0:T(8,128)(2,1)S(1)}, bf16[592,128]{1,0:T(8,128)(2,1)S(1)}, u32[]{:S(2)}, u32[]{:S(2)}) collective-permute-start(bf16[592,128]{1,0:T(8,128)(2,1)S(1)} %slice_select_fusion), channel_id=1, source_target_pairs={{0,256},{64,832},{128,384},{192,960},{256,512},{320,64},{384,640},... | collective-permute-start | bytes 454664 | tf_op jit(solution)/shard_map/ppermute | solution.py:36
  109.5 6.8 %copy-start = (bf16[2,592,256]{2,1,0:T(8,128)(2,1)}, bf16[2,592,256]{2,1,0:T(8,128)(2,1)S(1)}, u32[]{:S(2)}) copy-start(bf16[2,592,256]{2,1,0:T(8,128)(2,1)S(1)} %pad_maximum_fusion.r12) | copy-start | bytes 1818628
  109.5 6.8 %collective-permute-start.13 = (bf16[2,592,256]{2,1,0:T(8,128)(2,1)S(1)}, bf16[2,592,256]{2,1,0:T(8,128)(2,1)S(1)}, u32[]{:S(2)}, u32[]{:S(2)}) collective-permute-start(bf16[2,592,256]{2,1,0:T(8,128)(2,1)S(1)} %pad_maximum_fusion.r12), channel_id=1, source_target_pairs={{0,64},{64,0},{128,192},{192,128},{256,320},{320,256},{384,448},{4... | collective-permute-start | bytes 1818632 | tf_op jit(solution)/shard_map/ppermute | solution.py:40
  112.5 3.7 %copy-start.1 = (bf16[592,384]{1,0:T(8,128)(2,1)}, bf16[592,384]{1,0:T(8,128)(2,1)S(1)}, u32[]{:S(2)}) copy-start(bf16[592,384]{1,0:T(8,128)(2,1)S(1)} %constant_dynamic-update-slice_fusion.r34) | copy-start | bytes 1363972
  112.5 3.7 %collective-permute-start.14 = (bf16[592,384]{1,0:T(8,128)(2,1)S(1)}, bf16[592,384]{1,0:T(8,128)(2,1)S(1)}, u32[]{:S(2)}, u32[]{:S(2)}) collective-permute-start(bf16[592,384]{1,0:T(8,128)(2,1)S(1)} %constant_dynamic-update-slice_fusion.r34), channel_id=1, source_target_pairs={{0,64},{64,0},{128,192},{192,128},{256,320},{320,256},{384,448},{4... | collective-permute-start | bytes 1363976 | tf_op jit(solution)/shard_map/ppermute | solution.py:40
  116.2 0.8 copy-start.7
  116.2 1.0 copy-start.5

commit v3 on v2

--- a/solution.py
+++ b/solution.py
@@ -24,7 +24,7 @@
 
 score_scale = 192.0 ** (-0.5)
 norm_eps = 1e-06
-VMEM_BYTES = 56 * 1024 * 1024
+MIB = 1024 * 1024
 
 
 def chip_shift(value, by0, by1):
@@ -129,7 +129,7 @@
             pltpu.VMEM((BACK, QH, PAIR), jnp.float32),
             pltpu.VMEM((BACK, 2 * QH, PAIR), jnp.bfloat16),
         ],
-        compiler_params=pltpu.CompilerParams(vmem_limit_bytes=VMEM_BYTES),
+        compiler_params=pltpu.CompilerParams(vmem_limit_bytes=24 * MIB),
         name="attention_grads",
     )(info, own, par, rows, cols)
 
@@ -165,7 +165,10 @@
         members.append(member)
         squares = squares + jnp.where(member, jnp.sum(x * x, axis=0, keepdims=True), 0.0)
     norms = jnp.sum(squares, axis=1, keepdims=True)
-    factor = jnp.minimum(1.0, limits[:, 0:1] / jnp.sqrt(norms + norm_eps))
+    row = lax.broadcasted_iota(jnp.int32, (NDOC, NDOC), 0)
+    col = lax.broadcasted_iota(jnp.int32, (NDOC, NDOC), 1)
+    limit = jnp.sum(jnp.where(row == col, limits[...], 0.0), axis=1, keepdims=True)
+    factor = jnp.minimum(1.0, limit / jnp.sqrt(norms + norm_eps))
     for (ref, by), member in zip(blocks, members, strict=True):
         gain = jnp.sum(jnp.where(member, factor, 0.0), axis=0, keepdims=True)
         shard = lax.rem(chip + by + 2 * CHIPS - 2, CHIPS)
@@ -217,7 +220,7 @@
             pltpu.VMEM((KW, CHIPS * PAIR), jnp.bfloat16),
             pltpu.VMEM((KW, SLOT), jnp.bfloat16),
         ],
-        compiler_params=pltpu.CompilerParams(vmem_limit_bytes=VMEM_BYTES),
+        compiler_params=pltpu.CompilerParams(vmem_limit_bytes=20 * MIB),
         name="down_grad",
     )(info, limits, *blocks, hidden)
 
@@ -243,9 +246,8 @@
     grad_rows = grad_rows[0].reshape(QH, LATENT)
     rows = jnp.concatenate([query_rows, jnp.pad(grad_rows, ((0, 0), (0, KW - LATENT)))], axis=0)
     cols = rows.T
-    limits = jnp.broadcast_to(clip_limits[0][:, None], (NDOC, 128))
     own = jnp.stack([keys, near, next_near, chip_shift(near, 2, 2), fourth])
-    own, rows, cols, info, limits = lax.optimization_barrier((own, rows, cols, info, limits))
+    own, rows, cols, info = lax.optimization_barrier((own, rows, cols, info))
     par = core_swap(own)
     keep, send, mid = attention(info, own, par, rows, cols)
 
@@ -265,7 +267,7 @@
     nearer_par = core_swap(nearer)
     farther = jnp.concatenate([three, four], axis=1)
     blocks = [total, nearer, farther, nearer_par, core_swap(farther)]
-    chunks, own_grad = down_grad(info, limits, blocks, hidden[0].T)
+    chunks, own_grad = down_grad(info, clip_limits, blocks, hidden[0].T)
     return own_grad, chunks
 
 

time: 159 us -> 151 us (0.950)
  Pallas kernels: 15.6 us -> 11.2 us
  local copies, waits for them, and re-layouts: 7.89 us -> 5.52 us
  other arithmetic: 6.71 us -> 5.06 us
    pallas_call x1, Pallas kernels: 6.89 us -> 4.3 us  [down_grad(): pl.pallas_call(down_kernel, out_shape=(jax.ShapeDtypeStruct((SLOT, SLOT),...]
    unnamed x24 -> x10, local copies, waits for them, and re-layouts: 2.87 us -> 1.01 us
    pallas_call x1, Pallas kernels: 8.67 us -> 6.86 us  [attention(): pl.pallas_call(attention_kernel, out_shape=(block, block, jax.ShapeDtypeS...]
where the time goes in v3:
time: 151 us; the launch traced here: 150 us
  starting transfers between devices  57.4 us (38%)
  waiting for transfers between devices  37 us (25%)
  blocking collectives  33 us (22%)
  Pallas kernels  11.2 us (7%)
  local copies, waits for them, and re-layouts  5.52 us (4%)
  other arithmetic  5.06 us (3%)
    ppermute x10, starting transfers between devices, chip_shift(): return lax.ppermute(value, 'ctx', pairs)  47.7 us
    all_to_all x1, blocking collectives, on_device(): chunks = lax.all_to_all(chunks, 'grp', 0, 0, tiled=True)  33 us
    ppermute x10, waiting for transfers between devices, chip_shift(): return lax.ppermute(value, 'ctx', pairs)  31.1 us
    ppermute x5, starting transfers between devices, core_swap(): return lax.ppermute(value, 'ctx', [(i, i ^ 1) for i in range(2 * CHIPS)])  9.72 us
    pallas_call x1, Pallas kernels, attention(): pl.pallas_call(attention_kernel, out_shape=(block, block, jax.ShapeDtypeS...  6.86 us
    ppermute x5, waiting for transfers between devices, core_swap(): return lax.ppermute(value, 'ctx', [(i, i ^ 1) for i in range(2 * CHIPS)])  5.85 us
    pallas_call x1, Pallas kernels, down_grad(): pl.pallas_call(down_kernel, out_shape=(jax.ShapeDtypeStruct((SLOT, SLOT),...  4.3 us
  transfers between devices with their start and end apart: 15, of which 11 were waited for; matrix products, arithmetic and copies ran while one was open for 5% of the time, Pallas kernels for 0%

profile of v3, /device:TPU:4, one launch (start us, length us, event | category | flops | bytes accessed | tf_op | source)
XLA Modules:
  0.0 150.1 jit_solution(7872427291751874761)
XLA Ops:
  1.3 1.0 fusion.5
  2.3 7.9 %collective-permute-start.1 = (bf16[592,128]{1,0:T(8,128)(2,1)S(1)}, bf16[592,128]{1,0:T(8,128)(2,1)}, u32[]{:S(2)}, u32[]{:S(2)}) collective-permute-start(bf16[592,128]{1,0:T(8,128)(2,1)S(1)} %fusion.5), channel_id=1, source_target_pairs={{0,256},{64,320},{128,384},{192,448},{256,512},{320,576},{384,640}... | collective-permute-start | bytes 454664 | tf_op jit(solution)/shard_map/ppermute | solution.py:36
  10.2 5.2 %collective-permute-start = (bf16[592,128]{1,0:T(8,128)(2,1)S(1)}, bf16[592,128]{1,0:T(8,128)(2,1)S(1)}, u32[]{:S(2)}, u32[]{:S(2)}) collective-permute-start(bf16[592,128]{1,0:T(8,128)(2,1)S(1)} %fusion.5), channel_id=1, source_target_pairs={{0,128},{64,192},{128,256},{192,320},{256,384},{320,448},{384,512}... | collective-permute-start | bytes 454664 | tf_op jit(solution)/shard_map/ppermute | solution.py:36
  15.4 11.9 %collective-permute-start.3 = (bf16[592,128]{1,0:T(8,128)(2,1)S(1)}, bf16[592,128]{1,0:T(8,128)(2,1)S(1)}, u32[]{:S(2)}, u32[]{:S(2)}) collective-permute-start(bf16[592,128]{1,0:T(8,128)(2,1)S(1)} %fusion.5), channel_id=1, source_target_pairs={{0,512},{64,576},{128,640},{192,704},{256,768},{320,832},{384,896}... | collective-permute-start | bytes 454664 | tf_op jit(solution)/shard_map/ppermute | solution.py:36
  28.3 1.5 reshape_squeeze.7
  31.9 1.9 %collective-permute-start.2 = (bf16[592,128]{1,0:T(8,128)(2,1)S(1)}, bf16[592,128]{1,0:T(8,128)(2,1)S(1)}, u32[]{:S(2)}, u32[]{:S(2)}) collective-permute-start(bf16[592,128]{1,0:T(8,128)(2,1)S(1)} %collective-permute-done), channel_id=1, source_target_pairs={{0,256},{64,320},{128,384},{192,448},{256,512},{320,576},{384,640}... | collective-permute-start | bytes 454664 | tf_op jit(solution)/shard_map/ppermute | solution.py:36
  33.8 1.2 fusion.6
  35.0 11.5 %collective-permute-done.2 = bf16[592,128]{1,0:T(8,128)(2,1)S(1)} collective-permute-done((bf16[592,128]{1,0:T(8,128)(2,1)S(1)}, bf16[592,128]{1,0:T(8,128)(2,1)S(1)}, u32[]{:S(2)}, u32[]{:S(2)}) %collective-permute-start.2) | collective-permute-done | bytes 151584 | tf_op jit(solution)/shard_map/ppermute | solution.py:36
  46.6 1.9 %collective-permute-start.4 = (bf16[5,592,128]{2,1,0:T(8,128)(2,1)S(1)}, bf16[5,592,128]{2,1,0:T(8,128)(2,1)}, u32[]{:S(2)}, u32[]{:S(2)}) collective-permute-start(bf16[5,592,128]{2,1,0:T(8,128)(2,1)S(1)} %bitcast_dynamic-update-slice_fusion.own), channel_id=1, source_target_pairs={{0,64},{64,0},{128,192},{192,128},{256,320},{320,256},{384,448},{4... | collective-permute-start | bytes 2273288 | tf_op jit(solution)/shard_map/ppermute | solution.py:40
  48.5 1.7 %copy.11.rows_ref = bf16[1024,576]{1,0:T(8,128)(2,1)S(1)} copy(bf16[1024,576]{0,1:T(8,128)(2,1)} %get-tuple-element.22) | data formatting | bytes 2359296 | tf_op jit(solution)/shard_map/optimization_barrier | solution.py:250
  50.8 6.9 %attention_grads.1 = (bf16[2,592,256]{2,1,0:T(8,128)(2,1)S(1)}, bf16[2,592,256]{2,1,0:T(8,128)(2,1)S(1)}, bf16[592,256]{1,0:T(8,128)(2,1)S(1)}) custom-call(s32[2]{0:T(128)S(1)} %pad_add_fusion.info, bf16[5,592,128]{2,1,0:T(8,128)(2,1)S(1)} %bitcast_dynamic-update-slice_fusion.own, bf16[5,592,128]{2,1,0:T(8,128)(2,1)} %collective-permute-done.4.par, ...), custom_call_target="tpu_custom_call" | custom-call | tf_op jit(solution)/shard_map/attention_grads/pallas_call | solution.py:121
  57.7 2.0 %collective-permute-start.5 = (bf16[2,592,256]{2,1,0:T(8,128)(2,1)S(1)}, bf16[2,592,256]{2,1,0:T(8,128)(2,1)S(1)}, u32[]{:S(2)}, u32[]{:S(2)}) collective-permute-start(bf16[2,592,256]{2,1,0:T(8,128)(2,1)S(1)} %get-tuple-element.26), channel_id=1, source_target_pairs={{0,64},{64,0},{128,192},{192,128},{256,320},{320,256},{384,448},{4... | collective-permute-start | bytes 1818632 | tf_op jit(solution)/shard_map/ppermute | solution.py:40
  59.8 1.9 %collective-permute-done.5 = bf16[2,592,256]{2,1,0:T(8,128)(2,1)S(1)} collective-permute-done((bf16[2,592,256]{2,1,0:T(8,128)(2,1)S(1)}, bf16[2,592,256]{2,1,0:T(8,128)(2,1)S(1)}, u32[]{:S(2)}, u32[]{:S(2)}) %collective-permute-start.5) | collective-permute-done | bytes 606240 | tf_op jit(solution)/shard_map/ppermute | solution.py:40
  61.8 1.9 %collective-permute-start.6 = (bf16[592,256]{1,0:T(8,128)(2,1)S(1)}, bf16[592,256]{1,0:T(8,128)(2,1)S(1)}, u32[]{:S(2)}, u32[]{:S(2)}) collective-permute-start(bf16[592,256]{1,0:T(8,128)(2,1)S(1)} %get-tuple-element.32), channel_id=1, source_target_pairs={{0,256},{64,832},{128,384},{192,960},{256,512},{320,64},{384,640},... | collective-permute-start | bytes 909320 | tf_op jit(solution)/shard_map/ppermute | solution.py:36
  63.7 2.1 %collective-permute-start.7 = (bf16[592,256]{1,0:T(8,128)(2,1)S(1)}, bf16[592,256]{1,0:T(8,128)(2,1)S(1)}, u32[]{:S(2)}, u32[]{:S(2)}) collective-permute-start(bf16[592,256]{1,0:T(8,128)(2,1)S(1)} %get-tuple-element.33), channel_id=1, source_target_pairs={{0,128},{64,960},{128,256},{192,64},{256,384},{320,192},{384,512},... | collective-permute-start | bytes 909320 | tf_op jit(solution)/shard_map/ppermute | solution.py:36
  65.8 8.8 %collective-permute-done.6 = bf16[592,256]{1,0:T(8,128)(2,1)S(1)} collective-permute-done((bf16[592,256]{1,0:T(8,128)(2,1)S(1)}, bf16[592,256]{1,0:T(8,128)(2,1)S(1)}, u32[]{:S(2)}, u32[]{:S(2)}) %collective-permute-start.6) | collective-permute-done | bytes 303136 | tf_op jit(solution)/shard_map/ppermute | solution.py:36
  74.6 2.2 %collective-permute-done.7 = bf16[592,256]{1,0:T(8,128)(2,1)S(1)} collective-permute-done((bf16[592,256]{1,0:T(8,128)(2,1)S(1)}, bf16[592,256]{1,0:T(8,128)(2,1)S(1)}, u32[]{:S(2)}, u32[]{:S(2)}) %collective-permute-start.7) | collective-permute-done | bytes 303136 | tf_op jit(solution)/shard_map/ppermute | solution.py:36
  76.9 1.9 %collective-permute-start.8 = (bf16[592,256]{1,0:T(8,128)(2,1)S(1)}, bf16[592,256]{1,0:T(8,128)(2,1)S(1)}, u32[]{:S(2)}, u32[]{:S(2)}) collective-permute-start(bf16[592,256]{1,0:T(8,128)(2,1)S(1)} %add_convert_fusion.1), channel_id=1, source_target_pairs={{0,64},{64,0},{128,192},{192,128},{256,320},{320,256},{384,448},{4... | collective-permute-start | bytes 909320 | tf_op jit(solution)/shard_map/ppermute | solution.py:40
  78.9 1.6 %collective-permute-done.8 = bf16[592,256]{1,0:T(8,128)(2,1)S(1)} collective-permute-done((bf16[592,256]{1,0:T(8,128)(2,1)S(1)}, bf16[592,256]{1,0:T(8,128)(2,1)S(1)}, u32[]{:S(2)}, u32[]{:S(2)}) %collective-permute-start.8) | collective-permute-done | bytes 303136 | tf_op jit(solution)/shard_map/ppermute | solution.py:40
  80.5 2.1 %collective-permute-start.9 = (bf16[592,256]{1,0:T(8,128)(2,1)S(1)}, bf16[592,256]{1,0:T(8,128)(2,1)S(1)}, u32[]{:S(2)}, u32[]{:S(2)}) collective-permute-start(bf16[592,256]{1,0:T(8,128)(2,1)S(1)} %add_convert_fusion.g0), channel_id=1, source_target_pairs={{0,128},{64,960},{128,256},{192,64},{256,384},{320,192},{384,512},... | collective-permute-start | bytes 909320 | tf_op jit(solution)/shard_map/ppermute | solution.py:36
  82.6 4.4 %collective-permute-start.10 = (bf16[592,256]{1,0:T(8,128)(2,1)S(1)}, bf16[592,256]{1,0:T(8,128)(2,1)S(1)}, u32[]{:S(2)}, u32[]{:S(2)}) collective-permute-start(bf16[592,256]{1,0:T(8,128)(2,1)S(1)} %add_convert_fusion.g0), channel_id=1, source_target_pairs={{0,256},{64,832},{128,384},{192,960},{256,512},{320,64},{384,640},... | collective-permute-start | bytes 909320 | tf_op jit(solution)/shard_map/ppermute | solution.py:36
  87.0 5.0 %collective-permute-done.9 = bf16[592,256]{1,0:T(8,128)(2,1)S(1)} collective-permute-done((bf16[592,256]{1,0:T(8,128)(2,1)S(1)}, bf16[592,256]{1,0:T(8,128)(2,1)S(1)}, u32[]{:S(2)}, u32[]{:S(2)}) %collective-permute-start.9) | collective-permute-done | bytes 303136 | tf_op jit(solution)/shard_map/ppermute | solution.py:36
  92.0 1.9 %collective-permute-start.11 = (bf16[592,256]{1,0:T(8,128)(2,1)S(1)}, bf16[592,256]{1,0:T(8,128)(2,1)S(1)}, u32[]{:S(2)}, u32[]{:S(2)}) collective-permute-start(bf16[592,256]{1,0:T(8,128)(2,1)S(1)} %collective-permute-done.9), channel_id=1, source_target_pairs={{0,256},{64,832},{128,384},{192,960},{256,512},{320,64},{384,640},... | collective-permute-start | bytes 909320 | tf_op jit(solution)/shard_map/ppermute | solution.py:36
  93.9 1.4 collective-permute-done.10
  95.3 8.4 %collective-permute-start.12 = (bf16[592,128]{1,0:T(8,128)(2,1)S(1)}, bf16[592,128]{1,0:T(8,128)(2,1)S(1)}, u32[]{:S(2)}, u32[]{:S(2)}) collective-permute-start(bf16[592,128]{1,0:T(8,128)(2,1)S(1)} %slice_select_fusion), channel_id=1, source_target_pairs={{0,256},{64,832},{128,384},{192,960},{256,512},{320,64},{384,640},... | collective-permute-start | bytes 454664 | tf_op jit(solution)/shard_map/ppermute | solution.py:36
  103.8 1.1 collective-permute-done.11
  104.9 1.9 %collective-permute-start.13 = (bf16[2,592,256]{2,1,0:T(8,128)(2,1)S(1)}, bf16[2,592,256]{2,1,0:T(8,128)(2,1)S(1)}, u32[]{:S(2)}, u32[]{:S(2)}) collective-permute-start(bf16[2,592,256]{2,1,0:T(8,128)(2,1)S(1)} %pad_maximum_fusion.r12), channel_id=1, source_target_pairs={{0,64},{64,0},{128,192},{192,128},{256,320},{320,256},{384,448},{4... | collective-permute-start | bytes 1818632 | tf_op jit(solution)/shard_map/ppermute | solution.py:40
  106.9 1.2 collective-permute-done.12
  108.2 1.9 %collective-permute-start.14 = (bf16[592,384]{1,0:T(8,128)(2,1)S(1)}, bf16[592,384]{1,0:T(8,128)(2,1)S(1)}, u32[]{:S(2)}, u32[]{:S(2)}) collective-permute-start(bf16[592,384]{1,0:T(8,128)(2,1)S(1)} %constant_dynamic-update-slice_fusion.r34), channel_id=1, source_target_pairs={{0,64},{64,0},{128,192},{192,128},{256,320},{320,256},{384,448},{4... | collective-permute-start | bytes 1363976 | tf_op jit(solution)/shard_map/ppermute | solution.py:40
  110.1 1.8 %collective-permute-done.14.s34 = bf16[592,384]{1,0:T(8,128)(2,1)S(1)} collective-permute-done((bf16[592,384]{1,0:T(8,128)(2,1)S(1)}, bf16[592,384]{1,0:T(8,128)(2,1)S(1)}, u32[]{:S(2)}, u32[]{:S(2)}) %collective-permute-start.14) | collective-permute-done | bytes 454688 | tf_op jit(solution)/shard_map/ppermute | solution.py:40
  111.9 4.3 %down_grad.1 = (bf16[512,512]{1,0:T(8,128)(2,1)S(1)}, bf16[576,128]{1,0:T(8,128)(2,1)}) custom-call(s32[2]{0:T(128)S(1)} %pad_add_fusion.info, f32[1,8]{1,0:T(1,128)S(1)} %copy-done.1, bf16[592,256]{1,0:T(8,128)(2,1)S(1)} %add_convert_fusion.g0, bf16[2,592,256]{2,1,0:T(8,128)(2,1)S(1)} %pad_maximum_fusion.r12, ...), custom_call_target="tpu_custom_call" | custom-call | tf_op jit(solution)/shard_map/down_grad/pallas_call | solution.py:210
  116.2 33.0 %all_to_all.5 = bf16[64,8,512]{2,1,0:T(8,128)(2,1)S(1)} all-to-all(bf16[64,8,512]{2,1,0:T(8,128)(2,1)S(1)} %bitcast.32), channel_id=1, replica_groups=mesh['ctx'=16,'grp'=64] {'grp'}, dimensions={0} | all-to-all | bytes 1048576 | tf_op jit(solution)/shard_map/all_to_all | solution.py:278
  (32 shorter events, 5.9 us)
Async XLA Ops:
  1.3 28.7 %copy-start.2 = (bf16[1,4,73728]{2,1,0:T(4,128)(2,1)S(1)}, bf16[1,4,73728]{2,1,0:T(4,128)(2,1)}, u32[]{:S(2)}) copy-start(bf16[1,4,73728]{2,1,0:T(4,128)(2,1)} %param.7) | copy-start | bytes 1769476
  2.3 26.0 %collective-permute-start.1 = (bf16[592,128]{1,0:T(8,128)(2,1)S(1)}, bf16[592,128]{1,0:T(8,128)(2,1)}, u32[]{:S(2)}, u32[]{:S(2)}) collective-permute-start(bf16[592,128]{1,0:T(8,128)(2,1)S(1)} %fusion.5), channel_id=1, source_target_pairs={{0,256},{64,320},{128,384},{192,448},{256,512},{320,576},{384,640}... | collective-permute-start | bytes 454664 | tf_op jit(solution)/shard_map/ppermute | solution.py:36
  10.2 20.7 %collective-permute-start = (bf16[592,128]{1,0:T(8,128)(2,1)S(1)}, bf16[592,128]{1,0:T(8,128)(2,1)S(1)}, u32[]{:S(2)}, u32[]{:S(2)}) collective-permute-start(bf16[592,128]{1,0:T(8,128)(2,1)S(1)} %fusion.5), channel_id=1, source_target_pairs={{0,128},{64,192},{128,256},{192,320},{256,384},{320,448},{384,512}... | collective-permute-start | bytes 454664 | tf_op jit(solution)/shard_map/ppermute | solution.py:36
  15.4 31.1 %collective-permute-start.3 = (bf16[592,128]{1,0:T(8,128)(2,1)S(1)}, bf16[592,128]{1,0:T(8,128)(2,1)S(1)}, u32[]{:S(2)}, u32[]{:S(2)}) collective-permute-start(bf16[592,128]{1,0:T(8,128)(2,1)S(1)} %fusion.5), channel_id=1, source_target_pairs={{0,512},{64,576},{128,640},{192,704},{256,768},{320,832},{384,896}... | collective-permute-start | bytes 454664 | tf_op jit(solution)/shard_map/ppermute | solution.py:36
  31.9 14.6 %collective-permute-start.2 = (bf16[592,128]{1,0:T(8,128)(2,1)S(1)}, bf16[592,128]{1,0:T(8,128)(2,1)S(1)}, u32[]{:S(2)}, u32[]{:S(2)}) collective-permute-start(bf16[592,128]{1,0:T(8,128)(2,1)S(1)} %collective-permute-done), channel_id=1, source_target_pairs={{0,256},{64,320},{128,384},{192,448},{256,512},{320,576},{384,640}... | collective-permute-start | bytes 454664 | tf_op jit(solution)/shard_map/ppermute | solution.py:36
  46.6 4.3 %collective-permute-start.4 = (bf16[5,592,128]{2,1,0:T(8,128)(2,1)S(1)}, bf16[5,592,128]{2,1,0:T(8,128)(2,1)}, u32[]{:S(2)}, u32[]{:S(2)}) collective-permute-start(bf16[5,592,128]{2,1,0:T(8,128)(2,1)S(1)} %bitcast_dynamic-update-slice_fusion.own), channel_id=1, source_target_pairs={{0,64},{64,0},{128,192},{192,128},{256,320},{320,256},{384,448},{4... | collective-permute-start | bytes 2273288 | tf_op jit(solution)/shard_map/ppermute | solution.py:40
  57.7 3.9 %collective-permute-start.5 = (bf16[2,592,256]{2,1,0:T(8,128)(2,1)S(1)}, bf16[2,592,256]{2,1,0:T(8,128)(2,1)S(1)}, u32[]{:S(2)}, u32[]{:S(2)}) collective-permute-start(bf16[2,592,256]{2,1,0:T(8,128)(2,1)S(1)} %get-tuple-element.26), channel_id=1, source_target_pairs={{0,64},{64,0},{128,192},{192,128},{256,320},{320,256},{384,448},{4... | collective-permute-start | bytes 1818632 | tf_op jit(solution)/shard_map/ppermute | solution.py:40
  61.8 12.8 %collective-permute-start.6 = (bf16[592,256]{1,0:T(8,128)(2,1)S(1)}, bf16[592,256]{1,0:T(8,128)(2,1)S(1)}, u32[]{:S(2)}, u32[]{:S(2)}) collective-permute-start(bf16[592,256]{1,0:T(8,128)(2,1)S(1)} %get-tuple-element.32), channel_id=1, source_target_pairs={{0,256},{64,832},{128,384},{192,960},{256,512},{320,64},{384,640},... | collective-permute-start | bytes 909320 | tf_op jit(solution)/shard_map/ppermute | solution.py:36
  63.7 13.1 %collective-permute-start.7 = (bf16[592,256]{1,0:T(8,128)(2,1)S(1)}, bf16[592,256]{1,0:T(8,128)(2,1)S(1)}, u32[]{:S(2)}, u32[]{:S(2)}) collective-permute-start(bf16[592,256]{1,0:T(8,128)(2,1)S(1)} %get-tuple-element.33), channel_id=1, source_target_pairs={{0,128},{64,960},{128,256},{192,64},{256,384},{320,192},{384,512},... | collective-permute-start | bytes 909320 | tf_op jit(solution)/shard_map/ppermute | solution.py:36
  76.9 3.5 %collective-permute-start.8 = (bf16[592,256]{1,0:T(8,128)(2,1)S(1)}, bf16[592,256]{1,0:T(8,128)(2,1)S(1)}, u32[]{:S(2)}, u32[]{:S(2)}) collective-permute-start(bf16[592,256]{1,0:T(8,128)(2,1)S(1)} %add_convert_fusion.1), channel_id=1, source_target_pairs={{0,64},{64,0},{128,192},{192,128},{256,320},{320,256},{384,448},{4... | collective-permute-start | bytes 909320 | tf_op jit(solution)/shard_map/ppermute | solution.py:40
  80.5 31.3 %copy-start = (bf16[1,2048,448]{1,2,0:T(8,128)(2,1)S(1)}, bf16[1,2048,448]{1,2,0:T(8,128)(2,1)}, u32[]{:S(2)}) copy-start(bf16[1,2048,448]{1,2,0:T(8,128)(2,1)} %param.9) | copy-start | bytes 5505028
  80.5 31.3 %copy-start.1 = (f32[1,8]{1,0:T(1,128)S(1)}, f32[1,8]{1,0:T(1,128)}, u32[]{:S(2)}) copy-start(f32[1,8]{1,0:T(1,128)} %limits.1) | copy-start | bytes 100
  80.5 11.5 %collective-permute-start.9 = (bf16[592,256]{1,0:T(8,128)(2,1)S(1)}, bf16[592,256]{1,0:T(8,128)(2,1)S(1)}, u32[]{:S(2)}, u32[]{:S(2)}) collective-permute-start(bf16[592,256]{1,0:T(8,128)(2,1)S(1)} %add_convert_fusion.g0), channel_id=1, source_target_pairs={{0,128},{64,960},{128,256},{192,64},{256,384},{320,192},{384,512},... | collective-permute-start | bytes 909320 | tf_op jit(solution)/shard_map/ppermute | solution.py:36
  82.6 12.7 %collective-permute-start.10 = (bf16[592,256]{1,0:T(8,128)(2,1)S(1)}, bf16[592,256]{1,0:T(8,128)(2,1)S(1)}, u32[]{:S(2)}, u32[]{:S(2)}) collective-permute-start(bf16[592,256]{1,0:T(8,128)(2,1)S(1)} %add_convert_fusion.g0), channel_id=1, source_target_pairs={{0,256},{64,832},{128,384},{192,960},{256,512},{320,64},{384,640},... | collective-permute-start | bytes 909320 | tf_op jit(solution)/shard_map/ppermute | solution.py:36
  92.0 12.9 %collective-permute-start.11 = (bf16[592,256]{1,0:T(8,128)(2,1)S(1)}, bf16[592,256]{1,0:T(8,128)(2,1)S(1)}, u32[]{:S(2)}, u32[]{:S(2)}) collective-permute-start(bf16[592,256]{1,0:T(8,128)(2,1)S(1)} %collective-permute-done.9), channel_id=1, source_target_pairs={{0,256},{64,832},{128,384},{192,960},{256,512},{320,64},{384,640},... | collective-permute-start | bytes 909320 | tf_op jit(solution)/shard_map/ppermute | solution.py:36
  95.3 12.8 %collective-permute-start.12 = (bf16[592,128]{1,0:T(8,128)(2,1)S(1)}, bf16[592,128]{1,0:T(8,128)(2,1)S(1)}, u32[]{:S(2)}, u32[]{:S(2)}) collective-permute-start(bf16[592,128]{1,0:T(8,128)(2,1)S(1)} %slice_select_fusion), channel_id=1, source_target_pairs={{0,256},{64,832},{128,384},{192,960},{256,512},{320,64},{384,640},... | collective-permute-start | bytes 454664 | tf_op jit(solution)/shard_map/ppermute | solution.py:36
  104.9 6.9 %collective-permute-start.13 = (bf16[2,592,256]{2,1,0:T(8,128)(2,1)S(1)}, bf16[2,592,256]{2,1,0:T(8,128)(2,1)S(1)}, u32[]{:S(2)}, u32[]{:S(2)}) collective-permute-start(bf16[2,592,256]{2,1,0:T(8,128)(2,1)S(1)} %pad_maximum_fusion.r12), channel_id=1, source_target_pairs={{0,64},{64,0},{128,192},{192,128},{256,320},{320,256},{384,448},{4... | collective-permute-start | bytes 1818632 | tf_op jit(solution)/shard_map/ppermute | solution.py:40
  108.2 3.7 %collective-permute-start.14 = (bf16[592,384]{1,0:T(8,128)(2,1)S(1)}, bf16[592,384]{1,0:T(8,128)(2,1)S(1)}, u32[]{:S(2)}, u32[]{:S(2)}) collective-permute-start(bf16[592,384]{1,0:T(8,128)(2,1)S(1)} %constant_dynamic-update-slice_fusion.r34), channel_id=1, source_target_pairs={{0,64},{64,0},{128,192},{192,128},{256,320},{320,256},{384,448},{4... | collective-permute-start | bytes 1363976 | tf_op jit(solution)/shard_map/ppermute | solution.py:40

commit v4 on v3

--- a/solution.py
+++ b/solution.py
@@ -40,72 +40,116 @@
     return lax.ppermute(value, "ctx", [(i, i ^ 1) for i in range(2 * CHIPS)])
 
 
+def pack_kernel(latent_ref, ids_ref, out_ref):
+    out_ref[:KW, :] = latent_ref[...]
+    ids = jnp.broadcast_to(ids_ref[...].astype(jnp.float32), (ROWS - KW, TOK))
+    out_ref[KW:, :] = ids.astype(jnp.bfloat16)
+
+
+def rows_kernel(query_ref, grad_ref, rows_ref, cols_ref):
+    rows_ref[:QH, :] = query_ref[...]
+    rows_ref[QH:, :LATENT] = grad_ref[...]
+    rows_ref[QH:, LATENT:] = jnp.zeros((QH, KW - LATENT), jnp.bfloat16)
+    cols_ref[:, :QH] = query_ref[...].T
+    cols_ref[:LATENT, QH:] = grad_ref[...].T
+    cols_ref[LATENT:, QH:] = jnp.zeros((KW - LATENT, QH), jnp.bfloat16)
+
+
+def block_dots(rows_ref, blocks, out_ref):
+    for k in range(0, BACK - 1, 2):
+        two = jnp.concatenate([blocks[k, :KW, :], blocks[k + 1, :KW, :]], axis=1)
+        both = jnp.dot(rows_ref[...], two, preferred_element_type=jnp.float32)
+        out_ref[k] = both[:, :TOK]
+        out_ref[k + 1] = both[:, TOK:]
+    out_ref[BACK - 1] = jnp.dot(
+        rows_ref[...], blocks[BACK - 1, :KW, :], preferred_element_type=jnp.float32
+    )
+
+
+def scores_kernel(own, rows_ref, out_ref):
+    block_dots(rows_ref, own, out_ref)
+
+
+def grads_of(cols_ref, mixed, k):
+    g = jnp.dot(cols_ref[...], mixed[k], preferred_element_type=jnp.float32)
+    return g.astype(jnp.bfloat16)
+
+
+def lanes_of(core):
+    mine = pl.ds(pl.multiple_of(core * TOK, TOK), TOK)
+    other = pl.ds(pl.multiple_of((1 - core) * TOK, TOK), TOK)
+    return mine, other
+
+
 def attention_kernel(
-    info, own, par, rows_ref, cols_ref,
-    keep_ref, send_ref, mid_ref, keys, score, dprob, mixed,
+    info, own, par, own_both, rows_ref, cols_ref, send_ref, mixed, par_both, score
 ):
     chip, core = info[0], info[1]
-
-    mine = pl.ds(pl.multiple_of(core * TOK, TOK), TOK)
-    other = pl.ds(pl.multiple_of((1 - core) * TOK, TOK), TOK)
-    for k in range(BACK):
-        keys[k, :, mine] = own[k]
-        keys[k, :, other] = par[k]
-
+    block_dots(rows_ref, par, par_both)
     own_ids = own[0, KW:ROWS, :].astype(jnp.float32)[0:1]
     lane = lax.broadcasted_iota(jnp.int32, (1, TOK), 1)
     query_ids = [
         jnp.sum(jnp.where(lane == TOK - Q_DEV + i, own_ids, 0.0), axis=1, keepdims=True)
         for i in range(Q_DEV)
     ]
-    pair_lane = lax.broadcasted_iota(jnp.int32, (1, PAIR), 1)
+    both = (own_both, par_both)
     tops = [None] * Q_DEV
     for k in range(BACK):
-        both = jnp.dot(rows_ref[...], keys[k, :KW, :], preferred_element_type=jnp.float32)
-        ids = keys[k, KW:ROWS, :].astype(jnp.float32)[0:1]
-        place = pair_lane - k * PAIR
         there = chip - k >= 0
-        for i in range(Q_DEV):
-            at = core * TOK + TOK - Q_DEV + i
-            allowed = (ids == query_ids[i]) & (place <= at) & there
-            part = slice(i * HEADS, (i + 1) * HEADS)
-            s = jnp.where(allowed, both[part] * score_scale, -1e30)
-            score[k, part, :] = s
-            tops[i] = s if k == 0 else jnp.maximum(tops[i], s)
-        dprob[k] = both[QH:]
+        for side, keys in enumerate((own, par)):
+            ids = keys[k, KW:ROWS, :].astype(jnp.float32)[0:1]
+            place = lane - k * PAIR + (core if side == 0 else 1 - core) * TOK
+            for i in range(Q_DEV):
+                at = core * TOK + TOK - Q_DEV + i
+                allowed = (ids == query_ids[i]) & (place <= at) & there
+                part = slice(i * HEADS, (i + 1) * HEADS)
+                s = jnp.where(allowed, both[side][k, part, :] * score_scale, -1e30)
+                score[side, k, part, :] = s
+                tops[i] = s if tops[i] is None else jnp.maximum(tops[i], s)
     for i in range(Q_DEV):
         part = slice(i * HEADS, (i + 1) * HEADS)
+        low = slice(QH + i * HEADS, QH + (i + 1) * HEADS)
         top = jnp.max(tops[i], axis=1, keepdims=True)
         total = dots = None
         for k in range(BACK):
-            e = jnp.exp(score[k, part, :] - top)
-            score[k, part, :] = e
-            w = e * dprob[k, part, :]
-            total = e if k == 0 else total + e
-            dots = w if k == 0 else dots + w
+            for side in range(2):
+                e = jnp.exp(score[side, k, part, :] - top)
+                score[side, k, part, :] = e
+                w = e * both[side][k, low, :]
+                total = e if total is None else total + e
+                dots = w if dots is None else dots + w
         inv = 1.0 / jnp.sum(total, axis=1, keepdims=True)
         row_dot = jnp.sum(dots, axis=1, keepdims=True) * inv
         for k in range(BACK):
-            prob = score[k, part, :] * inv
-            grad = prob * (dprob[k, part, :] - row_dot) * score_scale
-            mixed[k, part, :] = grad.astype(jnp.bfloat16)
-            mixed[k, QH + i * HEADS : QH + (i + 1) * HEADS, :] = prob.astype(jnp.bfloat16)
-
-    blank = jnp.zeros((ROWS - KW, PAIR), jnp.bfloat16)
+            for side in range(2):
+                prob = score[side, k, part, :] * inv
+                grad = prob * (both[side][k, low, :] - row_dot) * score_scale
+                span = slice(side * TOK, (side + 1) * TOK)
+                mixed[k, part, span] = grad.astype(jnp.bfloat16)
+                mixed[k, low, span] = prob.astype(jnp.bfloat16)
+
+    mine, other = lanes_of(core)
     for slot in range(2):
-        keep_ref[slot, KW:, :] = blank
-        send_ref[slot, KW:, :] = blank
-    mid_ref[KW:, :] = (keys[2, KW:ROWS, :].astype(jnp.float32) * 0.5).astype(jnp.bfloat16)
-
-    def grads(k):
-        g = jnp.dot(cols_ref[...], mixed[k], preferred_element_type=jnp.float32)
-        return g.astype(jnp.bfloat16)
-
+        g = grads_of(cols_ref, mixed, jnp.where(core == 0, 4 - slot, slot))
+        send_ref[slot, :KW, mine] = g[:, :TOK]
+        send_ref[slot, :KW, other] = g[:, TOK:]
+        send_ref[slot, KW:, :] = jnp.zeros((ROWS - KW, PAIR), jnp.bfloat16)
+
+
+def kept_kernel(info, own, par, mixed, cols_ref, keep_ref, mid_ref):
+    core = info[1]
+    mine, other = lanes_of(core)
     for slot in range(2):
-        send_ref[slot, :KW, :] = grads(jnp.where(core == 0, 4 - slot, slot))
-    for slot in range(2):
-        keep_ref[slot, :KW, :] = grads(jnp.where(core == 0, slot, 4 - slot))
-    mid_ref[:KW, :] = grads(2)
+        g = grads_of(cols_ref, mixed, jnp.where(core == 0, slot, 4 - slot))
+        keep_ref[slot, :KW, mine] = g[:, :TOK]
+        keep_ref[slot, :KW, other] = g[:, TOK:]
+        keep_ref[slot, KW:, :] = jnp.zeros((ROWS - KW, PAIR), jnp.bfloat16)
+    g = grads_of(cols_ref, mixed, 2)
+    mid_ref[:KW, mine] = g[:, :TOK]
+    mid_ref[:KW, other] = g[:, TOK:]
+    for side, where in ((own, mine), (par, other)):
+        half = side[2, KW:ROWS, :].astype(jnp.float32) * 0.5
+        mid_ref[KW:, where] = half.astype(jnp.bfloat16)
 
 
 def vmem():
@@ -116,22 +160,54 @@
     return pl.BlockSpec(memory_space=pltpu.SMEM)
 
 
-def attention(info, own, par, rows, cols):
-    block = jax.ShapeDtypeStruct((2, ROWS, PAIR), jnp.bfloat16)
+def call(kernel, shapes, smem_first, count, mib, scratch, flops, name, operands):
+    specs = [smem()] * smem_first + [vmem()] * count
     return pl.pallas_call(
-        attention_kernel,
-        out_shape=(block, block, jax.ShapeDtypeStruct((ROWS, PAIR), jnp.bfloat16)),
-        in_specs=[smem()] + [vmem()] * 4,
-        out_specs=(vmem(), vmem(), vmem()),
-        scratch_shapes=[
-            pltpu.VMEM((BACK, ROWS, PAIR), jnp.bfloat16),
-            pltpu.VMEM((BACK, QH, PAIR), jnp.float32),
-            pltpu.VMEM((BACK, QH, PAIR), jnp.float32),
-            pltpu.VMEM((BACK, 2 * QH, PAIR), jnp.bfloat16),
-        ],
-        compiler_params=pltpu.CompilerParams(vmem_limit_bytes=24 * MIB),
-        name="attention_grads",
-    )(info, own, par, rows, cols)
+        kernel,
+        out_shape=shapes,
+        in_specs=specs,
+        out_specs=jax.tree.map(lambda _: vmem(), shapes),
+        scratch_shapes=scratch,
+        compiler_params=pltpu.CompilerParams(vmem_limit_bytes=mib * MIB),
+        cost_estimate=pl.CostEstimate(flops=flops, bytes_accessed=4 * MIB, transcendentals=0),
+        name=name,
+    )(*operands)
+
+
+def shape(dims, dtype=jnp.bfloat16):
+    return jax.ShapeDtypeStruct(dims, dtype)
+
+
+def pack(latent, ids):
+    return call(pack_kernel, shape((ROWS, TOK)), 0, 2, 4, [], 0, "pack_keys", (latent, ids))
+
+
+def query_views(queries, grads):
+    shapes = (shape((2 * QH, KW)), shape((KW, 2 * QH)))
+    return call(rows_kernel, shapes, 0, 2, 16, [], 0, "query_views", (queries, grads))
+
+
+def scores_of(own, rows):
+    out = shape((BACK, 2 * QH, TOK), jnp.float32)
+    flops = 4 * QH * KW * BACK * TOK
+    return call(scores_kernel, out, 0, 2, 20, [], flops, "own_scores", (own, rows))
+
+
+def attention(info, own, par, own_both, rows, cols):
+    shapes = (shape((2, ROWS, PAIR)), shape((BACK, 2 * QH, PAIR)))
+    scratch = [
+        pltpu.VMEM((BACK, 2 * QH, TOK), jnp.float32),
+        pltpu.VMEM((2, BACK, QH, TOK), jnp.float32),
+    ]
+    operands = (info, own, par, own_both, rows, cols)
+    flops = 8 * QH * KW * BACK * TOK
+    return call(attention_kernel, shapes, 1, 5, 28, scratch, flops, "attention_grads", operands)
+
+
+def kept(info, own, par, mixed, cols):
+    shapes = (shape((2, ROWS, PAIR)), shape((ROWS, PAIR)))
+    flops = 6 * 2 * QH * KW * PAIR
+    return call(kept_kernel, shapes, 1, 4, 20, [], flops, "kept_grads", (info, own, par, mixed, cols))
 
 
 def down_kernel(
@@ -236,20 +312,21 @@
     position = lax.axis_index("ctx")
     core = position % 2
     info = jnp.stack([position // 2, core]).astype(jnp.int32)
-    ids = jnp.pad(doc_ids.astype(jnp.bfloat16), ((0, ROWS - KW - 1), (0, 0)))
-    keys = jnp.concatenate([latent[0].T, ids], axis=0)
+    keys = pack(latent[0].T, doc_ids)
     near = chip_shift(keys, 1, 1)
-    fourth = chip_shift(keys, 4, 4)
     next_near = chip_shift(keys, 2, 2)
-    next_near, query_rows, grad_rows = lax.optimization_barrier((next_near, queries, out_grad))
-    query_rows = query_rows[0].reshape(QH, KW)
-    grad_rows = grad_rows[0].reshape(QH, LATENT)
-    rows = jnp.concatenate([query_rows, jnp.pad(grad_rows, ((0, 0), (0, KW - LATENT)))], axis=0)
-    cols = rows.T
-    own = jnp.stack([keys, near, next_near, chip_shift(near, 2, 2), fourth])
+    query_rows = queries[0].reshape(QH, KW)
+    far_keys, query_rows = lax.optimization_barrier((keys, query_rows))
+    fourth = chip_shift(far_keys, 4, 4)
+    near, grads = lax.optimization_barrier((near, out_grad))
+    grad_rows = grads[0].reshape(QH, LATENT)
+    rows, cols = query_views(query_rows, grad_rows)
+    third = chip_shift(near, 2, 2)
+    own = jnp.stack([keys, near, next_near, third, fourth])
     own, rows, cols, info = lax.optimization_barrier((own, rows, cols, info))
     par = core_swap(own)
-    keep, send, mid = attention(info, own, par, rows, cols)
+    send, mixed = attention(info, own, par, scores_of(own, rows), rows, cols)
+    keep, mid = kept(info, own, par, mixed, cols)
 
     arrived = core_swap(send)
     far = chip_shift(added(keep[0], arrived[0]), 2, -2)

time: 151 us -> 147 us (0.974)
  other arithmetic: 5.06 us -> 1.28 us
  waiting for transfers between devices: 37 us -> 39 us
    ppermute x10, waiting for transfers between devices: 31.1 us -> 34.6 us  [chip_shift(): return lax.ppermute(value, 'ctx', pairs)]
    optimization_barrier x1 -> x0, local copies, waits for them, and re-layouts: 1.7 us -> none  [group_part(): own, rows, cols, info = lax.optimization_barrier((own, rows, cols, info))]
    pallas_call x1 -> x5, Pallas kernels: 6.86 us -> 7.63 us  [call(): pl.pallas_call(kernel, out_shape=shapes, in_specs=specs, out_specs=jax.tr...]
  transfers between devices with their start and end apart: 15 -> 15, of which waited for: 11 -> 12; matrix products, arithmetic and copies ran while one was open for 5% -> 2% of each run, Pallas kernels for 0% -> 2%
where the time goes in v4:
time: 147 us
  starting transfers between devices  56.4 us (38%)
  waiting for transfers between devices  39 us (27%)
  blocking collectives  33 us (22%)
  Pallas kernels  12 us (8%)
  local copies, waits for them, and re-layouts  4.04 us (3%)
    ppermute x10, starting transfers between devices, chip_shift(): return lax.ppermute(value, 'ctx', pairs)  46.6 us
    ppermute x10, waiting for transfers between devices, chip_shift(): return lax.ppermute(value, 'ctx', pairs)  34.6 us
    all_to_all x1, blocking collectives, on_device(): chunks = lax.all_to_all(chunks, 'grp', 0, 0, tiled=True)  33 us
    ppermute x5, starting transfers between devices, core_swap(): return lax.ppermute(value, 'ctx', [(i, i ^ 1) for i in range(2 * CHIPS)])  9.86 us
    pallas_call x5, Pallas kernels, call(): pl.pallas_call(kernel, out_shape=shapes, in_specs=specs, out_specs=jax.tr...  7.63 us
    ppermute x5, waiting for transfers between devices, core_swap(): return lax.ppermute(value, 'ctx', [(i, i ^ 1) for i in range(2 * CHIPS)])  4.4 us
    pallas_call x1, Pallas kernels, down_grad(): pl.pallas_call(down_kernel, out_shape=(jax.ShapeDtypeStruct((SLOT, SLOT),...  4.35 us
  transfers between devices with their start and end apart: 15, of which 12 were waited for; matrix products, arithmetic and copies ran while one was open for 2% of the time, Pallas kernels for 2%

profile of v4, /device:TPU:4, one launch (start us, length us, event | category | flops | bytes accessed | tf_op | source)
XLA Modules:
  0.0 146.7 jit_solution(10601344957523753715)
XLA Ops:
  0.6 0.9 copy-done.1
  2.2 8.0 %collective-permute-start.1 = (bf16[592,128]{1,0:T(8,128)(2,1)S(1)}, bf16[592,128]{1,0:T(8,128)(2,1)S(1)}, u32[]{:S(2)}, u32[]{:S(2)}) collective-permute-start(bf16[592,128]{1,0:T(8,128)(2,1)S(1)} %pack_keys.1), channel_id=1, source_target_pairs={{0,256},{64,320},{128,384},{192,448},{256,512},{320,576},{384,640}... | collective-permute-start | bytes 454664 | tf_op jit(solution)/shard_map/ppermute | solution.py:36
  10.3 5.2 %collective-permute-start = (bf16[592,128]{1,0:T(8,128)(2,1)S(1)}, bf16[592,128]{1,0:T(8,128)(2,1)S(1)}, u32[]{:S(2)}, u32[]{:S(2)}) collective-permute-start(bf16[592,128]{1,0:T(8,128)(2,1)S(1)} %pack_keys.1), channel_id=1, source_target_pairs={{0,128},{64,192},{128,256},{192,320},{256,384},{320,448},{384,512}... | collective-permute-start | bytes 454664 | tf_op jit(solution)/shard_map/ppermute | solution.py:36
  15.5 1.7 %reshape_squeeze.6.query_ref = bf16[512,576]{1,0:T(8,128)(2,1)S(1)} reshape(bf16[1,4,73728]{2,1,0:T(4,128)(2,1)} %param.7) | data formatting | bytes 1179648 | tf_op jit(solution)/shard_map/reshape;squeeze | solution.py:318
  17.2 11.9 %collective-permute-start.3 = (bf16[592,128]{1,0:T(8,128)(2,1)S(1)}, bf16[592,128]{1,0:T(8,128)(2,1)S(1)}, u32[]{:S(2)}, u32[]{:S(2)}) collective-permute-start(bf16[592,128]{1,0:T(8,128)(2,1)S(1)} %pack_keys.1), channel_id=1, source_target_pairs={{0,512},{64,576},{128,640},{192,704},{256,768},{320,832},{384,896}... | collective-permute-start | bytes 454664 | tf_op jit(solution)/shard_map/ppermute | solution.py:36
  29.3 1.9 %collective-permute-start.2 = (bf16[592,128]{1,0:T(8,128)(2,1)S(1)}, bf16[592,128]{1,0:T(8,128)(2,1)S(1)}, u32[]{:S(2)}, u32[]{:S(2)}) collective-permute-start(bf16[592,128]{1,0:T(8,128)(2,1)S(1)} %collective-permute-done), channel_id=1, source_target_pairs={{0,256},{64,320},{128,384},{192,448},{256,512},{320,576},{384,640}... | collective-permute-start | bytes 454664 | tf_op jit(solution)/shard_map/ppermute | solution.py:36
  32.2 13.4 %collective-permute-done.2 = bf16[592,128]{1,0:T(8,128)(2,1)S(1)} collective-permute-done((bf16[592,128]{1,0:T(8,128)(2,1)S(1)}, bf16[592,128]{1,0:T(8,128)(2,1)S(1)}, u32[]{:S(2)}, u32[]{:S(2)}) %collective-permute-start.2) | collective-permute-done | bytes 151584 | tf_op jit(solution)/shard_map/ppermute | solution.py:36
  45.7 1.9 %collective-permute-start.4 = (bf16[5,592,128]{2,1,0:T(8,128)(2,1)S(1)}, bf16[5,592,128]{2,1,0:T(8,128)(2,1)S(1)}, u32[]{:S(2)}, u32[]{:S(2)}) collective-permute-start(bf16[5,592,128]{2,1,0:T(8,128)(2,1)S(1)} %bitcast_dynamic-update-slice_fusion.own), channel_id=1, source_target_pairs={{0,64},{64,0},{128,192},{192,128},{256,320},{320,256},{384,448},{4... | collective-permute-start | bytes 2273288 | tf_op jit(solution)/shard_map/ppermute | solution.py:40
  47.6 1.3 own_scores.1.own_both
  48.9 0.9 collective-permute-done.4.par
  49.8 4.2 %attention_grads.1 = (bf16[2,592,256]{2,1,0:T(8,128)(2,1)S(1)}, bf16[5,1024,256]{2,1,0:T(8,128)(2,1)S(1)}) custom-call(s32[2]{0:T(128)S(1)} %pad_add_fusion.info, bf16[5,592,128]{2,1,0:T(8,128)(2,1)S(1)} %bitcast_dynamic-update-slice_fusion.own, bf16[5,592,128]{2,1,0:T(8,128)(2,1)S(1)} %collective-permute-done.4.par, ...), custom_call_target="tpu_custom_call" | custom-call | flops 1509949440 | bytes 4194304 | tf_op jit(solution)/shard_map/attention_grads/pallas_call | solution.py:165
  54.0 2.0 %collective-permute-start.5 = (bf16[2,592,256]{2,1,0:T(8,128)(2,1)S(1)}, bf16[2,592,256]{2,1,0:T(8,128)(2,1)S(1)}, u32[]{:S(2)}, u32[]{:S(2)}) collective-permute-start(bf16[2,592,256]{2,1,0:T(8,128)(2,1)S(1)} %get-tuple-element.34), channel_id=1, source_target_pairs={{0,64},{64,0},{128,192},{192,128},{256,320},{320,256},{384,448},{4... | collective-permute-start | bytes 1818632 | tf_op jit(solution)/shard_map/ppermute | solution.py:40
  56.1 1.7 %kept_grads.1 = (bf16[2,592,256]{2,1,0:T(8,128)(2,1)S(1)}, bf16[592,256]{1,0:T(8,128)(2,1)S(1)}) custom-call(s32[2]{0:T(128)S(1)} %pad_add_fusion.info, bf16[5,592,128]{2,1,0:T(8,128)(2,1)S(1)} %bitcast_dynamic-update-slice_fusion.own, bf16[5,592,128]{2,1,0:T(8,128)(2,1)S(1)} %collective-permute-done.4.par, ...), custom_call_target="tpu_custom_call" | custom-call | flops 905969664 | bytes 4194304 | tf_op jit(solution)/shard_map/kept_grads/pallas_call | solution.py:165
  58.1 1.9 %collective-permute-start.6 = (bf16[592,256]{1,0:T(8,128)(2,1)S(1)}, bf16[592,256]{1,0:T(8,128)(2,1)S(1)}, u32[]{:S(2)}, u32[]{:S(2)}) collective-permute-start(bf16[592,256]{1,0:T(8,128)(2,1)S(1)} %get-tuple-element.40), channel_id=1, source_target_pairs={{0,256},{64,832},{128,384},{192,960},{256,512},{320,64},{384,640},... | collective-permute-start | bytes 909320 | tf_op jit(solution)/shard_map/ppermute | solution.py:36
  60.0 1.9 %collective-permute-start.7 = (bf16[592,256]{1,0:T(8,128)(2,1)S(1)}, bf16[592,256]{1,0:T(8,128)(2,1)S(1)}, u32[]{:S(2)}, u32[]{:S(2)}) collective-permute-start(bf16[592,256]{1,0:T(8,128)(2,1)S(1)} %get-tuple-element.41), channel_id=1, source_target_pairs={{0,128},{64,960},{128,256},{192,64},{256,384},{320,192},{384,512},... | collective-permute-start | bytes 909320 | tf_op jit(solution)/shard_map/ppermute | solution.py:36
  62.0 8.8 %collective-permute-done.6 = bf16[592,256]{1,0:T(8,128)(2,1)S(1)} collective-permute-done((bf16[592,256]{1,0:T(8,128)(2,1)S(1)}, bf16[592,256]{1,0:T(8,128)(2,1)S(1)}, u32[]{:S(2)}, u32[]{:S(2)}) %collective-permute-start.6) | collective-permute-done | bytes 303136 | tf_op jit(solution)/shard_map/ppermute | solution.py:36
  70.8 2.3 %collective-permute-done.7 = bf16[592,256]{1,0:T(8,128)(2,1)S(1)} collective-permute-done((bf16[592,256]{1,0:T(8,128)(2,1)S(1)}, bf16[592,256]{1,0:T(8,128)(2,1)S(1)}, u32[]{:S(2)}, u32[]{:S(2)}) %collective-permute-start.7) | collective-permute-done | bytes 303136 | tf_op jit(solution)/shard_map/ppermute | solution.py:36
  73.3 2.1 %collective-permute-start.8 = (bf16[592,256]{1,0:T(8,128)(2,1)S(1)}, bf16[592,256]{1,0:T(8,128)(2,1)S(1)}, u32[]{:S(2)}, u32[]{:S(2)}) collective-permute-start(bf16[592,256]{1,0:T(8,128)(2,1)S(1)} %add_convert_fusion.1), channel_id=1, source_target_pairs={{0,64},{64,0},{128,192},{192,128},{256,320},{320,256},{384,448},{4... | collective-permute-start | bytes 909320 | tf_op jit(solution)/shard_map/ppermute | solution.py:40
  75.3 1.6 %collective-permute-done.8 = bf16[592,256]{1,0:T(8,128)(2,1)S(1)} collective-permute-done((bf16[592,256]{1,0:T(8,128)(2,1)S(1)}, bf16[592,256]{1,0:T(8,128)(2,1)S(1)}, u32[]{:S(2)}, u32[]{:S(2)}) %collective-permute-start.8) | collective-permute-done | bytes 303136 | tf_op jit(solution)/shard_map/ppermute | solution.py:40
  77.0 1.9 %collective-permute-start.9 = (bf16[592,256]{1,0:T(8,128)(2,1)S(1)}, bf16[592,256]{1,0:T(8,128)(2,1)S(1)}, u32[]{:S(2)}, u32[]{:S(2)}) collective-permute-start(bf16[592,256]{1,0:T(8,128)(2,1)S(1)} %add_convert_fusion.g0), channel_id=1, source_target_pairs={{0,128},{64,960},{128,256},{192,64},{256,384},{320,192},{384,512},... | collective-permute-start | bytes 909320 | tf_op jit(solution)/shard_map/ppermute | solution.py:36
  78.9 4.2 %collective-permute-start.10 = (bf16[592,256]{1,0:T(8,128)(2,1)S(1)}, bf16[592,256]{1,0:T(8,128)(2,1)S(1)}, u32[]{:S(2)}, u32[]{:S(2)}) collective-permute-start(bf16[592,256]{1,0:T(8,128)(2,1)S(1)} %add_convert_fusion.g0), channel_id=1, source_target_pairs={{0,256},{64,832},{128,384},{192,960},{256,512},{320,64},{384,640},... | collective-permute-start | bytes 909320 | tf_op jit(solution)/shard_map/ppermute | solution.py:36
  83.2 5.6 %collective-permute-done.9 = bf16[592,256]{1,0:T(8,128)(2,1)S(1)} collective-permute-done((bf16[592,256]{1,0:T(8,128)(2,1)S(1)}, bf16[592,256]{1,0:T(8,128)(2,1)S(1)}, u32[]{:S(2)}, u32[]{:S(2)}) %collective-permute-start.9) | collective-permute-done | bytes 303136 | tf_op jit(solution)/shard_map/ppermute | solution.py:36
  88.8 1.9 %collective-permute-start.11 = (bf16[592,256]{1,0:T(8,128)(2,1)S(1)}, bf16[592,256]{1,0:T(8,128)(2,1)S(1)}, u32[]{:S(2)}, u32[]{:S(2)}) collective-permute-start(bf16[592,256]{1,0:T(8,128)(2,1)S(1)} %collective-permute-done.9), channel_id=1, source_target_pairs={{0,256},{64,832},{128,384},{192,960},{256,512},{320,64},{384,640},... | collective-permute-start | bytes 909320 | tf_op jit(solution)/shard_map/ppermute | solution.py:36
  90.7 2.1 %collective-permute-done.10 = bf16[592,256]{1,0:T(8,128)(2,1)S(1)} collective-permute-done((bf16[592,256]{1,0:T(8,128)(2,1)S(1)}, bf16[592,256]{1,0:T(8,128)(2,1)S(1)}, u32[]{:S(2)}, u32[]{:S(2)}) %collective-permute-start.10) | collective-permute-done | bytes 303136 | tf_op jit(solution)/shard_map/ppermute | solution.py:36
  92.9 7.7 %collective-permute-start.12 = (bf16[592,128]{1,0:T(8,128)(2,1)S(1)}, bf16[592,128]{1,0:T(8,128)(2,1)S(1)}, u32[]{:S(2)}, u32[]{:S(2)}) collective-permute-start(bf16[592,128]{1,0:T(8,128)(2,1)S(1)} %slice_select_fusion), channel_id=1, source_target_pairs={{0,256},{64,832},{128,384},{192,960},{256,512},{320,64},{384,640},... | collective-permute-start | bytes 454664 | tf_op jit(solution)/shard_map/ppermute | solution.py:36
  100.6 0.9 collective-permute-done.11
  101.5 1.9 %collective-permute-start.13 = (bf16[2,592,256]{2,1,0:T(8,128)(2,1)S(1)}, bf16[2,592,256]{2,1,0:T(8,128)(2,1)S(1)}, u32[]{:S(2)}, u32[]{:S(2)}) collective-permute-start(bf16[2,592,256]{2,1,0:T(8,128)(2,1)S(1)} %pad_maximum_fusion.r12), channel_id=1, source_target_pairs={{0,64},{64,0},{128,192},{192,128},{256,320},{320,256},{384,448},{4... | collective-permute-start | bytes 1818632 | tf_op jit(solution)/shard_map/ppermute | solution.py:40
  103.5 1.2 collective-permute-done.12
  104.7 1.9 %collective-permute-start.14 = (bf16[592,384]{1,0:T(8,128)(2,1)S(1)}, bf16[592,384]{1,0:T(8,128)(2,1)S(1)}, u32[]{:S(2)}, u32[]{:S(2)}) collective-permute-start(bf16[592,384]{1,0:T(8,128)(2,1)S(1)} %constant_dynamic-update-slice_fusion.r34), channel_id=1, source_target_pairs={{0,64},{64,0},{128,192},{192,128},{256,320},{320,256},{384,448},{4... | collective-permute-start | bytes 1363976 | tf_op jit(solution)/shard_map/ppermute | solution.py:40
  106.7 1.8 %collective-permute-done.14.s34 = bf16[592,384]{1,0:T(8,128)(2,1)S(1)} collective-permute-done((bf16[592,384]{1,0:T(8,128)(2,1)S(1)}, bf16[592,384]{1,0:T(8,128)(2,1)S(1)}, u32[]{:S(2)}, u32[]{:S(2)}) %collective-permute-start.14) | collective-permute-done | bytes 454688 | tf_op jit(solution)/shard_map/ppermute | solution.py:40
  108.4 4.4 %down_grad.1 = (bf16[512,512]{1,0:T(8,128)(2,1)S(1)}, bf16[576,128]{1,0:T(8,128)(2,1)}) custom-call(s32[2]{0:T(128)S(1)} %pad_add_fusion.info, f32[1,8]{1,0:T(1,128)S(1)} %copy-done.3, bf16[592,256]{1,0:T(8,128)(2,1)S(1)} %add_convert_fusion.g0, bf16[2,592,256]{2,1,0:T(8,128)(2,1)S(1)} %pad_maximum_fusion.r12, ...), custom_call_target="tpu_custom_call" | custom-call | tf_op jit(solution)/shard_map/down_grad/pallas_call | solution.py:286
  112.8 33.0 %all_to_all.5 = bf16[64,8,512]{2,1,0:T(8,128)(2,1)S(1)} all-to-all(bf16[64,8,512]{2,1,0:T(8,128)(2,1)S(1)} %bitcast.30), channel_id=1, replica_groups=mesh['ctx'=16,'grp'=64] {'grp'}, dimensions={0} | all-to-all | bytes 1048576 | tf_op jit(solution)/shard_map/all_to_all | solution.py:355
  (34 shorter events, 3.5 us)
Async XLA Ops:
  0.6 0.9 copy-start.1
  1.5 0.7 copy-start.2
  2.2 29.0 %copy-start.4 = (bf16[1,4,65536]{2,1,0:T(4,128)(2,1)S(1)}, bf16[1,4,65536]{2,1,0:T(4,128)(2,1)}, u32[]{:S(2)}) copy-start(bf16[1,4,65536]{2,1,0:T(4,128)(2,1)} %param.8) | copy-start | bytes 1572868
  2.2 29.9 %collective-permute-start.1 = (bf16[592,128]{1,0:T(8,128)(2,1)S(1)}, bf16[592,128]{1,0:T(8,128)(2,1)S(1)}, u32[]{:S(2)}, u32[]{:S(2)}) collective-permute-start(bf16[592,128]{1,0:T(8,128)(2,1)S(1)} %pack_keys.1), channel_id=1, source_target_pairs={{0,256},{64,320},{128,384},{192,448},{256,512},{320,576},{384,640}... | collective-permute-start | bytes 454664 | tf_op jit(solution)/shard_map/ppermute | solution.py:36
  10.3 19.1 %collective-permute-start = (bf16[592,128]{1,0:T(8,128)(2,1)S(1)}, bf16[592,128]{1,0:T(8,128)(2,1)S(1)}, u32[]{:S(2)}, u32[]{:S(2)}) collective-permute-start(bf16[592,128]{1,0:T(8,128)(2,1)S(1)} %pack_keys.1), channel_id=1, source_target_pairs={{0,128},{64,192},{128,256},{192,320},{256,384},{320,448},{384,512}... | collective-permute-start | bytes 454664 | tf_op jit(solution)/shard_map/ppermute | solution.py:36
  17.2 28.4 %collective-permute-start.3 = (bf16[592,128]{1,0:T(8,128)(2,1)S(1)}, bf16[592,128]{1,0:T(8,128)(2,1)S(1)}, u32[]{:S(2)}, u32[]{:S(2)}) collective-permute-start(bf16[592,128]{1,0:T(8,128)(2,1)S(1)} %pack_keys.1), channel_id=1, source_target_pairs={{0,512},{64,576},{128,640},{192,704},{256,768},{320,832},{384,896}... | collective-permute-start | bytes 454664 | tf_op jit(solution)/shard_map/ppermute | solution.py:36
  29.3 16.3 %collective-permute-start.2 = (bf16[592,128]{1,0:T(8,128)(2,1)S(1)}, bf16[592,128]{1,0:T(8,128)(2,1)S(1)}, u32[]{:S(2)}, u32[]{:S(2)}) collective-permute-start(bf16[592,128]{1,0:T(8,128)(2,1)S(1)} %collective-permute-done), channel_id=1, source_target_pairs={{0,256},{64,320},{128,384},{192,448},{256,512},{320,576},{384,640}... | collective-permute-start | bytes 454664 | tf_op jit(solution)/shard_map/ppermute | solution.py:36
  45.7 4.1 %collective-permute-start.4 = (bf16[5,592,128]{2,1,0:T(8,128)(2,1)S(1)}, bf16[5,592,128]{2,1,0:T(8,128)(2,1)S(1)}, u32[]{:S(2)}, u32[]{:S(2)}) collective-permute-start(bf16[5,592,128]{2,1,0:T(8,128)(2,1)S(1)} %bitcast_dynamic-update-slice_fusion.own), channel_id=1, source_target_pairs={{0,64},{64,0},{128,192},{192,128},{256,320},{320,256},{384,448},{4... | collective-permute-start | bytes 2273288 | tf_op jit(solution)/shard_map/ppermute | solution.py:40
  54.0 3.9 %collective-permute-start.5 = (bf16[2,592,256]{2,1,0:T(8,128)(2,1)S(1)}, bf16[2,592,256]{2,1,0:T(8,128)(2,1)S(1)}, u32[]{:S(2)}, u32[]{:S(2)}) collective-permute-start(bf16[2,592,256]{2,1,0:T(8,128)(2,1)S(1)} %get-tuple-element.34), channel_id=1, source_target_pairs={{0,64},{64,0},{128,192},{192,128},{256,320},{320,256},{384,448},{4... | collective-permute-start | bytes 1818632 | tf_op jit(solution)/shard_map/ppermute | solution.py:40
  58.1 12.6 %collective-permute-start.6 = (bf16[592,256]{1,0:T(8,128)(2,1)S(1)}, bf16[592,256]{1,0:T(8,128)(2,1)S(1)}, u32[]{:S(2)}, u32[]{:S(2)}) collective-permute-start(bf16[592,256]{1,0:T(8,128)(2,1)S(1)} %get-tuple-element.40), channel_id=1, source_target_pairs={{0,256},{64,832},{128,384},{192,960},{256,512},{320,64},{384,640},... | collective-permute-start | bytes 909320 | tf_op jit(solution)/shard_map/ppermute | solution.py:36
  60.0 13.1 %collective-permute-start.7 = (bf16[592,256]{1,0:T(8,128)(2,1)S(1)}, bf16[592,256]{1,0:T(8,128)(2,1)S(1)}, u32[]{:S(2)}, u32[]{:S(2)}) collective-permute-start(bf16[592,256]{1,0:T(8,128)(2,1)S(1)} %get-tuple-element.41), channel_id=1, source_target_pairs={{0,128},{64,960},{128,256},{192,64},{256,384},{320,192},{384,512},... | collective-permute-start | bytes 909320 | tf_op jit(solution)/shard_map/ppermute | solution.py:36
  73.2 35.2 %copy-start = (bf16[1,2048,448]{1,2,0:T(8,128)(2,1)S(1)}, bf16[1,2048,448]{1,2,0:T(8,128)(2,1)}, u32[]{:S(2)}) copy-start(bf16[1,2048,448]{1,2,0:T(8,128)(2,1)} %param.9) | copy-start | bytes 5505028
  73.3 35.2 %copy-start.3 = (f32[1,8]{1,0:T(1,128)S(1)}, f32[1,8]{1,0:T(1,128)}, u32[]{:S(2)}) copy-start(f32[1,8]{1,0:T(1,128)} %limits.1) | copy-start | bytes 100
  73.3 3.6 %collective-permute-start.8 = (bf16[592,256]{1,0:T(8,128)(2,1)S(1)}, bf16[592,256]{1,0:T(8,128)(2,1)S(1)}, u32[]{:S(2)}, u32[]{:S(2)}) collective-permute-start(bf16[592,256]{1,0:T(8,128)(2,1)S(1)} %add_convert_fusion.1), channel_id=1, source_target_pairs={{0,64},{64,0},{128,192},{192,128},{256,320},{320,256},{384,448},{4... | collective-permute-start | bytes 909320 | tf_op jit(solution)/shard_map/ppermute | solution.py:40
  77.0 11.8 %collective-permute-start.9 = (bf16[592,256]{1,0:T(8,128)(2,1)S(1)}, bf16[592,256]{1,0:T(8,128)(2,1)S(1)}, u32[]{:S(2)}, u32[]{:S(2)}) collective-permute-start(bf16[592,256]{1,0:T(8,128)(2,1)S(1)} %add_convert_fusion.g0), channel_id=1, source_target_pairs={{0,128},{64,960},{128,256},{192,64},{256,384},{320,192},{384,512},... | collective-permute-start | bytes 909320 | tf_op jit(solution)/shard_map/ppermute | solution.py:36
  78.9 14.0 %collective-permute-start.10 = (bf16[592,256]{1,0:T(8,128)(2,1)S(1)}, bf16[592,256]{1,0:T(8,128)(2,1)S(1)}, u32[]{:S(2)}, u32[]{:S(2)}) collective-permute-start(bf16[592,256]{1,0:T(8,128)(2,1)S(1)} %add_convert_fusion.g0), channel_id=1, source_target_pairs={{0,256},{64,832},{128,384},{192,960},{256,512},{320,64},{384,640},... | collective-permute-start | bytes 909320 | tf_op jit(solution)/shard_map/ppermute | solution.py:36
  88.8 12.7 %collective-permute-start.11 = (bf16[592,256]{1,0:T(8,128)(2,1)S(1)}, bf16[592,256]{1,0:T(8,128)(2,1)S(1)}, u32[]{:S(2)}, u32[]{:S(2)}) collective-permute-start(bf16[592,256]{1,0:T(8,128)(2,1)S(1)} %collective-permute-done.9), channel_id=1, source_target_pairs={{0,256},{64,832},{128,384},{192,960},{256,512},{320,64},{384,640},... | collective-permute-start | bytes 909320 | tf_op jit(solution)/shard_map/ppermute | solution.py:36
  92.9 11.8 %collective-permute-start.12 = (bf16[592,128]{1,0:T(8,128)(2,1)S(1)}, bf16[592,128]{1,0:T(8,128)(2,1)S(1)}, u32[]{:S(2)}, u32[]{:S(2)}) collective-permute-start(bf16[592,128]{1,0:T(8,128)(2,1)S(1)} %slice_select_fusion), channel_id=1, source_target_pairs={{0,256},{64,832},{128,384},{192,960},{256,512},{320,64},{384,640},... | collective-permute-start | bytes 454664 | tf_op jit(solution)/shard_map/ppermute | solution.py:36
  101.5 6.9 %collective-permute-start.13 = (bf16[2,592,256]{2,1,0:T(8,128)(2,1)S(1)}, bf16[2,592,256]{2,1,0:T(8,128)(2,1)S(1)}, u32[]{:S(2)}, u32[]{:S(2)}) collective-permute-start(bf16[2,592,256]{2,1,0:T(8,128)(2,1)S(1)} %pad_maximum_fusion.r12), channel_id=1, source_target_pairs={{0,64},{64,0},{128,192},{192,128},{256,320},{320,256},{384,448},{4... | collective-permute-start | bytes 1818632 | tf_op jit(solution)/shard_map/ppermute | solution.py:40
  104.7 3.7 %collective-permute-start.14 = (bf16[592,384]{1,0:T(8,128)(2,1)S(1)}, bf16[592,384]{1,0:T(8,128)(2,1)S(1)}, u32[]{:S(2)}, u32[]{:S(2)}) collective-permute-start(bf16[592,384]{1,0:T(8,128)(2,1)S(1)} %constant_dynamic-update-slice_fusion.r34), channel_id=1, source_target_pairs={{0,64},{64,0},{128,192},{192,128},{256,320},{320,256},{384,448},{4... | collective-permute-start | bytes 1363976 | tf_op jit(solution)/shard_map/ppermute | solution.py:40

commit v5 on v4

--- a/solution.py
+++ b/solution.py
@@ -316,7 +316,7 @@
     near = chip_shift(keys, 1, 1)
     next_near = chip_shift(keys, 2, 2)
     query_rows = queries[0].reshape(QH, KW)
-    far_keys, query_rows = lax.optimization_barrier((keys, query_rows))
+    far_keys, info = lax.optimization_barrier((keys, info))
     fourth = chip_shift(far_keys, 4, 4)
     near, grads = lax.optimization_barrier((near, out_grad))
     grad_rows = grads[0].reshape(QH, LATENT)

time: 147 us -> 146 us (level)
  waiting for transfers between devices: 39 us -> 37.1 us
    ppermute x10, waiting for transfers between devices: 34.6 us -> 33 us  [chip_shift(): return lax.ppermute(value, 'ctx', pairs)]
where the time goes in v5:
time: 146 us
  starting transfers between devices  57.1 us (39%)
  waiting for transfers between devices  37.1 us (25%)
  blocking collectives  33.3 us (23%)
  Pallas kernels  12 us (8%)
  local copies, waits for them, and re-layouts  4.04 us (3%)
    ppermute x10, starting transfers between devices, chip_shift(): return lax.ppermute(value, 'ctx', pairs)  46.8 us
    all_to_all x1, blocking collectives, on_device(): chunks = lax.all_to_all(chunks, 'grp', 0, 0, tiled=True)  33.3 us
    ppermute x10, waiting for transfers between devices, chip_shift(): return lax.ppermute(value, 'ctx', pairs)  33 us
    ppermute x5, starting transfers between devices, core_swap(): return lax.ppermute(value, 'ctx', [(i, i ^ 1) for i in range(2 * CHIPS)])  10.3 us
    pallas_call x5, Pallas kernels, call(): pl.pallas_call(kernel, out_shape=shapes, in_specs=specs, out_specs=jax.tr...  7.63 us
    pallas_call x1, Pallas kernels, down_grad(): pl.pallas_call(down_kernel, out_shape=(jax.ShapeDtypeStruct((SLOT, SLOT),...  4.35 us
    ppermute x5, waiting for transfers between devices, core_swap(): return lax.ppermute(value, 'ctx', [(i, i ^ 1) for i in range(2 * CHIPS)])  4.04 us
  transfers between devices with their start and end apart: 15, of which 12 were waited for; matrix products, arithmetic and copies ran while one was open for 2% of the time, Pallas kernels for 2%

profile of v5, /device:TPU:4, one launch (start us, length us, event | category | flops | bytes accessed | tf_op | source)
XLA Modules:
  0.0 145.7 jit_solution(8504387539646301114)
XLA Ops:
  0.6 0.9 copy-done.1
  1.5 0.7 copy-done.2
  2.2 8.0 %collective-permute-start.1 = (bf16[592,128]{1,0:T(8,128)(2,1)S(1)}, bf16[592,128]{1,0:T(8,128)(2,1)S(1)}, u32[]{:S(2)}, u32[]{:S(2)}) collective-permute-start(bf16[592,128]{1,0:T(8,128)(2,1)S(1)} %pack_keys.1), channel_id=1, source_target_pairs={{0,256},{64,320},{128,384},{192,448},{256,512},{320,576},{384,640}... | collective-permute-start | bytes 454664 | tf_op jit(solution)/shard_map/ppermute | solution.py:36
  10.3 5.2 %collective-permute-start = (bf16[592,128]{1,0:T(8,128)(2,1)S(1)}, bf16[592,128]{1,0:T(8,128)(2,1)S(1)}, u32[]{:S(2)}, u32[]{:S(2)}) collective-permute-start(bf16[592,128]{1,0:T(8,128)(2,1)S(1)} %pack_keys.1), channel_id=1, source_target_pairs={{0,128},{64,192},{128,256},{192,320},{256,384},{320,448},{384,512}... | collective-permute-start | bytes 454664 | tf_op jit(solution)/shard_map/ppermute | solution.py:36
  15.6 11.8 %collective-permute-start.3 = (bf16[592,128]{1,0:T(8,128)(2,1)S(1)}, bf16[592,128]{1,0:T(8,128)(2,1)S(1)}, u32[]{:S(2)}, u32[]{:S(2)}) collective-permute-start(bf16[592,128]{1,0:T(8,128)(2,1)S(1)} %pack_keys.1), channel_id=1, source_target_pairs={{0,512},{64,576},{128,640},{192,704},{256,768},{320,832},{384,896}... | collective-permute-start | bytes 454664 | tf_op jit(solution)/shard_map/ppermute | solution.py:36
  27.4 1.7 %reshape_squeeze.6.query_ref = bf16[512,576]{1,0:T(8,128)(2,1)S(1)} reshape(bf16[1,4,73728]{2,1,0:T(4,128)(2,1)} %param.7) | data formatting | bytes 1179648 | tf_op jit(solution)/shard_map/reshape;squeeze | solution.py:318
  29.6 1.9 %collective-permute-start.2 = (bf16[592,128]{1,0:T(8,128)(2,1)S(1)}, bf16[592,128]{1,0:T(8,128)(2,1)S(1)}, u32[]{:S(2)}, u32[]{:S(2)}) collective-permute-start(bf16[592,128]{1,0:T(8,128)(2,1)S(1)} %collective-permute-done), channel_id=1, source_target_pairs={{0,256},{64,320},{128,384},{192,448},{256,512},{320,576},{384,640}... | collective-permute-start | bytes 454664 | tf_op jit(solution)/shard_map/ppermute | solution.py:36
  32.5 12.5 %collective-permute-done.2 = bf16[592,128]{1,0:T(8,128)(2,1)S(1)} collective-permute-done((bf16[592,128]{1,0:T(8,128)(2,1)S(1)}, bf16[592,128]{1,0:T(8,128)(2,1)S(1)}, u32[]{:S(2)}, u32[]{:S(2)}) %collective-permute-start.2) | collective-permute-done | bytes 151584 | tf_op jit(solution)/shard_map/ppermute | solution.py:36
  45.1 1.9 %collective-permute-start.4 = (bf16[5,592,128]{2,1,0:T(8,128)(2,1)S(1)}, bf16[5,592,128]{2,1,0:T(8,128)(2,1)S(1)}, u32[]{:S(2)}, u32[]{:S(2)}) collective-permute-start(bf16[5,592,128]{2,1,0:T(8,128)(2,1)S(1)} %bitcast_dynamic-update-slice_fusion.own), channel_id=1, source_target_pairs={{0,64},{64,0},{128,192},{192,128},{256,320},{320,256},{384,448},{4... | collective-permute-start | bytes 2273288 | tf_op jit(solution)/shard_map/ppermute | solution.py:40
  47.0 1.3 own_scores.1.own_both
  48.3 0.9 collective-permute-done.4.par
  49.2 4.2 %attention_grads.1 = (bf16[2,592,256]{2,1,0:T(8,128)(2,1)S(1)}, bf16[5,1024,256]{2,1,0:T(8,128)(2,1)S(1)}) custom-call(s32[2]{0:T(128)S(1)} %pad_add_fusion.info, bf16[5,592,128]{2,1,0:T(8,128)(2,1)S(1)} %bitcast_dynamic-update-slice_fusion.own, bf16[5,592,128]{2,1,0:T(8,128)(2,1)S(1)} %collective-permute-done.4.par, ...), custom_call_target="tpu_custom_call" | custom-call | flops 1509949440 | bytes 4194304 | tf_op jit(solution)/shard_map/attention_grads/pallas_call | solution.py:165
  53.4 2.0 %collective-permute-start.5 = (bf16[2,592,256]{2,1,0:T(8,128)(2,1)S(1)}, bf16[2,592,256]{2,1,0:T(8,128)(2,1)S(1)}, u32[]{:S(2)}, u32[]{:S(2)}) collective-permute-start(bf16[2,592,256]{2,1,0:T(8,128)(2,1)S(1)} %get-tuple-element.34), channel_id=1, source_target_pairs={{0,64},{64,0},{128,192},{192,128},{256,320},{320,256},{384,448},{4... | collective-permute-start | bytes 1818632 | tf_op jit(solution)/shard_map/ppermute | solution.py:40
  55.5 1.7 %kept_grads.1 = (bf16[2,592,256]{2,1,0:T(8,128)(2,1)S(1)}, bf16[592,256]{1,0:T(8,128)(2,1)S(1)}) custom-call(s32[2]{0:T(128)S(1)} %pad_add_fusion.info, bf16[5,592,128]{2,1,0:T(8,128)(2,1)S(1)} %bitcast_dynamic-update-slice_fusion.own, bf16[5,592,128]{2,1,0:T(8,128)(2,1)S(1)} %collective-permute-done.4.par, ...), custom_call_target="tpu_custom_call" | custom-call | flops 905969664 | bytes 4194304 | tf_op jit(solution)/shard_map/kept_grads/pallas_call | solution.py:165
  57.5 1.9 %collective-permute-start.6 = (bf16[592,256]{1,0:T(8,128)(2,1)S(1)}, bf16[592,256]{1,0:T(8,128)(2,1)S(1)}, u32[]{:S(2)}, u32[]{:S(2)}) collective-permute-start(bf16[592,256]{1,0:T(8,128)(2,1)S(1)} %get-tuple-element.40), channel_id=1, source_target_pairs={{0,256},{64,832},{128,384},{192,960},{256,512},{320,64},{384,640},... | collective-permute-start | bytes 909320 | tf_op jit(solution)/shard_map/ppermute | solution.py:36
  59.4 3.0 %collective-permute-start.7 = (bf16[592,256]{1,0:T(8,128)(2,1)S(1)}, bf16[592,256]{1,0:T(8,128)(2,1)S(1)}, u32[]{:S(2)}, u32[]{:S(2)}) collective-permute-start(bf16[592,256]{1,0:T(8,128)(2,1)S(1)} %get-tuple-element.41), channel_id=1, source_target_pairs={{0,128},{64,960},{128,256},{192,64},{256,384},{320,192},{384,512},... | collective-permute-start | bytes 909320 | tf_op jit(solution)/shard_map/ppermute | solution.py:36
  62.5 8.8 %collective-permute-done.6 = bf16[592,256]{1,0:T(8,128)(2,1)S(1)} collective-permute-done((bf16[592,256]{1,0:T(8,128)(2,1)S(1)}, bf16[592,256]{1,0:T(8,128)(2,1)S(1)}, u32[]{:S(2)}, u32[]{:S(2)}) %collective-permute-start.6) | collective-permute-done | bytes 303136 | tf_op jit(solution)/shard_map/ppermute | solution.py:36
  71.3 1.2 collective-permute-done.7
  72.7 2.1 %collective-permute-start.8 = (bf16[592,256]{1,0:T(8,128)(2,1)S(1)}, bf16[592,256]{1,0:T(8,128)(2,1)S(1)}, u32[]{:S(2)}, u32[]{:S(2)}) collective-permute-start(bf16[592,256]{1,0:T(8,128)(2,1)S(1)} %add_convert_fusion.1), channel_id=1, source_target_pairs={{0,64},{64,0},{128,192},{192,128},{256,320},{320,256},{384,448},{4... | collective-permute-start | bytes 909320 | tf_op jit(solution)/shard_map/ppermute | solution.py:40
  74.7 1.6 %collective-permute-done.8 = bf16[592,256]{1,0:T(8,128)(2,1)S(1)} collective-permute-done((bf16[592,256]{1,0:T(8,128)(2,1)S(1)}, bf16[592,256]{1,0:T(8,128)(2,1)S(1)}, u32[]{:S(2)}, u32[]{:S(2)}) %collective-permute-start.8) | collective-permute-done | bytes 303136 | tf_op jit(solution)/shard_map/ppermute | solution.py:40
  76.4 2.2 %collective-permute-start.9 = (bf16[592,256]{1,0:T(8,128)(2,1)S(1)}, bf16[592,256]{1,0:T(8,128)(2,1)S(1)}, u32[]{:S(2)}, u32[]{:S(2)}) collective-permute-start(bf16[592,256]{1,0:T(8,128)(2,1)S(1)} %add_convert_fusion.g0), channel_id=1, source_target_pairs={{0,128},{64,960},{128,256},{192,64},{256,384},{320,192},{384,512},... | collective-permute-start | bytes 909320 | tf_op jit(solution)/shard_map/ppermute | solution.py:36
  78.6 5.1 %collective-permute-start.10 = (bf16[592,256]{1,0:T(8,128)(2,1)S(1)}, bf16[592,256]{1,0:T(8,128)(2,1)S(1)}, u32[]{:S(2)}, u32[]{:S(2)}) collective-permute-start(bf16[592,256]{1,0:T(8,128)(2,1)S(1)} %add_convert_fusion.g0), channel_id=1, source_target_pairs={{0,256},{64,832},{128,384},{192,960},{256,512},{320,64},{384,640},... | collective-permute-start | bytes 909320 | tf_op jit(solution)/shard_map/ppermute | solution.py:36
  83.6 2.6 %collective-permute-done.9 = bf16[592,256]{1,0:T(8,128)(2,1)S(1)} collective-permute-done((bf16[592,256]{1,0:T(8,128)(2,1)S(1)}, bf16[592,256]{1,0:T(8,128)(2,1)S(1)}, u32[]{:S(2)}, u32[]{:S(2)}) %collective-permute-start.9) | collective-permute-done | bytes 303136 | tf_op jit(solution)/shard_map/ppermute | solution.py:36
  86.3 2.9 %collective-permute-start.11 = (bf16[592,256]{1,0:T(8,128)(2,1)S(1)}, bf16[592,256]{1,0:T(8,128)(2,1)S(1)}, u32[]{:S(2)}, u32[]{:S(2)}) collective-permute-start(bf16[592,256]{1,0:T(8,128)(2,1)S(1)} %collective-permute-done.9), channel_id=1, source_target_pairs={{0,256},{64,832},{128,384},{192,960},{256,512},{320,64},{384,640},... | collective-permute-start | bytes 909320 | tf_op jit(solution)/shard_map/ppermute | solution.py:36
  89.2 2.8 %collective-permute-done.10 = bf16[592,256]{1,0:T(8,128)(2,1)S(1)} collective-permute-done((bf16[592,256]{1,0:T(8,128)(2,1)S(1)}, bf16[592,256]{1,0:T(8,128)(2,1)S(1)}, u32[]{:S(2)}, u32[]{:S(2)}) %collective-permute-start.10) | collective-permute-done | bytes 303136 | tf_op jit(solution)/shard_map/ppermute | solution.py:36
  92.0 4.7 %collective-permute-start.12 = (bf16[592,128]{1,0:T(8,128)(2,1)S(1)}, bf16[592,128]{1,0:T(8,128)(2,1)S(1)}, u32[]{:S(2)}, u32[]{:S(2)}) collective-permute-start(bf16[592,128]{1,0:T(8,128)(2,1)S(1)} %slice_select_fusion), channel_id=1, source_target_pairs={{0,256},{64,832},{128,384},{192,960},{256,512},{320,64},{384,640},... | collective-permute-start | bytes 454664 | tf_op jit(solution)/shard_map/ppermute | solution.py:36
  96.7 4.5 %collective-permute-done.11 = bf16[592,256]{1,0:T(8,128)(2,1)S(1)} collective-permute-done((bf16[592,256]{1,0:T(8,128)(2,1)S(1)}, bf16[592,256]{1,0:T(8,128)(2,1)S(1)}, u32[]{:S(2)}, u32[]{:S(2)}) %collective-permute-start.11) | collective-permute-done | bytes 303136 | tf_op jit(solution)/shard_map/ppermute | solution.py:36
  101.3 1.9 %collective-permute-start.13 = (bf16[2,592,256]{2,1,0:T(8,128)(2,1)S(1)}, bf16[2,592,256]{2,1,0:T(8,128)(2,1)S(1)}, u32[]{:S(2)}, u32[]{:S(2)}) collective-permute-start(bf16[2,592,256]{2,1,0:T(8,128)(2,1)S(1)} %pad_maximum_fusion.r12), channel_id=1, source_target_pairs={{0,64},{64,0},{128,192},{192,128},{256,320},{320,256},{384,448},{4... | collective-permute-start | bytes 1818632 | tf_op jit(solution)/shard_map/ppermute | solution.py:40
  103.4 2.3 %collective-permute-start.14 = (bf16[592,384]{1,0:T(8,128)(2,1)S(1)}, bf16[592,384]{1,0:T(8,128)(2,1)S(1)}, u32[]{:S(2)}, u32[]{:S(2)}) collective-permute-start(bf16[592,384]{1,0:T(8,128)(2,1)S(1)} %constant_dynamic-update-slice_fusion.r34), channel_id=1, source_target_pairs={{0,64},{64,0},{128,192},{192,128},{256,320},{320,256},{384,448},{4... | collective-permute-start | bytes 1363976 | tf_op jit(solution)/shard_map/ppermute | solution.py:40
  105.7 1.4 collective-permute-done.14.s34
  107.1 4.4 %down_grad.1 = (bf16[512,512]{1,0:T(8,128)(2,1)S(1)}, bf16[576,128]{1,0:T(8,128)(2,1)}) custom-call(s32[2]{0:T(128)S(1)} %pad_add_fusion.info, f32[1,8]{1,0:T(1,128)S(1)} %copy-done.3, bf16[592,256]{1,0:T(8,128)(2,1)S(1)} %add_convert_fusion.g0, bf16[2,592,256]{2,1,0:T(8,128)(2,1)S(1)} %pad_maximum_fusion.r12, ...), custom_call_target="tpu_custom_call" | custom-call | tf_op jit(solution)/shard_map/down_grad/pallas_call | solution.py:286
  111.5 33.3 %all_to_all.5 = bf16[64,8,512]{2,1,0:T(8,128)(2,1)S(1)} all-to-all(bf16[64,8,512]{2,1,0:T(8,128)(2,1)S(1)} %bitcast.30), channel_id=1, replica_groups=mesh['ctx'=16,'grp'=64] {'grp'}, dimensions={0} | all-to-all | bytes 1048576 | tf_op jit(solution)/shard_map/all_to_all | solution.py:355
  (34 shorter events, 3.2 us)
Async XLA Ops:
  0.6 0.9 copy-start.1
  1.5 0.7 copy-start.2
  2.2 29.4 %copy-start.4 = (bf16[1,4,65536]{2,1,0:T(4,128)(2,1)S(1)}, bf16[1,4,65536]{2,1,0:T(4,128)(2,1)}, u32[]{:S(2)}) copy-start(bf16[1,4,65536]{2,1,0:T(4,128)(2,1)} %param.8) | copy-start | bytes 1572868
  2.2 30.2 %collective-permute-start.1 = (bf16[592,128]{1,0:T(8,128)(2,1)S(1)}, bf16[592,128]{1,0:T(8,128)(2,1)S(1)}, u32[]{:S(2)}, u32[]{:S(2)}) collective-permute-start(bf16[592,128]{1,0:T(8,128)(2,1)S(1)} %pack_keys.1), channel_id=1, source_target_pairs={{0,256},{64,320},{128,384},{192,448},{256,512},{320,576},{384,640}... | collective-permute-start | bytes 454664 | tf_op jit(solution)/shard_map/ppermute | solution.py:36
  10.3 19.4 %collective-permute-start = (bf16[592,128]{1,0:T(8,128)(2,1)S(1)}, bf16[592,128]{1,0:T(8,128)(2,1)S(1)}, u32[]{:S(2)}, u32[]{:S(2)}) collective-permute-start(bf16[592,128]{1,0:T(8,128)(2,1)S(1)} %pack_keys.1), channel_id=1, source_target_pairs={{0,128},{64,192},{128,256},{192,320},{256,384},{320,448},{384,512}... | collective-permute-start | bytes 454664 | tf_op jit(solution)/shard_map/ppermute | solution.py:36
  15.6 29.5 %collective-permute-start.3 = (bf16[592,128]{1,0:T(8,128)(2,1)S(1)}, bf16[592,128]{1,0:T(8,128)(2,1)S(1)}, u32[]{:S(2)}, u32[]{:S(2)}) collective-permute-start(bf16[592,128]{1,0:T(8,128)(2,1)S(1)} %pack_keys.1), channel_id=1, source_target_pairs={{0,512},{64,576},{128,640},{192,704},{256,768},{320,832},{384,896}... | collective-permute-start | bytes 454664 | tf_op jit(solution)/shard_map/ppermute | solution.py:36
  29.6 15.4 %collective-permute-start.2 = (bf16[592,128]{1,0:T(8,128)(2,1)S(1)}, bf16[592,128]{1,0:T(8,128)(2,1)S(1)}, u32[]{:S(2)}, u32[]{:S(2)}) collective-permute-start(bf16[592,128]{1,0:T(8,128)(2,1)S(1)} %collective-permute-done), channel_id=1, source_target_pairs={{0,256},{64,320},{128,384},{192,448},{256,512},{320,576},{384,640}... | collective-permute-start | bytes 454664 | tf_op jit(solution)/shard_map/ppermute | solution.py:36
  45.1 4.1 %collective-permute-start.4 = (bf16[5,592,128]{2,1,0:T(8,128)(2,1)S(1)}, bf16[5,592,128]{2,1,0:T(8,128)(2,1)S(1)}, u32[]{:S(2)}, u32[]{:S(2)}) collective-permute-start(bf16[5,592,128]{2,1,0:T(8,128)(2,1)S(1)} %bitcast_dynamic-update-slice_fusion.own), channel_id=1, source_target_pairs={{0,64},{64,0},{128,192},{192,128},{256,320},{320,256},{384,448},{4... | collective-permute-start | bytes 2273288 | tf_op jit(solution)/shard_map/ppermute | solution.py:40
  53.4 3.9 %collective-permute-start.5 = (bf16[2,592,256]{2,1,0:T(8,128)(2,1)S(1)}, bf16[2,592,256]{2,1,0:T(8,128)(2,1)S(1)}, u32[]{:S(2)}, u32[]{:S(2)}) collective-permute-start(bf16[2,592,256]{2,1,0:T(8,128)(2,1)S(1)} %get-tuple-element.34), channel_id=1, source_target_pairs={{0,64},{64,0},{128,192},{192,128},{256,320},{320,256},{384,448},{4... | collective-permute-start | bytes 1818632 | tf_op jit(solution)/shard_map/ppermute | solution.py:40
  57.5 13.8 %collective-permute-start.6 = (bf16[592,256]{1,0:T(8,128)(2,1)S(1)}, bf16[592,256]{1,0:T(8,128)(2,1)S(1)}, u32[]{:S(2)}, u32[]{:S(2)}) collective-permute-start(bf16[592,256]{1,0:T(8,128)(2,1)S(1)} %get-tuple-element.40), channel_id=1, source_target_pairs={{0,256},{64,832},{128,384},{192,960},{256,512},{320,64},{384,640},... | collective-permute-start | bytes 909320 | tf_op jit(solution)/shard_map/ppermute | solution.py:36
  59.4 13.1 %collective-permute-start.7 = (bf16[592,256]{1,0:T(8,128)(2,1)S(1)}, bf16[592,256]{1,0:T(8,128)(2,1)S(1)}, u32[]{:S(2)}, u32[]{:S(2)}) collective-permute-start(bf16[592,256]{1,0:T(8,128)(2,1)S(1)} %get-tuple-element.41), channel_id=1, source_target_pairs={{0,128},{64,960},{128,256},{192,64},{256,384},{320,192},{384,512},... | collective-permute-start | bytes 909320 | tf_op jit(solution)/shard_map/ppermute | solution.py:36
  72.6 34.5 %copy-start = (bf16[1,2048,448]{1,2,0:T(8,128)(2,1)S(1)}, bf16[1,2048,448]{1,2,0:T(8,128)(2,1)}, u32[]{:S(2)}) copy-start(bf16[1,2048,448]{1,2,0:T(8,128)(2,1)} %param.9) | copy-start | bytes 5505028
  72.7 34.5 %copy-start.3 = (f32[1,8]{1,0:T(1,128)S(1)}, f32[1,8]{1,0:T(1,128)}, u32[]{:S(2)}) copy-start(f32[1,8]{1,0:T(1,128)} %limits.1) | copy-start | bytes 100
  72.7 3.6 %collective-permute-start.8 = (bf16[592,256]{1,0:T(8,128)(2,1)S(1)}, bf16[592,256]{1,0:T(8,128)(2,1)S(1)}, u32[]{:S(2)}, u32[]{:S(2)}) collective-permute-start(bf16[592,256]{1,0:T(8,128)(2,1)S(1)} %add_convert_fusion.1), channel_id=1, source_target_pairs={{0,64},{64,0},{128,192},{192,128},{256,320},{320,256},{384,448},{4... | collective-permute-start | bytes 909320 | tf_op jit(solution)/shard_map/ppermute | solution.py:40
  76.4 9.9 %collective-permute-start.9 = (bf16[592,256]{1,0:T(8,128)(2,1)S(1)}, bf16[592,256]{1,0:T(8,128)(2,1)S(1)}, u32[]{:S(2)}, u32[]{:S(2)}) collective-permute-start(bf16[592,256]{1,0:T(8,128)(2,1)S(1)} %add_convert_fusion.g0), channel_id=1, source_target_pairs={{0,128},{64,960},{128,256},{192,64},{256,384},{320,192},{384,512},... | collective-permute-start | bytes 909320 | tf_op jit(solution)/shard_map/ppermute | solution.py:36
  78.6 13.4 %collective-permute-start.10 = (bf16[592,256]{1,0:T(8,128)(2,1)S(1)}, bf16[592,256]{1,0:T(8,128)(2,1)S(1)}, u32[]{:S(2)}, u32[]{:S(2)}) collective-permute-start(bf16[592,256]{1,0:T(8,128)(2,1)S(1)} %add_convert_fusion.g0), channel_id=1, source_target_pairs={{0,256},{64,832},{128,384},{192,960},{256,512},{320,64},{384,640},... | collective-permute-start | bytes 909320 | tf_op jit(solution)/shard_map/ppermute | solution.py:36
  86.3 14.9 %collective-permute-start.11 = (bf16[592,256]{1,0:T(8,128)(2,1)S(1)}, bf16[592,256]{1,0:T(8,128)(2,1)S(1)}, u32[]{:S(2)}, u32[]{:S(2)}) collective-permute-start(bf16[592,256]{1,0:T(8,128)(2,1)S(1)} %collective-permute-done.9), channel_id=1, source_target_pairs={{0,256},{64,832},{128,384},{192,960},{256,512},{320,64},{384,640},... | collective-permute-start | bytes 909320 | tf_op jit(solution)/shard_map/ppermute | solution.py:36
  92.0 11.3 %collective-permute-start.12 = (bf16[592,128]{1,0:T(8,128)(2,1)S(1)}, bf16[592,128]{1,0:T(8,128)(2,1)S(1)}, u32[]{:S(2)}, u32[]{:S(2)}) collective-permute-start(bf16[592,128]{1,0:T(8,128)(2,1)S(1)} %slice_select_fusion), channel_id=1, source_target_pairs={{0,256},{64,832},{128,384},{192,960},{256,512},{320,64},{384,640},... | collective-permute-start | bytes 454664 | tf_op jit(solution)/shard_map/ppermute | solution.py:36
  101.3 5.8 %collective-permute-start.13 = (bf16[2,592,256]{2,1,0:T(8,128)(2,1)S(1)}, bf16[2,592,256]{2,1,0:T(8,128)(2,1)S(1)}, u32[]{:S(2)}, u32[]{:S(2)}) collective-permute-start(bf16[2,592,256]{2,1,0:T(8,128)(2,1)S(1)} %pad_maximum_fusion.r12), channel_id=1, source_target_pairs={{0,64},{64,0},{128,192},{192,128},{256,320},{320,256},{384,448},{4... | collective-permute-start | bytes 1818632 | tf_op jit(solution)/shard_map/ppermute | solution.py:40
  103.4 3.7 %collective-permute-start.14 = (bf16[592,384]{1,0:T(8,128)(2,1)S(1)}, bf16[592,384]{1,0:T(8,128)(2,1)S(1)}, u32[]{:S(2)}, u32[]{:S(2)}) collective-permute-start(bf16[592,384]{1,0:T(8,128)(2,1)S(1)} %constant_dynamic-update-slice_fusion.r34), channel_id=1, source_target_pairs={{0,64},{64,0},{128,192},{192,128},{256,320},{320,256},{384,448},{4... | collective-permute-start | bytes 1363976 | tf_op jit(solution)/shard_map/ppermute | solution.py:40

commit v6 on v5

--- a/solution.py
+++ b/solution.py
@@ -316,12 +316,12 @@
     near = chip_shift(keys, 1, 1)
     next_near = chip_shift(keys, 2, 2)
     query_rows = queries[0].reshape(QH, KW)
+    third = chip_shift(keys, 3, 3)
     far_keys, info = lax.optimization_barrier((keys, info))
     fourth = chip_shift(far_keys, 4, 4)
     near, grads = lax.optimization_barrier((near, out_grad))
     grad_rows = grads[0].reshape(QH, LATENT)
     rows, cols = query_views(query_rows, grad_rows)
-    third = chip_shift(near, 2, 2)
     own = jnp.stack([keys, near, next_near, third, fourth])
     own, rows, cols, info = lax.optimization_barrier((own, rows, cols, info))
     par = core_swap(own)

time: 146 us -> 150 us (1.027)
  waiting for transfers between devices: 37.1 us -> 46.1 us
  starting transfers between devices: 57.1 us -> 51.7 us
    ppermute x10, waiting for transfers between devices: 33 us -> 42 us  [chip_shift(): return lax.ppermute(value, 'ctx', pairs)]
    ppermute x10, starting transfers between devices: 46.8 us -> 41.4 us  [chip_shift(): return lax.ppermute(value, 'ctx', pairs)]
  transfers between devices with their start and end apart: 15 -> 15, of which waited for: 12 -> 10; matrix products, arithmetic and copies ran while one was open for 2% -> 2% of each run, Pallas kernels for 2% -> 2%
where the time goes in v6:
time: 150 us; the launch traced here: 149 us
  starting transfers between devices  51.7 us (34%)
  waiting for transfers between devices  46.1 us (31%)
  blocking collectives  33.3 us (22%)
  Pallas kernels  12 us (8%)
  local copies, waits for them, and re-layouts  4.04 us (3%)
    ppermute x10, waiting for transfers between devices, chip_shift(): return lax.ppermute(value, 'ctx', pairs)  42 us
    ppermute x10, starting transfers between devices, chip_shift(): return lax.ppermute(value, 'ctx', pairs)  41.4 us
    all_to_all x1, blocking collectives, on_device(): chunks = lax.all_to_all(chunks, 'grp', 0, 0, tiled=True)  33.3 us
    ppermute x5, starting transfers between devices, core_swap(): return lax.ppermute(value, 'ctx', [(i, i ^ 1) for i in range(2 * CHIPS)])  10.3 us
    pallas_call x5, Pallas kernels, call(): pl.pallas_call(kernel, out_shape=shapes, in_specs=specs, out_specs=jax.tr...  7.63 us
    pallas_call x1, Pallas kernels, down_grad(): pl.pallas_call(down_kernel, out_shape=(jax.ShapeDtypeStruct((SLOT, SLOT),...  4.35 us
    ppermute x5, waiting for transfers between devices, core_swap(): return lax.ppermute(value, 'ctx', [(i, i ^ 1) for i in range(2 * CHIPS)])  4.05 us
  transfers between devices with their start and end apart: 15, of which 10 were waited for; matrix products, arithmetic and copies ran while one was open for 2% of the time, Pallas kernels for 2%

profile of v6, /device:TPU:4, one launch (start us, length us, event | category | flops | bytes accessed | tf_op | source)
XLA Modules:
  0.0 149.3 jit_solution(4997077330411490499)
XLA Ops:
  0.6 0.9 copy-done.1
  1.5 0.7 copy-done.2
  2.2 10.8 %collective-permute-start.2 = (bf16[592,128]{1,0:T(8,128)(2,1)S(1)}, bf16[592,128]{1,0:T(8,128)(2,1)S(1)}, u32[]{:S(2)}, u32[]{:S(2)}) collective-permute-start(bf16[592,128]{1,0:T(8,128)(2,1)S(1)} %pack_keys.1), channel_id=1, source_target_pairs={{0,384},{64,448},{128,512},{192,576},{256,640},{320,704},{384,768}... | collective-permute-start | bytes 454664 | tf_op jit(solution)/shard_map/ppermute | solution.py:36
  13.0 8.2 %collective-permute-start.1 = (bf16[592,128]{1,0:T(8,128)(2,1)S(1)}, bf16[592,128]{1,0:T(8,128)(2,1)S(1)}, u32[]{:S(2)}, u32[]{:S(2)}) collective-permute-start(bf16[592,128]{1,0:T(8,128)(2,1)S(1)} %pack_keys.1), channel_id=1, source_target_pairs={{0,256},{64,320},{128,384},{192,448},{256,512},{320,576},{384,640}... | collective-permute-start | bytes 454664 | tf_op jit(solution)/shard_map/ppermute | solution.py:36
  21.2 4.3 %collective-permute-start = (bf16[592,128]{1,0:T(8,128)(2,1)S(1)}, bf16[592,128]{1,0:T(8,128)(2,1)S(1)}, u32[]{:S(2)}, u32[]{:S(2)}) collective-permute-start(bf16[592,128]{1,0:T(8,128)(2,1)S(1)} %pack_keys.1), channel_id=1, source_target_pairs={{0,128},{64,192},{128,256},{192,320},{256,384},{320,448},{384,512}... | collective-permute-start | bytes 454664 | tf_op jit(solution)/shard_map/ppermute | solution.py:36
  25.6 3.7 %collective-permute-start.3 = (bf16[592,128]{1,0:T(8,128)(2,1)S(1)}, bf16[592,128]{1,0:T(8,128)(2,1)S(1)}, u32[]{:S(2)}, u32[]{:S(2)}) collective-permute-start(bf16[592,128]{1,0:T(8,128)(2,1)S(1)} %pack_keys.1), channel_id=1, source_target_pairs={{0,512},{64,576},{128,640},{192,704},{256,768},{320,832},{384,896}... | collective-permute-start | bytes 454664 | tf_op jit(solution)/shard_map/ppermute | solution.py:36
  29.3 1.7 %reshape_squeeze.6.query_ref = bf16[512,576]{1,0:T(8,128)(2,1)S(1)} reshape(bf16[1,4,73728]{2,1,0:T(4,128)(2,1)} %param.7) | data formatting | bytes 1179648 | tf_op jit(solution)/shard_map/reshape;squeeze | solution.py:318
  31.1 7.0 %collective-permute-done = bf16[592,128]{1,0:T(8,128)(2,1)S(1)} collective-permute-done((bf16[592,128]{1,0:T(8,128)(2,1)S(1)}, bf16[592,128]{1,0:T(8,128)(2,1)S(1)}, u32[]{:S(2)}, u32[]{:S(2)}) %collective-permute-start) | collective-permute-done | bytes 151584 | tf_op jit(solution)/shard_map/ppermute | solution.py:36
  39.1 10.2 %collective-permute-done.3 = bf16[592,128]{1,0:T(8,128)(2,1)S(1)} collective-permute-done((bf16[592,128]{1,0:T(8,128)(2,1)S(1)}, bf16[592,128]{1,0:T(8,128)(2,1)S(1)}, u32[]{:S(2)}, u32[]{:S(2)}) %collective-permute-start.3) | collective-permute-done | bytes 151584 | tf_op jit(solution)/shard_map/ppermute | solution.py:36
  49.3 1.9 %collective-permute-start.4 = (bf16[5,592,128]{2,1,0:T(8,128)(2,1)S(1)}, bf16[5,592,128]{2,1,0:T(8,128)(2,1)S(1)}, u32[]{:S(2)}, u32[]{:S(2)}) collective-permute-start(bf16[5,592,128]{2,1,0:T(8,128)(2,1)S(1)} %bitcast_dynamic-update-slice_fusion.own), channel_id=1, source_target_pairs={{0,64},{64,0},{128,192},{192,128},{256,320},{320,256},{384,448},{4... | collective-permute-start | bytes 2273288 | tf_op jit(solution)/shard_map/ppermute | solution.py:40
  51.2 1.3 own_scores.1.own_both
  52.6 0.9 collective-permute-done.4.par
  53.4 4.2 %attention_grads.1 = (bf16[2,592,256]{2,1,0:T(8,128)(2,1)S(1)}, bf16[5,1024,256]{2,1,0:T(8,128)(2,1)S(1)}) custom-call(s32[2]{0:T(128)S(1)} %pad_add_fusion.info, bf16[5,592,128]{2,1,0:T(8,128)(2,1)S(1)} %bitcast_dynamic-update-slice_fusion.own, bf16[5,592,128]{2,1,0:T(8,128)(2,1)S(1)} %collective-permute-done.4.par, ...), custom_call_target="tpu_custom_call" | custom-call | flops 1509949440 | bytes 4194304 | tf_op jit(solution)/shard_map/attention_grads/pallas_call | solution.py:165
  57.6 2.0 %collective-permute-start.5 = (bf16[2,592,256]{2,1,0:T(8,128)(2,1)S(1)}, bf16[2,592,256]{2,1,0:T(8,128)(2,1)S(1)}, u32[]{:S(2)}, u32[]{:S(2)}) collective-permute-start(bf16[2,592,256]{2,1,0:T(8,128)(2,1)S(1)} %get-tuple-element.34), channel_id=1, source_target_pairs={{0,64},{64,0},{128,192},{192,128},{256,320},{320,256},{384,448},{4... | collective-permute-start | bytes 1818632 | tf_op jit(solution)/shard_map/ppermute | solution.py:40
  59.7 1.7 %kept_grads.1 = (bf16[2,592,256]{2,1,0:T(8,128)(2,1)S(1)}, bf16[592,256]{1,0:T(8,128)(2,1)S(1)}) custom-call(s32[2]{0:T(128)S(1)} %pad_add_fusion.info, bf16[5,592,128]{2,1,0:T(8,128)(2,1)S(1)} %bitcast_dynamic-update-slice_fusion.own, bf16[5,592,128]{2,1,0:T(8,128)(2,1)S(1)} %collective-permute-done.4.par, ...), custom_call_target="tpu_custom_call" | custom-call | flops 905969664 | bytes 4194304 | tf_op jit(solution)/shard_map/kept_grads/pallas_call | solution.py:165
  61.7 1.9 %collective-permute-start.6 = (bf16[592,256]{1,0:T(8,128)(2,1)S(1)}, bf16[592,256]{1,0:T(8,128)(2,1)S(1)}, u32[]{:S(2)}, u32[]{:S(2)}) collective-permute-start(bf16[592,256]{1,0:T(8,128)(2,1)S(1)} %get-tuple-element.40), channel_id=1, source_target_pairs={{0,256},{64,832},{128,384},{192,960},{256,512},{320,64},{384,640},... | collective-permute-start | bytes 909320 | tf_op jit(solution)/shard_map/ppermute | solution.py:36
  63.7 1.9 %collective-permute-start.7 = (bf16[592,256]{1,0:T(8,128)(2,1)S(1)}, bf16[592,256]{1,0:T(8,128)(2,1)S(1)}, u32[]{:S(2)}, u32[]{:S(2)}) collective-permute-start(bf16[592,256]{1,0:T(8,128)(2,1)S(1)} %get-tuple-element.41), channel_id=1, source_target_pairs={{0,128},{64,960},{128,256},{192,64},{256,384},{320,192},{384,512},... | collective-permute-start | bytes 909320 | tf_op jit(solution)/shard_map/ppermute | solution.py:36
  65.6 7.9 %collective-permute-done.6 = bf16[592,256]{1,0:T(8,128)(2,1)S(1)} collective-permute-done((bf16[592,256]{1,0:T(8,128)(2,1)S(1)}, bf16[592,256]{1,0:T(8,128)(2,1)S(1)}, u32[]{:S(2)}, u32[]{:S(2)}) %collective-permute-start.6) | collective-permute-done | bytes 303136 | tf_op jit(solution)/shard_map/ppermute | solution.py:36
  73.5 2.6 %collective-permute-done.7 = bf16[592,256]{1,0:T(8,128)(2,1)S(1)} collective-permute-done((bf16[592,256]{1,0:T(8,128)(2,1)S(1)}, bf16[592,256]{1,0:T(8,128)(2,1)S(1)}, u32[]{:S(2)}, u32[]{:S(2)}) %collective-permute-start.7) | collective-permute-done | bytes 303136 | tf_op jit(solution)/shard_map/ppermute | solution.py:36
  76.2 2.1 %collective-permute-start.8 = (bf16[592,256]{1,0:T(8,128)(2,1)S(1)}, bf16[592,256]{1,0:T(8,128)(2,1)S(1)}, u32[]{:S(2)}, u32[]{:S(2)}) collective-permute-start(bf16[592,256]{1,0:T(8,128)(2,1)S(1)} %add_convert_fusion.1), channel_id=1, source_target_pairs={{0,64},{64,0},{128,192},{192,128},{256,320},{320,256},{384,448},{4... | collective-permute-start | bytes 909320 | tf_op jit(solution)/shard_map/ppermute | solution.py:40
  78.3 1.6 %collective-permute-done.8 = bf16[592,256]{1,0:T(8,128)(2,1)S(1)} collective-permute-done((bf16[592,256]{1,0:T(8,128)(2,1)S(1)}, bf16[592,256]{1,0:T(8,128)(2,1)S(1)}, u32[]{:S(2)}, u32[]{:S(2)}) %collective-permute-start.8) | collective-permute-done | bytes 303136 | tf_op jit(solution)/shard_map/ppermute | solution.py:40
  79.9 1.9 %collective-permute-start.9 = (bf16[592,256]{1,0:T(8,128)(2,1)S(1)}, bf16[592,256]{1,0:T(8,128)(2,1)S(1)}, u32[]{:S(2)}, u32[]{:S(2)}) collective-permute-start(bf16[592,256]{1,0:T(8,128)(2,1)S(1)} %add_convert_fusion.g0), channel_id=1, source_target_pairs={{0,128},{64,960},{128,256},{192,64},{256,384},{320,192},{384,512},... | collective-permute-start | bytes 909320 | tf_op jit(solution)/shard_map/ppermute | solution.py:36
  81.9 1.9 %collective-permute-start.10 = (bf16[592,256]{1,0:T(8,128)(2,1)S(1)}, bf16[592,256]{1,0:T(8,128)(2,1)S(1)}, u32[]{:S(2)}, u32[]{:S(2)}) collective-permute-start(bf16[592,256]{1,0:T(8,128)(2,1)S(1)} %add_convert_fusion.g0), channel_id=1, source_target_pairs={{0,256},{64,832},{128,384},{192,960},{256,512},{320,64},{384,640},... | collective-permute-start | bytes 909320 | tf_op jit(solution)/shard_map/ppermute | solution.py:36
  83.8 9.3 %collective-permute-done.9 = bf16[592,256]{1,0:T(8,128)(2,1)S(1)} collective-permute-done((bf16[592,256]{1,0:T(8,128)(2,1)S(1)}, bf16[592,256]{1,0:T(8,128)(2,1)S(1)}, u32[]{:S(2)}, u32[]{:S(2)}) %collective-permute-start.9) | collective-permute-done | bytes 303136 | tf_op jit(solution)/shard_map/ppermute | solution.py:36
  93.1 1.9 %collective-permute-start.11 = (bf16[592,256]{1,0:T(8,128)(2,1)S(1)}, bf16[592,256]{1,0:T(8,128)(2,1)S(1)}, u32[]{:S(2)}, u32[]{:S(2)}) collective-permute-start(bf16[592,256]{1,0:T(8,128)(2,1)S(1)} %collective-permute-done.9), channel_id=1, source_target_pairs={{0,256},{64,832},{128,384},{192,960},{256,512},{320,64},{384,640},... | collective-permute-start | bytes 909320 | tf_op jit(solution)/shard_map/ppermute | solution.py:36
  95.1 4.8 %collective-permute-start.12 = (bf16[592,128]{1,0:T(8,128)(2,1)S(1)}, bf16[592,128]{1,0:T(8,128)(2,1)S(1)}, u32[]{:S(2)}, u32[]{:S(2)}) collective-permute-start(bf16[592,128]{1,0:T(8,128)(2,1)S(1)} %slice_select_fusion), channel_id=1, source_target_pairs={{0,256},{64,832},{128,384},{192,960},{256,512},{320,64},{384,640},... | collective-permute-start | bytes 454664 | tf_op jit(solution)/shard_map/ppermute | solution.py:36
  99.8 5.0 %collective-permute-done.11 = bf16[592,256]{1,0:T(8,128)(2,1)S(1)} collective-permute-done((bf16[592,256]{1,0:T(8,128)(2,1)S(1)}, bf16[592,256]{1,0:T(8,128)(2,1)S(1)}, u32[]{:S(2)}, u32[]{:S(2)}) %collective-permute-start.11) | collective-permute-done | bytes 303136 | tf_op jit(solution)/shard_map/ppermute | solution.py:36
  105.0 1.9 %collective-permute-start.13 = (bf16[2,592,256]{2,1,0:T(8,128)(2,1)S(1)}, bf16[2,592,256]{2,1,0:T(8,128)(2,1)S(1)}, u32[]{:S(2)}, u32[]{:S(2)}) collective-permute-start(bf16[2,592,256]{2,1,0:T(8,128)(2,1)S(1)} %pad_maximum_fusion.r12), channel_id=1, source_target_pairs={{0,64},{64,0},{128,192},{192,128},{256,320},{320,256},{384,448},{4... | collective-permute-start | bytes 1818632 | tf_op jit(solution)/shard_map/ppermute | solution.py:40
  107.0 2.4 %collective-permute-start.14 = (bf16[592,384]{1,0:T(8,128)(2,1)S(1)}, bf16[592,384]{1,0:T(8,128)(2,1)S(1)}, u32[]{:S(2)}, u32[]{:S(2)}) collective-permute-start(bf16[592,384]{1,0:T(8,128)(2,1)S(1)} %constant_dynamic-update-slice_fusion.r34), channel_id=1, source_target_pairs={{0,64},{64,0},{128,192},{192,128},{256,320},{320,256},{384,448},{4... | collective-permute-start | bytes 1363976 | tf_op jit(solution)/shard_map/ppermute | solution.py:40
  109.4 1.4 collective-permute-done.14.s34
  110.8 4.4 %down_grad.1 = (bf16[512,512]{1,0:T(8,128)(2,1)S(1)}, bf16[576,128]{1,0:T(8,128)(2,1)}) custom-call(s32[2]{0:T(128)S(1)} %pad_add_fusion.info, f32[1,8]{1,0:T(1,128)S(1)} %copy-done.3, bf16[592,256]{1,0:T(8,128)(2,1)S(1)} %add_convert_fusion.g0, bf16[2,592,256]{2,1,0:T(8,128)(2,1)S(1)} %pad_maximum_fusion.r12, ...), custom_call_target="tpu_custom_call" | custom-call | tf_op jit(solution)/shard_map/down_grad/pallas_call | solution.py:286
  115.2 33.3 %all_to_all.5 = bf16[64,8,512]{2,1,0:T(8,128)(2,1)S(1)} all-to-all(bf16[64,8,512]{2,1,0:T(8,128)(2,1)S(1)} %bitcast.30), channel_id=1, replica_groups=mesh['ctx'=16,'grp'=64] {'grp'}, dimensions={0} | all-to-all | bytes 1048576 | tf_op jit(solution)/shard_map/all_to_all | solution.py:355
  (34 shorter events, 2.7 us)
Async XLA Ops:
  0.6 0.9 copy-start.1
  1.5 0.7 copy-start.2
  2.2 35.9 %copy-start.4 = (bf16[1,4,65536]{2,1,0:T(4,128)(2,1)S(1)}, bf16[1,4,65536]{2,1,0:T(4,128)(2,1)}, u32[]{:S(2)}) copy-start(bf16[1,4,65536]{2,1,0:T(4,128)(2,1)} %param.8) | copy-start | bytes 1572868
  2.2 36.9 %collective-permute-start.2 = (bf16[592,128]{1,0:T(8,128)(2,1)S(1)}, bf16[592,128]{1,0:T(8,128)(2,1)S(1)}, u32[]{:S(2)}, u32[]{:S(2)}) collective-permute-start(bf16[592,128]{1,0:T(8,128)(2,1)S(1)} %pack_keys.1), channel_id=1, source_target_pairs={{0,384},{64,448},{128,512},{192,576},{256,640},{320,704},{384,768}... | collective-permute-start | bytes 454664 | tf_op jit(solution)/shard_map/ppermute | solution.py:36
  13.0 26.1 %collective-permute-start.1 = (bf16[592,128]{1,0:T(8,128)(2,1)S(1)}, bf16[592,128]{1,0:T(8,128)(2,1)S(1)}, u32[]{:S(2)}, u32[]{:S(2)}) collective-permute-start(bf16[592,128]{1,0:T(8,128)(2,1)S(1)} %pack_keys.1), channel_id=1, source_target_pairs={{0,256},{64,320},{128,384},{192,448},{256,512},{320,576},{384,640}... | collective-permute-start | bytes 454664 | tf_op jit(solution)/shard_map/ppermute | solution.py:36
  21.2 16.9 %collective-permute-start = (bf16[592,128]{1,0:T(8,128)(2,1)S(1)}, bf16[592,128]{1,0:T(8,128)(2,1)S(1)}, u32[]{:S(2)}, u32[]{:S(2)}) collective-permute-start(bf16[592,128]{1,0:T(8,128)(2,1)S(1)} %pack_keys.1), channel_id=1, source_target_pairs={{0,128},{64,192},{128,256},{192,320},{256,384},{320,448},{384,512}... | collective-permute-start | bytes 454664 | tf_op jit(solution)/shard_map/ppermute | solution.py:36
  25.6 23.7 %collective-permute-start.3 = (bf16[592,128]{1,0:T(8,128)(2,1)S(1)}, bf16[592,128]{1,0:T(8,128)(2,1)S(1)}, u32[]{:S(2)}, u32[]{:S(2)}) collective-permute-start(bf16[592,128]{1,0:T(8,128)(2,1)S(1)} %pack_keys.1), channel_id=1, source_target_pairs={{0,512},{64,576},{128,640},{192,704},{256,768},{320,832},{384,896}... | collective-permute-start | bytes 454664 | tf_op jit(solution)/shard_map/ppermute | solution.py:36
  49.3 4.1 %collective-permute-start.4 = (bf16[5,592,128]{2,1,0:T(8,128)(2,1)S(1)}, bf16[5,592,128]{2,1,0:T(8,128)(2,1)S(1)}, u32[]{:S(2)}, u32[]{:S(2)}) collective-permute-start(bf16[5,592,128]{2,1,0:T(8,128)(2,1)S(1)} %bitcast_dynamic-update-slice_fusion.own), channel_id=1, source_target_pairs={{0,64},{64,0},{128,192},{192,128},{256,320},{320,256},{384,448},{4... | collective-permute-start | bytes 2273288 | tf_op jit(solution)/shard_map/ppermute | solution.py:40
  57.6 3.9 %collective-permute-start.5 = (bf16[2,592,256]{2,1,0:T(8,128)(2,1)S(1)}, bf16[2,592,256]{2,1,0:T(8,128)(2,1)S(1)}, u32[]{:S(2)}, u32[]{:S(2)}) collective-permute-start(bf16[2,592,256]{2,1,0:T(8,128)(2,1)S(1)} %get-tuple-element.34), channel_id=1, source_target_pairs={{0,64},{64,0},{128,192},{192,128},{256,320},{320,256},{384,448},{4... | collective-permute-start | bytes 1818632 | tf_op jit(solution)/shard_map/ppermute | solution.py:40
  61.7 11.8 %collective-permute-start.6 = (bf16[592,256]{1,0:T(8,128)(2,1)S(1)}, bf16[592,256]{1,0:T(8,128)(2,1)S(1)}, u32[]{:S(2)}, u32[]{:S(2)}) collective-permute-start(bf16[592,256]{1,0:T(8,128)(2,1)S(1)} %get-tuple-element.40), channel_id=1, source_target_pairs={{0,256},{64,832},{128,384},{192,960},{256,512},{320,64},{384,640},... | collective-permute-start | bytes 909320 | tf_op jit(solution)/shard_map/ppermute | solution.py:36
  63.7 12.4 %collective-permute-start.7 = (bf16[592,256]{1,0:T(8,128)(2,1)S(1)}, bf16[592,256]{1,0:T(8,128)(2,1)S(1)}, u32[]{:S(2)}, u32[]{:S(2)}) collective-permute-start(bf16[592,256]{1,0:T(8,128)(2,1)S(1)} %get-tuple-element.41), channel_id=1, source_target_pairs={{0,128},{64,960},{128,256},{192,64},{256,384},{320,192},{384,512},... | collective-permute-start | bytes 909320 | tf_op jit(solution)/shard_map/ppermute | solution.py:36
  76.2 34.6 %copy-start = (bf16[1,2048,448]{1,2,0:T(8,128)(2,1)S(1)}, bf16[1,2048,448]{1,2,0:T(8,128)(2,1)}, u32[]{:S(2)}) copy-start(bf16[1,2048,448]{1,2,0:T(8,128)(2,1)} %param.9) | copy-start | bytes 5505028
  76.2 34.6 %copy-start.3 = (f32[1,8]{1,0:T(1,128)S(1)}, f32[1,8]{1,0:T(1,128)}, u32[]{:S(2)}) copy-start(f32[1,8]{1,0:T(1,128)} %limits.1) | copy-start | bytes 100
  76.2 3.6 %collective-permute-start.8 = (bf16[592,256]{1,0:T(8,128)(2,1)S(1)}, bf16[592,256]{1,0:T(8,128)(2,1)S(1)}, u32[]{:S(2)}, u32[]{:S(2)}) collective-permute-start(bf16[592,256]{1,0:T(8,128)(2,1)S(1)} %add_convert_fusion.1), channel_id=1, source_target_pairs={{0,64},{64,0},{128,192},{192,128},{256,320},{320,256},{384,448},{4... | collective-permute-start | bytes 909320 | tf_op jit(solution)/shard_map/ppermute | solution.py:40
  79.9 13.2 %collective-permute-start.9 = (bf16[592,256]{1,0:T(8,128)(2,1)S(1)}, bf16[592,256]{1,0:T(8,128)(2,1)S(1)}, u32[]{:S(2)}, u32[]{:S(2)}) collective-permute-start(bf16[592,256]{1,0:T(8,128)(2,1)S(1)} %add_convert_fusion.g0), channel_id=1, source_target_pairs={{0,128},{64,960},{128,256},{192,64},{256,384},{320,192},{384,512},... | collective-permute-start | bytes 909320 | tf_op jit(solution)/shard_map/ppermute | solution.py:36
  81.9 13.2 %collective-permute-start.10 = (bf16[592,256]{1,0:T(8,128)(2,1)S(1)}, bf16[592,256]{1,0:T(8,128)(2,1)S(1)}, u32[]{:S(2)}, u32[]{:S(2)}) collective-permute-start(bf16[592,256]{1,0:T(8,128)(2,1)S(1)} %add_convert_fusion.g0), channel_id=1, source_target_pairs={{0,256},{64,832},{128,384},{192,960},{256,512},{320,64},{384,640},... | collective-permute-start | bytes 909320 | tf_op jit(solution)/shard_map/ppermute | solution.py:36
  93.1 11.8 %collective-permute-start.11 = (bf16[592,256]{1,0:T(8,128)(2,1)S(1)}, bf16[592,256]{1,0:T(8,128)(2,1)S(1)}, u32[]{:S(2)}, u32[]{:S(2)}) collective-permute-start(bf16[592,256]{1,0:T(8,128)(2,1)S(1)} %collective-permute-done.9), channel_id=1, source_target_pairs={{0,256},{64,832},{128,384},{192,960},{256,512},{320,64},{384,640},... | collective-permute-start | bytes 909320 | tf_op jit(solution)/shard_map/ppermute | solution.py:36
  95.1 11.9 %collective-permute-start.12 = (bf16[592,128]{1,0:T(8,128)(2,1)S(1)}, bf16[592,128]{1,0:T(8,128)(2,1)S(1)}, u32[]{:S(2)}, u32[]{:S(2)}) collective-permute-start(bf16[592,128]{1,0:T(8,128)(2,1)S(1)} %slice_select_fusion), channel_id=1, source_target_pairs={{0,256},{64,832},{128,384},{192,960},{256,512},{320,64},{384,640},... | collective-permute-start | bytes 454664 | tf_op jit(solution)/shard_map/ppermute | solution.py:36
  105.0 5.8 %collective-permute-start.13 = (bf16[2,592,256]{2,1,0:T(8,128)(2,1)S(1)}, bf16[2,592,256]{2,1,0:T(8,128)(2,1)S(1)}, u32[]{:S(2)}, u32[]{:S(2)}) collective-permute-start(bf16[2,592,256]{2,1,0:T(8,128)(2,1)S(1)} %pad_maximum_fusion.r12), channel_id=1, source_target_pairs={{0,64},{64,0},{128,192},{192,128},{256,320},{320,256},{384,448},{4... | collective-permute-start | bytes 1818632 | tf_op jit(solution)/shard_map/ppermute | solution.py:40
  107.0 3.8 %collective-permute-start.14 = (bf16[592,384]{1,0:T(8,128)(2,1)S(1)}, bf16[592,384]{1,0:T(8,128)(2,1)S(1)}, u32[]{:S(2)}, u32[]{:S(2)}) collective-permute-start(bf16[592,384]{1,0:T(8,128)(2,1)S(1)} %constant_dynamic-update-slice_fusion.r34), channel_id=1, source_target_pairs={{0,64},{64,0},{128,192},{192,128},{256,320},{320,256},{384,448},{4... | collective-permute-start | bytes 1363976 | tf_op jit(solution)/shard_map/ppermute | solution.py:40
